TPU v7x, 512 devices: a whole 4x8x8 slice. The times are simulated.
512 devices in a mesh: prow: 32 (over y, x), pcol: 16 (over z, core).
Axes of the slice: x: 4, y: 8, z: 8, core: 2. Of those that a mesh axis runs over, the one named last changes fastest.
Arguments:
- panel_transposed: float32 [2, 512, 12288], P(None, 'pcol', 'prow'), may hold values from -0.75 to 0.75
- inverse_transposed: float32 [2, 512, 512], P(None, 'pcol'), as said below
- targets: int32 [2, 96], replicated, may hold values from 0 to 127, as said below
Outputs:
- updates: float32 [16384, 16384], P('prow', 'pcol')
Inputs may be any that keep to these rules, and one draw needn't show every extreme that they name: Along each panel the targets rise strictly. Row block i lies on prow index i // 3; its target's owner, targets // 4, is that index or the one before it. The first row block targets 0 and the last targets 128 - 1. `inverse_transposed`: upper triangular with a positive diagonal.
All inputs are finite; a program needn't handle non-finite values.
Results may differ from a plain program's by a relative error of at most 0.000086.
Values sent between devices are 32-bit elements; how exact they have to be, the bound alone decides.
No kernel may reach another device: no remote copies, remote signals or barrier semaphores. Data moves between devices by JAX's collectives and lax.ppermute only.
A program may use at most 64 MiB of HBM per device.

v0:
```python
import jax
import jax.numpy as jnp
from jax import lax
from jax.sharding import PartitionSpec as P

BLOCK = 128


def passed_along(value, axis, steps):
    count = lax.axis_size(axis)
    first, last = (max(0, -steps), min(count, count - steps))
    return lax.ppermute(value, axis, [(source, source + steps) for source in range(first, last)])


def broadcast(x, axis, root):
    mine = lax.axis_index(axis) == root
    return lax.psum(jnp.where(mine, x, jnp.zeros_like(x)), axis)


def body(panel_transposed, inverse_transposed, targets):
    per_device = panel_transposed.shape[2]
    blocks_dev = per_device // BLOCK
    anc_dev = blocks_dev + 1
    partial_update_value = jnp.einsum(
        "yqg,yqz->ygz", inverse_transposed, panel_transposed, precision=lax.Precision.HIGHEST
    )
    cholesky_factor = lax.psum(partial_update_value, "pcol")
    following = passed_along(cholesky_factor, "prow", -1)
    widened = jnp.concatenate([cholesky_factor, following], axis=2)
    prow_idx = lax.axis_index("prow")
    padding = jnp.full((2, blocks_dev), -1, jnp.int32)
    padded = jnp.concatenate([targets, padding], axis=1)
    neighbour_blocks = lax.dynamic_slice_in_dim(padded, prow_idx * blocks_dev, 2 * blocks_dev, 1)
    owned_rows = prow_idx * anc_dev + jnp.arange(anc_dev, dtype=jnp.int32)
    select = (neighbour_blocks[:, None, :] == owned_rows[None, :, None]).astype(jnp.float32)
    columns = widened.shape[1]
    update_pieces = widened.reshape(2, columns, 2 * blocks_dev, BLOCK)
    placed = jnp.zeros((2, columns, anc_dev, BLOCK), jnp.float32)
    for source in range(2 * blocks_dev):
        placed = placed + select[:, None, :, source, None] * update_pieces[:, :, None, source, :]
    placed = placed.reshape(2, columns, anc_dev * BLOCK)
    col_idx = lax.axis_index("pcol")
    spread = lax.axis_size("prow") // lax.axis_size("pcol")
    collected_columns = []
    for offset in range(spread):
        collected_columns.append(broadcast(placed, "prow", col_idx * spread + offset))
    across = jnp.concatenate(collected_columns, axis=2)
    total_cols = placed.shape[1]
    left_rows = placed.reshape(2 * total_cols, anc_dev * BLOCK)
    right_rows = across.reshape(2 * total_cols, across.shape[2])
    updates = jnp.dot(
        left_rows.T, right_rows, precision=lax.Precision.HIGHEST, preferred_element_type=jnp.float32
    )
    return updates


def solution(mesh):
    placed = (P(None, "pcol", "prow"), P(None, "pcol", None), P())
    return jax.shard_map(
        body, mesh=mesh, in_specs=placed, out_specs=P("prow", "pcol"), check_vma=False
    )
```

profile of v0, /device:TPU:64, one launch (start us, length us, event | category | flops | bytes accessed | tf_op | source)
XLA Modules:
  0.0 407.1 jit_solution(3780175294253718320)
XLA Ops:
  6.5 0.9 copy-done
  7.4 3.5 fusion.3
  11.0 120.6 %all-reduce.5.cloned.1.call-done = f32[2,512,384]{2,1,0:T(8,128)} async-done(((f32[2,512,384]{2,1,0:T(8,128)}), f32[2,512,384]{2,1,0:T(8,128)}) %all-reduce.5.cloned.1.call-update) | async-done | bytes 1572880 | tf_op jit(solution)/shard_map/psum | solution.py:27
  131.6 1.3 collective-permute-start
  133.4 36.7 %collective-permute-done = f32[2,512,384]{2,1,0:T(8,128)S(1)} collective-permute-done((f32[2,512,384]{2,1,0:T(8,128)}, f32[2,512,384]{2,1,0:T(8,128)S(1)}, u32[]{:S(2)}, u32[]{:S(2)}) %collective-permute-start) | collective-permute-done | bytes 1572896 | tf_op jit(solution)/shard_map/ppermute | solution.py:12
  170.2 3.3 pad_maximum_fusion.1
  173.4 2.4 copy.6
  175.8 1.7 slice_bitcast_fusion.5
  177.5 1.3 copy.7
  178.9 1.3 copy.12
  180.2 1.0 copy.11
  181.2 1.0 copy.10
  182.2 1.0 copy.9
  183.2 1.0 copy.8
  184.2 0.4 mul.231
  184.6 1.8 mul.262
  186.4 1.4 mul.236
  187.8 1.9 mul.267
  189.7 1.4 mul.241
  191.1 1.9 mul.272
  193.0 1.4 mul.246
  194.4 1.9 mul.277
  196.3 1.4 mul.251
  197.7 1.9 mul.282
  199.5 0.4 mul.256
  199.9 1.8 mul.287
  201.7 7.6 %broadcast_select_fusion.1 = (f32[2,512,512]{2,1,0:T(8,128)}, f32[2,512,512]{2,1,0:T(8,128)S(1)}) fusion(pred[]{:T(512)S(6)} %eq.22, f32[2,512,512]{2,1,0:T(8,128)} %mul.287, f32[2,512]{1,0:T(2,128)S(1)} %bitcast.69, f32[2,512,512]{2,1,0:T(8,128)} %mul.282, f32[2,512]{1,0:T(2,128)S(1)} %bitcast.70, f32[2,512,512]{2,1,0:T(8,128)} %mul.277, ...), kind=kLoop, calls=%fused_computation.8 | loop fusion | flops 6291456 | bytes 16801792 | tf_op jit(solution)/shard_map/jit(_where)/select_n | solution.py:17
  209.3 1.6 broadcast_select_fusion
  210.9 4.9 %multiply_add_fusion.1 = f32[2,512,4,128]{3,2,1,0:T(4,128)S(1)} fusion(f32[2,512,128]{2,1,0:T(8,128)S(1)} %copy.12, f32[2,4]{1,0:T(2,128)S(1)} %get-tuple-element.16, f32[2,512,128]{2,1,0:T(8,128)} %copy.11, f32[2,4]{1,0:T(2,128)S(1)} %get-tuple-element.17, f32[2,512,128]{2,1,0:T(8,128)} %copy.10, f32[2,4]{1,0:T(2,128)S(1)} %get-tuple-element.18, ...), kind=kLoop, calls=%fused_computation.6 | loop fusion | flops 5767168 | bytes 5243072 | tf_op jit(solution)/shard_map/add | solution.py:40
  215.8 173.6 %all-reduce.7.cloned.1.call-done = (f32[2,512,512]{2,1,0:T(8,128)}, f32[2,512,512]{2,1,0:T(8,128)}) async-done(((f32[2,512,512]{2,1,0:T(8,128)}, f32[2,512,512]{2,1,0:T(8,128)}), (f32[2,512,512]{2,1,0:T(8,128)}, f32[2,512,512]{2,1,0:T(8,128)})) %all-reduce.7.cloned.1.call-update) | async-done | bytes 4194320 | tf_op jit(solution)/shard_map/psum | solution.py:17
  389.4 2.7 pad_maximum_fusion
  392.1 8.1 %fusion = f32[512,1024]{1,0:T(8,128)} fusion(f32[1024,1024]{1,0:T(8,128)S(1)} %bitcast.64, f32[128,8,4,128]{3,2,1,0:T(4,128)S(1)} %bitcast.66), kind=kOutput, calls=%fused_computation.2 | convolution fusion | flops 6442450944 | bytes 8388608 | tf_op jit(solution)/shard_map/dot_general | solution.py:51
  (29 shorter events, 0.6 us)
Async XLA Ops:
  6.5 0.9 copy-start
  6.5 126.4 %copy-start.5 = (s32[2,96]{1,0:T(2,128)S(1)}, s32[2,96]{1,0:T(2,128)}, u32[]{:S(2)}) copy-start(s32[2,96]{1,0:T(2,128)} %param.5) | copy-start | bytes 2308
  6.5 125.1 %all-reduce.5.cloned.1.call-start = ((), (), s32[]{:S(2)}) async-start(), calls=%async_computation | async-start | bytes 3145728 | tf_op jit(solution)/shard_map/psum | solution.py:27
  10.9 378.5 %all-reduce.7.cloned.1.call-start = ((), (), s32[]{:S(2)}) async-start(), calls=%async_computation.1 | async-start | bytes 8388608 | tf_op jit(solution)/shard_map/psum | solution.py:17
  131.6 38.5 %collective-permute-start = (f32[2,512,384]{2,1,0:T(8,128)}, f32[2,512,384]{2,1,0:T(8,128)S(1)}, u32[]{:S(2)}, u32[]{:S(2)}) collective-permute-start(f32[2,512,384]{2,1,0:T(8,128)} %all-reduce.5.cloned.1.call-done), channel_id=1, source_target_pairs={{16,0},{32,16},{48,32},{64,48},{80,64},{96,80},{112,96},{128,112},... | collective-permute-start | bytes 4718600 | tf_op jit(solution)/shard_map/ppermute | solution.py:12
  177.5 2.7 copy-start.4
  177.5 3.7 copy-start.3
  177.5 4.7 %copy-start.2 = (f32[2,512,128]{1,2,0:T(8,128)S(1)}, f32[2,512,128]{1,2,0:T(8,128)}, u32[]{:S(2)}) copy-start(f32[2,512,128]{1,2,0:T(8,128)} %get-tuple-element.13) | copy-start | bytes 1572868
  178.9 4.3 %copy-start.1 = (f32[2,512,128]{1,2,0:T(8,128)S(1)}, f32[2,512,128]{1,2,0:T(8,128)}, u32[]{:S(2)}) copy-start(f32[2,512,128]{1,2,0:T(8,128)} %get-tuple-element.14) | copy-start | bytes 1572868
Sparse Core Ops, SparseCore 0:
  11.1 120.5 all-reduce.4
  211.1 178.3 all-reduce.6
where the time goes:
time: 408 us; the launch traced here: 407 us
  waiting for transfers between devices  331 us (81%)
  local copies, waits for them, and re-layouts  29.5 us (7%)
  other arithmetic  20.1 us (5%)
  between operations  13.5 us (3%)
  matrix products  11.6 us (3%)
    psum x1, waiting for transfers between devices, broadcast(): return lax.psum(jnp.where(mine, x, jnp.zeros_like(x)), axis)  174 us
    psum x1, waiting for transfers between devices, body(): cholesky_factor = lax.psum(partial_update_value, 'pcol')  121 us
    ppermute x1, waiting for transfers between devices, passed_along(): lax.ppermute(value, axis, [(source, source + steps) for source in range(f...  36.7 us
    mul x20, local copies, waits for them, and re-layouts, body(): select[:, None, :, source, None] * update_pieces[:, :, None, source, :]  25.8 us
    select_n x2, other arithmetic, broadcast(): return lax.psum(jnp.where(mine, x, jnp.zeros_like(x)), axis)  9.17 us
  transfers between devices with their start and end apart: 3, of which 3 were waited for; matrix products, arithmetic and copies ran while one was open for 1% of the time, Pallas kernels for 0%

commit v1 on v0

v1 whole, which is shorter than its diff:
```python
import functools
import jax
import jax.numpy as jnp
from jax import lax
from jax.experimental import pallas as pl
from jax.experimental.pallas import tpu as pltpu
from jax.sharding import PartitionSpec as P

BLOCK = 128
NX, NZ, NC = 4, 8, 2
AXES = ("prow", "pcol")
F32, BF16 = jnp.float32, jnp.bfloat16
MIB = 1 << 20
PIECE_OFFSETS = (0, 4, -1, 3, 1, -3, -2, 2)


def device(y, x, z, core):
    return ((y % 8) * NX + x) * NZ * NC + z * NC + core


def every():
    for y in range(8):
        for x in range(NX):
            for z in range(NZ):
                for core in range(NC):
                    yield y, x, z, core


def transposing(lift):
    return [(device(y, x, z, k), device(2 * y - z + lift, x, y, k)) for y, x, z, k in every()]


def along_y(distance):
    return [(device(y + distance, x, z, k), device(y, x, z, k)) for y, x, z, k in every()]


def to_columns():
    first, second, sibling, relay_home, relay_other = [], [], [], [], []
    for y, x, z, k in every():
        here = device(y, x, z, k)
        wanted_by = x // 2
        near, across = device(y, x ^ 1, z, wanted_by), device(y, 3 - x, z, wanted_by)
        first.append((here, near if k == 0 else across))
        second.append((here, across if k == 0 else near))
        if wanted_by == k:
            relay_home.append((here, device(y, 3 - x, z, k)))
        else:
            sibling.append((here, device(y, x, z, 1 - k)))
            relay_other.append((here, device(y, x ^ 1, z, k)))
    return first, second, sibling, relay_home, relay_other


def send(value, pairs):
    return lax.ppermute(value, AXES, pairs)


def split(value):
    high = value.astype(BF16)
    return high, (value - high.astype(F32)).astype(BF16)


def dot3(a, b, dims):
    (a_high, a_low), (b_high, b_low) = a, b
    mul = functools.partial(lax.dot_general, dimension_numbers=(dims, ((), ())), preferred_element_type=F32)
    return mul(a_high, b_high) + (mul(a_high, b_low) + mul(a_low, b_high))


def place_kernel(row_ref, targets_ref, own_ref, next_ref, inverse_ref, placed_ref, both_ref):
    row = row_ref[0]
    blocks = 3
    count = targets_ref.shape[1]
    for panel in range(2):
        for slot in range(4):
            total = jnp.zeros((own_ref.shape[1], BLOCK), F32)
            for source in range(2 * blocks):
                index = row * blocks + source
                target = targets_ref[panel, jnp.minimum(index, count - 1)]
                hit = jnp.logical_and(index < count, target == row * 4 + slot)
                ref = own_ref if source < blocks else next_ref
                at = (source % blocks) * BLOCK
                total = jnp.where(hit, ref[panel, :, at : at + BLOCK], total)
            placed_ref[panel, :, slot * BLOCK : (slot + 1) * BLOCK] = total
            both_ref[panel, :, slot * BLOCK : (slot + 1) * BLOCK] = total
        both_ref[2 + panel] = inverse_ref[panel]


def rows_kernel(gathered_ref, inv_high, inv_low, row_high, row_low):
    for panel in range(2):
        inverse = gathered_ref[:, 2 + panel].reshape(512, 512)
        rows = gathered_ref[:, panel].reshape(512, 512)
        factor = dot3(split(inverse), split(rows), ((0,), (0,)))
        row_high[panel], row_low[panel] = split(factor.T)
        inv_high[panel], inv_low[panel] = split(inverse.T)


def columns_kernel(
    info, inv_high, inv_low, row_high, row_low, own, first, second, sibling, relay_a, relay_b, out, high, low
):
    home = info[0] == 1
    at_a = pl.multiple_of(info[1] * 512, 512)
    at_b = pl.multiple_of(512 - info[1] * 512, 512)

    def unpack(piece, _):
        z = info[8 + piece]
        for half, refs, at in ((2, (first,), at_a), (3, (second,), at_a), (4, (own, relay_a), at_b), (5, (sibling, relay_b), at_b)):
            start = pl.multiple_of(z * 64 + info[half] * 32, 32)
            for panel in range(2):
                value = refs[0][piece, panel]
                if len(refs) == 2:
                    value = jnp.where(home, value, refs[1][piece, panel])
                value_high, value_low = split(value)
                high[panel, pl.ds(start, 32), pl.ds(at, 512)] = value_high
                low[panel, pl.ds(start, 32), pl.ds(at, 512)] = value_low
        return 0

    lax.fori_loop(0, 8, unpack, 0)

    def tile(step, _):
        at = pl.multiple_of(step * 256, 256)
        total = None
        for panel in range(2):
            cols = (high[panel, :, pl.ds(at, 256)], low[panel, :, pl.ds(at, 256)])
            factor = dot3((inv_high[panel], inv_low[panel]), cols, ((1,), (0,)))
            part = dot3((row_high[panel], row_low[panel]), split(factor), ((1,), (0,)))
            total = part if total is None else total + part
        out[:, pl.ds(at, 256)] = total
        return 0

    lax.fori_loop(0, 4, tile, 0)


VMEM = pl.BlockSpec(memory_space=pltpu.VMEM)
SMEM = pl.BlockSpec(memory_space=pltpu.SMEM)


def body(panel, inverse, targets):
    row, col = lax.axis_index("prow"), lax.axis_index("pcol")
    y, x, z, core = row // NX, row % NX, col // NC, col % NC

    following = send(panel, [(r * 16 + c, (r - 1) * 16 + c) for r in range(1, 32) for c in range(16)])
    placed, both = pl.pallas_call(
        place_kernel,
        out_shape=(jax.ShapeDtypeStruct((2, 32, 512), F32), jax.ShapeDtypeStruct((4, 32, 512), F32)),
        in_specs=[SMEM, SMEM, VMEM, VMEM, VMEM],
        out_specs=(VMEM, VMEM),
        name="place",
    )(row.reshape(1), targets, panel, following, inverse)

    gathered = lax.all_gather(both, "pcol")

    low_piece, high_piece = send(placed, transposing(0)), send(placed, transposing(4))
    pair = jnp.stack([low_piece, high_piece])
    up, down = send(pair, along_y(1)), send(pair, along_y(-1))
    up2, down2 = send(low_piece, along_y(2)), send(low_piece, along_y(-2))
    own = jnp.concatenate([pair, up, down, up2[None], down2[None]])

    p_first, p_second, p_sibling, p_home, p_other = to_columns()
    first, second, sibling = send(own, p_first), send(own, p_second), send(own, p_sibling)
    relay_a, relay_b = send(first, p_home), send(first, p_other)

    weights = jax.ShapeDtypeStruct((2, 512, 512), BF16)
    inv_high, inv_low, row_high, row_low = pl.pallas_call(
        rows_kernel,
        out_shape=(weights,) * 4,
        in_specs=[VMEM],
        out_specs=(VMEM,) * 4,
        compiler_params=pltpu.CompilerParams(vmem_limit_bytes=40 * MIB),
        cost_estimate=pl.CostEstimate(flops=2 * 3 * 2 * 512**3, bytes_accessed=8 * MIB, transcendentals=0),
        name="rows",
    )(gathered)

    is_home = (x // 2 == core).astype(jnp.int32)
    near = jnp.where(is_home == 1, x ^ 1, 3 - x)
    info = jnp.stack(
        [
            is_home,
            near - 2 * core,
            1 - is_home,
            is_home,
            jnp.where(is_home == 1, core, 0),
            jnp.where(is_home == 1, 1 - core, 1),
            0 * core,
            0 * core,
        ]
    )
    info = jnp.concatenate([info, (2 * z - y + jnp.array(PIECE_OFFSETS, jnp.int32)) % 8])
    return pl.pallas_call(
        columns_kernel,
        out_shape=jax.ShapeDtypeStruct((512, 1024), F32),
        in_specs=[SMEM] + [VMEM] * 10,
        out_specs=VMEM,
        scratch_shapes=[pltpu.VMEM((2, 512, 1024), BF16), pltpu.VMEM((2, 512, 1024), BF16)],
        compiler_params=pltpu.CompilerParams(vmem_limit_bytes=48 * MIB),
        cost_estimate=pl.CostEstimate(flops=2 * 3 * 4 * 512 * 512 * 1024, bytes_accessed=12 * MIB, transcendentals=0),
        name="columns",
    )(info, inv_high, inv_low, row_high, row_low, own, first, second, sibling, relay_a, relay_b)


def solution(mesh):
    specs = (P(None, "pcol", "prow"), P(None, "pcol", None), P())
    return jax.shard_map(body, mesh=mesh, in_specs=specs, out_specs=P("prow", "pcol"), check_vma=False)
```

time: 408 us -> 136 us (0.33)
  the two profiles are of different devices: /device:TPU:64 before, /device:TPU:22 now
where the time goes in v1:
time: 136 us
  starting transfers between devices  54 us (40%)
  waiting for transfers between devices  45.3 us (33%)
  Pallas kernels  18.9 us (14%)
  between operations  13.7 us (10%)
  local copies, waits for them, and re-layouts  3.01 us (2%)
    ppermute x12, starting transfers between devices, send(): return lax.ppermute(value, AXES, pairs)  54 us
    ppermute x12, waiting for transfers between devices, send(): return lax.ppermute(value, AXES, pairs)  45.3 us
    pallas_call x1, Pallas kernels, body(): pl.pallas_call(columns_kernel, out_shape=jax.ShapeDtypeStruct((512, 1024)...  15 us
    unnamed x13, local copies, waits for them, and re-layouts  2.91 us
  transfers between devices with their start and end apart: 13, of which 6 were waited for; matrix products, arithmetic and copies ran while one was open for 1% of the time, Pallas kernels for 2%

profile of v1, /device:TPU:22, one launch (start us, length us, event | category | flops | bytes accessed | tf_op | source)
XLA Modules:
  0.0 135.6 jit_solution(3575945849594884229)
XLA Ops:
  6.5 2.7 %collective-permute-start = (f32[2,32,384]{2,1,0:T(8,128)}, f32[2,32,384]{2,1,0:T(8,128)S(1)}, u32[]{:S(2)}, u32[]{:S(2)}) collective-permute-start(f32[2,32,384]{2,1,0:T(8,128)} %own_ref.1), channel_id=1, source_target_pairs={{16,0},{17,1},{18,2},{19,3},{20,4},{21,5},{22,6},{23,7},{24,8},{25... | collective-permute-start | bytes 294920 | tf_op jit(solution)/shard_map/ppermute | solution.py:54
  9.3 6.1 %collective-permute-done.next_ref = f32[2,32,384]{2,1,0:T(8,128)S(1)} collective-permute-done((f32[2,32,384]{2,1,0:T(8,128)}, f32[2,32,384]{2,1,0:T(8,128)S(1)}, u32[]{:S(2)}, u32[]{:S(2)}) %collective-permute-start) | collective-permute-done | bytes 98336 | tf_op jit(solution)/shard_map/ppermute | solution.py:54
  15.4 0.6 copy-done.1
  16.0 1.8 %place.1 = (f32[2,32,512]{2,1,0:T(8,128)}, f32[4,32,512]{2,1,0:T(8,128)}) custom-call(s32[1]{0:T(128)} %bitcast.5.row_ref, s32[2,96]{1,0:T(2,128)} %targets_ref.1, f32[2,32,384]{2,1,0:T(8,128)} %own_ref.1, f32[2,32,384]{2,1,0:T(8,128)} %copy-done.1, f32[2,32,512]{2,1,0:T(8,128)} %inverse_ref.1), custom_call_target="tpu_custom_call" | custom-call | tf_op jit(solution)/shard_map/place/pallas_call | solution.py:141
  17.8 0.0 all-gather.3.cloned.1.call-update
  17.9 5.9 %collective-permute-start.2 = (f32[2,32,512]{2,1,0:T(8,128)}, f32[2,32,512]{2,1,0:T(8,128)S(1)}, u32[]{:S(2)}, u32[]{:S(2)}) collective-permute-start(f32[2,32,512]{2,1,0:T(8,128)} %get-tuple-element.16), channel_id=1, source_target_pairs={{0,256},{1,257},{2,192},{3,193},{4,128},{5,129},{6,64},{7,65},{8,0... | collective-permute-start | bytes 393224 | tf_op jit(solution)/shard_map/ppermute | solution.py:54
  23.7 10.5 %collective-permute-start.1 = (f32[2,32,512]{2,1,0:T(8,128)}, f32[2,32,512]{2,1,0:T(8,128)S(1)}, u32[]{:S(2)}, u32[]{:S(2)}) collective-permute-start(f32[2,32,512]{2,1,0:T(8,128)} %get-tuple-element.16), channel_id=1, source_target_pairs={{0,0},{1,1},{2,448},{3,449},{4,384},{5,385},{6,320},{7,321},{8,256... | collective-permute-start | bytes 393224 | tf_op jit(solution)/shard_map/ppermute | solution.py:54
  34.3 0.0 collective-permute-done.2
  34.3 2.8 %collective-permute-done.1 = f32[2,32,512]{2,1,0:T(8,128)S(1)} collective-permute-done((f32[2,32,512]{2,1,0:T(8,128)}, f32[2,32,512]{2,1,0:T(8,128)S(1)}, u32[]{:S(2)}, u32[]{:S(2)}) %collective-permute-start.1) | collective-permute-done | bytes 131104 | tf_op jit(solution)/shard_map/ppermute | solution.py:54
  37.1 7.7 %collective-permute-start.4 = (f32[2,2,32,512]{3,2,1,0:T(8,128)S(1)}, f32[2,2,32,512]{3,2,1,0:T(8,128)S(1)}, u32[]{:S(2)}, u32[]{:S(2)}) collective-permute-start(f32[2,2,32,512]{3,2,1,0:T(8,128)S(1)} %pad_maximum_fusion), channel_id=1, source_target_pairs={{448,0},{449,1},{450,2},{451,3},{452,4},{453,5},{454,6},{455,7},{4... | collective-permute-start | bytes 786440 | tf_op jit(solution)/shard_map/ppermute | solution.py:54
  44.9 1.9 %collective-permute-start.3 = (f32[2,2,32,512]{3,2,1,0:T(8,128)S(1)}, f32[2,2,32,512]{3,2,1,0:T(8,128)S(1)}, u32[]{:S(2)}, u32[]{:S(2)}) collective-permute-start(f32[2,2,32,512]{3,2,1,0:T(8,128)S(1)} %pad_maximum_fusion), channel_id=1, source_target_pairs={{64,0},{65,1},{66,2},{67,3},{68,4},{69,5},{70,6},{71,7},{72,8},{73... | collective-permute-start | bytes 786440 | tf_op jit(solution)/shard_map/ppermute | solution.py:54
  46.8 12.0 %collective-permute-start.6 = (f32[2,32,512]{2,1,0:T(8,128)S(1)}, f32[2,32,512]{2,1,0:T(8,128)S(1)}, u32[]{:S(2)}, u32[]{:S(2)}) collective-permute-start(f32[2,32,512]{2,1,0:T(8,128)S(1)} %collective-permute-done.1), channel_id=1, source_target_pairs={{384,0},{385,1},{386,2},{387,3},{388,4},{389,5},{390,6},{391,7},{3... | collective-permute-start | bytes 393224 | tf_op jit(solution)/shard_map/ppermute | solution.py:54
  58.8 1.9 %collective-permute-start.5 = (f32[2,32,512]{2,1,0:T(8,128)S(1)}, f32[2,32,512]{2,1,0:T(8,128)S(1)}, u32[]{:S(2)}, u32[]{:S(2)}) collective-permute-start(f32[2,32,512]{2,1,0:T(8,128)S(1)} %collective-permute-done.1), channel_id=1, source_target_pairs={{128,0},{129,1},{130,2},{131,3},{132,4},{133,5},{134,6},{135,7},{1... | collective-permute-start | bytes 393224 | tf_op jit(solution)/shard_map/ppermute | solution.py:54
  60.8 0.0 collective-permute-done.3
  60.8 0.0 collective-permute-done.4
  60.9 8.0 %collective-permute-done.5 = f32[2,32,512]{2,1,0:T(8,128)S(1)} collective-permute-done((f32[2,32,512]{2,1,0:T(8,128)S(1)}, f32[2,32,512]{2,1,0:T(8,128)S(1)}, u32[]{:S(2)}, u32[]{:S(2)}) %collective-permute-start.5) | collective-permute-done | bytes 131104 | tf_op jit(solution)/shard_map/ppermute | solution.py:54
  68.8 0.0 collective-permute-done.6
  68.9 1.9 %collective-permute-start.7 = (f32[8,2,32,512]{3,2,1,0:T(8,128)S(1)}, f32[8,2,32,512]{3,2,1,0:T(8,128)S(1)}, u32[]{:S(2)}, u32[]{:S(2)}) collective-permute-start(f32[8,2,32,512]{3,2,1,0:T(8,128)S(1)} %bitcast_dynamic-update-slice_fusion.own), channel_id=1, source_target_pairs={{0,16},{1,48},{2,18},{3,50},{4,20},{5,52},{6,22},{7,54},{8,24},{9,... | collective-permute-start | bytes 3145736 | tf_op jit(solution)/shard_map/ppermute | solution.py:54
  70.8 1.4 %collective-permute-start.9 = (f32[8,2,32,512]{3,2,1,0:T(8,128)S(1)}, f32[8,2,32,512]{3,2,1,0:T(8,128)S(1)}, u32[]{:S(2)}, u32[]{:S(2)}) collective-permute-start(f32[8,2,32,512]{3,2,1,0:T(8,128)S(1)} %bitcast_dynamic-update-slice_fusion.own), channel_id=1, source_target_pairs={{1,0},{3,2},{5,4},{7,6},{9,8},{11,10},{13,12},{15,14},{17,16},{19,... | collective-permute-start | bytes 3145736 | tf_op jit(solution)/shard_map/ppermute | solution.py:54
  72.1 4.9 %collective-permute-start.8 = (f32[8,2,32,512]{3,2,1,0:T(8,128)S(1)}, f32[8,2,32,512]{3,2,1,0:T(8,128)}, u32[]{:S(2)}, u32[]{:S(2)}) collective-permute-start(f32[8,2,32,512]{3,2,1,0:T(8,128)S(1)} %bitcast_dynamic-update-slice_fusion.own), channel_id=1, source_target_pairs={{0,48},{1,16},{2,50},{3,18},{4,52},{5,20},{6,54},{7,22},{8,56},{9,... | collective-permute-start | bytes 3145736 | tf_op jit(solution)/shard_map/ppermute | solution.py:54
  77.0 16.9 %collective-permute-done.7.first = f32[8,2,32,512]{3,2,1,0:T(8,128)S(1)} collective-permute-done((f32[8,2,32,512]{3,2,1,0:T(8,128)S(1)}, f32[8,2,32,512]{3,2,1,0:T(8,128)S(1)}, u32[]{:S(2)}, u32[]{:S(2)}) %collective-permute-start.7) | collective-permute-done | bytes 1048608 | tf_op jit(solution)/shard_map/ppermute | solution.py:54
  93.9 1.9 %collective-permute-start.11 = (f32[8,2,32,512]{3,2,1,0:T(8,128)S(1)}, f32[8,2,32,512]{3,2,1,0:T(8,128)}, u32[]{:S(2)}, u32[]{:S(2)}) collective-permute-start(f32[8,2,32,512]{3,2,1,0:T(8,128)S(1)} %collective-permute-done.7.first), channel_id=1, source_target_pairs={{1,17},{3,19},{5,21},{7,23},{9,25},{11,27},{13,29},{15,31},{17,1},... | collective-permute-start | bytes 3145736 | tf_op jit(solution)/shard_map/ppermute | solution.py:54
  95.8 1.3 collective-permute-start.10
  97.2 0.7 and_select_fusion
  97.9 0.1 concatenate.7.info
  98.0 2.2 %copy-done = f32[64,32,512]{2,1,0:T(8,128)S(1)} copy-done((f32[64,32,512]{2,1,0:T(8,128)S(1)}, f32[64,32,512]{2,1,0:T(8,128)}, u32[]{:S(2)}) %copy-start) | copy-done | bytes 4194328
  100.1 2.1 %rows.1 = (bf16[2,512,512]{2,1,0:T(8,128)(2,1)S(1)}, bf16[2,512,512]{2,1,0:T(8,128)(2,1)S(1)}, bf16[2,512,512]{2,1,0:T(8,128)(2,1)S(1)}, bf16[2,512,512]{2,1,0:T(8,128)(2,1)S(1)}) custom-call(f32[16,4,32,512]{3,2,1,0:T(8,128)S(1)} %bitcast.15), custom_call_target="tpu_custom_call" | custom-call | flops 1610612736 | bytes 8388608 | tf_op jit(solution)/shard_map/rows/pallas_call | solution.py:162
  102.2 0.0 collective-permute-done.9.sibling
  102.3 0.0 collective-permute-done.8.second
  102.3 8.4 %collective-permute-done.11.relay_b = f32[8,2,32,512]{3,2,1,0:T(8,128)} collective-permute-done((f32[8,2,32,512]{3,2,1,0:T(8,128)S(1)}, f32[8,2,32,512]{3,2,1,0:T(8,128)}, u32[]{:S(2)}, u32[]{:S(2)}) %collective-permute-start.11) | collective-permute-done | bytes 1048608 | tf_op jit(solution)/shard_map/ppermute | solution.py:54
  110.7 3.1 %collective-permute-done.10.relay_a = f32[8,2,32,512]{3,2,1,0:T(8,128)} collective-permute-done((f32[8,2,32,512]{3,2,1,0:T(8,128)S(1)}, f32[8,2,32,512]{3,2,1,0:T(8,128)}, u32[]{:S(2)}, u32[]{:S(2)}) %collective-permute-start.10) | collective-permute-done | bytes 1048608 | tf_op jit(solution)/shard_map/ppermute | solution.py:54
  113.8 15.0 %columns.1 = f32[512,1024]{1,0:T(8,128)} custom-call(s32[16]{0:T(128)S(1)} %concatenate.7.info, bf16[2,512,512]{2,1,0:T(8,128)(2,1)S(1)} %get-tuple-element.12.inv_high, bf16[2,512,512]{2,1,0:T(8,128)(2,1)S(1)} %get-tuple-element.13.inv_low, bf16[2,512,512]{2,1,0:T(8,128)(2,1)S(1)} %get-tuple-element.14.row_high, ...), custom_call_target="tpu_custom_call" | custom-call | flops 6442450944 | bytes 12582912 | tf_op jit(solution)/shard_map/columns/pallas_call | solution.py:187
  (16 shorter events, 0.1 us)
Async XLA Ops:
  6.5 91.4 %all-gather.3.cloned.1.call-start = ((), (), s32[]{:S(2)}) async-start(), calls=%async_computation | async-start | bytes 4456448 | tf_op jit(solution)/shard_map/all_gather | solution.py:149
  6.5 8.8 %collective-permute-start = (f32[2,32,384]{2,1,0:T(8,128)}, f32[2,32,384]{2,1,0:T(8,128)S(1)}, u32[]{:S(2)}, u32[]{:S(2)}) collective-permute-start(f32[2,32,384]{2,1,0:T(8,128)} %own_ref.1), channel_id=1, source_target_pairs={{16,0},{17,1},{18,2},{19,3},{20,4},{21,5},{22,6},{23,7},{24,8},{25... | collective-permute-start | bytes 294920 | tf_op jit(solution)/shard_map/ppermute | solution.py:54
  15.4 0.6 copy-start.1
  17.9 16.4 %collective-permute-start.2 = (f32[2,32,512]{2,1,0:T(8,128)}, f32[2,32,512]{2,1,0:T(8,128)S(1)}, u32[]{:S(2)}, u32[]{:S(2)}) collective-permute-start(f32[2,32,512]{2,1,0:T(8,128)} %get-tuple-element.16), channel_id=1, source_target_pairs={{0,256},{1,257},{2,192},{3,193},{4,128},{5,129},{6,64},{7,65},{8,0... | collective-permute-start | bytes 393224 | tf_op jit(solution)/shard_map/ppermute | solution.py:54
  23.7 13.4 %collective-permute-start.1 = (f32[2,32,512]{2,1,0:T(8,128)}, f32[2,32,512]{2,1,0:T(8,128)S(1)}, u32[]{:S(2)}, u32[]{:S(2)}) collective-permute-start(f32[2,32,512]{2,1,0:T(8,128)} %get-tuple-element.16), channel_id=1, source_target_pairs={{0,0},{1,1},{2,448},{3,449},{4,384},{5,385},{6,320},{7,321},{8,256... | collective-permute-start | bytes 393224 | tf_op jit(solution)/shard_map/ppermute | solution.py:54
  37.1 23.7 %collective-permute-start.4 = (f32[2,2,32,512]{3,2,1,0:T(8,128)S(1)}, f32[2,2,32,512]{3,2,1,0:T(8,128)S(1)}, u32[]{:S(2)}, u32[]{:S(2)}) collective-permute-start(f32[2,2,32,512]{3,2,1,0:T(8,128)S(1)} %pad_maximum_fusion), channel_id=1, source_target_pairs={{448,0},{449,1},{450,2},{451,3},{452,4},{453,5},{454,6},{455,7},{4... | collective-permute-start | bytes 786440 | tf_op jit(solution)/shard_map/ppermute | solution.py:54
  44.9 15.9 %collective-permute-start.3 = (f32[2,2,32,512]{3,2,1,0:T(8,128)S(1)}, f32[2,2,32,512]{3,2,1,0:T(8,128)S(1)}, u32[]{:S(2)}, u32[]{:S(2)}) collective-permute-start(f32[2,2,32,512]{3,2,1,0:T(8,128)S(1)} %pad_maximum_fusion), channel_id=1, source_target_pairs={{64,0},{65,1},{66,2},{67,3},{68,4},{69,5},{70,6},{71,7},{72,8},{73... | collective-permute-start | bytes 786440 | tf_op jit(solution)/shard_map/ppermute | solution.py:54
  46.8 22.0 %collective-permute-start.6 = (f32[2,32,512]{2,1,0:T(8,128)S(1)}, f32[2,32,512]{2,1,0:T(8,128)S(1)}, u32[]{:S(2)}, u32[]{:S(2)}) collective-permute-start(f32[2,32,512]{2,1,0:T(8,128)S(1)} %collective-permute-done.1), channel_id=1, source_target_pairs={{384,0},{385,1},{386,2},{387,3},{388,4},{389,5},{390,6},{391,7},{3... | collective-permute-start | bytes 393224 | tf_op jit(solution)/shard_map/ppermute | solution.py:54
  58.8 10.0 %collective-permute-start.5 = (f32[2,32,512]{2,1,0:T(8,128)S(1)}, f32[2,32,512]{2,1,0:T(8,128)S(1)}, u32[]{:S(2)}, u32[]{:S(2)}) collective-permute-start(f32[2,32,512]{2,1,0:T(8,128)S(1)} %collective-permute-done.1), channel_id=1, source_target_pairs={{128,0},{129,1},{130,2},{131,3},{132,4},{133,5},{134,6},{135,7},{1... | collective-permute-start | bytes 393224 | tf_op jit(solution)/shard_map/ppermute | solution.py:54
  68.9 25.0 %collective-permute-start.7 = (f32[8,2,32,512]{3,2,1,0:T(8,128)S(1)}, f32[8,2,32,512]{3,2,1,0:T(8,128)S(1)}, u32[]{:S(2)}, u32[]{:S(2)}) collective-permute-start(f32[8,2,32,512]{3,2,1,0:T(8,128)S(1)} %bitcast_dynamic-update-slice_fusion.own), channel_id=1, source_target_pairs={{0,16},{1,48},{2,18},{3,50},{4,20},{5,52},{6,22},{7,54},{8,24},{9,... | collective-permute-start | bytes 3145736 | tf_op jit(solution)/shard_map/ppermute | solution.py:54
  70.8 31.4 %collective-permute-start.9 = (f32[8,2,32,512]{3,2,1,0:T(8,128)S(1)}, f32[8,2,32,512]{3,2,1,0:T(8,128)S(1)}, u32[]{:S(2)}, u32[]{:S(2)}) collective-permute-start(f32[8,2,32,512]{3,2,1,0:T(8,128)S(1)} %bitcast_dynamic-update-slice_fusion.own), channel_id=1, source_target_pairs={{1,0},{3,2},{5,4},{7,6},{9,8},{11,10},{13,12},{15,14},{17,16},{19,... | collective-permute-start | bytes 3145736 | tf_op jit(solution)/shard_map/ppermute | solution.py:54
  72.1 30.1 %collective-permute-start.8 = (f32[8,2,32,512]{3,2,1,0:T(8,128)S(1)}, f32[8,2,32,512]{3,2,1,0:T(8,128)}, u32[]{:S(2)}, u32[]{:S(2)}) collective-permute-start(f32[8,2,32,512]{3,2,1,0:T(8,128)S(1)} %bitcast_dynamic-update-slice_fusion.own), channel_id=1, source_target_pairs={{0,48},{1,16},{2,50},{3,18},{4,52},{5,20},{6,54},{7,22},{8,56},{9,... | collective-permute-start | bytes 3145736 | tf_op jit(solution)/shard_map/ppermute | solution.py:54
  93.9 19.9 %copy-start.2 = (f32[8,2,32,512]{3,2,1,0:T(8,128)}, f32[8,2,32,512]{3,2,1,0:T(8,128)S(1)}, u32[]{:S(2)}) copy-start(f32[8,2,32,512]{3,2,1,0:T(8,128)S(1)} %collective-permute-done.7.first) | copy-start | bytes 3145732
  93.9 16.8 %collective-permute-start.11 = (f32[8,2,32,512]{3,2,1,0:T(8,128)S(1)}, f32[8,2,32,512]{3,2,1,0:T(8,128)}, u32[]{:S(2)}, u32[]{:S(2)}) collective-permute-start(f32[8,2,32,512]{3,2,1,0:T(8,128)S(1)} %collective-permute-done.7.first), channel_id=1, source_target_pairs={{1,17},{3,19},{5,21},{7,23},{9,25},{11,27},{13,29},{15,31},{17,1},... | collective-permute-start | bytes 3145736 | tf_op jit(solution)/shard_map/ppermute | solution.py:54
  95.8 18.0 %collective-permute-start.10 = (f32[8,2,32,512]{3,2,1,0:T(8,128)S(1)}, f32[8,2,32,512]{3,2,1,0:T(8,128)}, u32[]{:S(2)}, u32[]{:S(2)}) collective-permute-start(f32[8,2,32,512]{3,2,1,0:T(8,128)S(1)} %collective-permute-done.7.first), channel_id=1, source_target_pairs={{0,48},{2,50},{4,52},{6,54},{8,56},{10,58},{12,60},{14,62},{16,32}... | collective-permute-start | bytes 3145736 | tf_op jit(solution)/shard_map/ppermute | solution.py:54
  97.9 2.2 %copy-start = (f32[64,32,512]{2,1,0:T(8,128)S(1)}, f32[64,32,512]{2,1,0:T(8,128)}, u32[]{:S(2)}) copy-start(f32[64,32,512]{2,1,0:T(8,128)} %all-gather.3.cloned.1.call-done) | copy-start | bytes 12582916
  102.2 11.6 %copy-start.3 = (f32[8,2,32,512]{3,2,1,0:T(8,128)}, f32[8,2,32,512]{3,2,1,0:T(8,128)S(1)}, u32[]{:S(2)}) copy-start(f32[8,2,32,512]{3,2,1,0:T(8,128)S(1)} %collective-permute-done.9.sibling) | copy-start | bytes 3145732
Sparse Core Ops, SparseCore 0:
  18.0 53.6 all-gather.2

commit v2 on v0

v2 whole, which is shorter than its diff:
```python
import functools
import jax
import jax.numpy as jnp
from jax import lax
from jax.experimental import pallas as pl
from jax.experimental.pallas import tpu as pltpu
from jax.sharding import PartitionSpec as P

BLOCK = 128
NX, NZ, NC = 4, 8, 2
AXES = ("prow", "pcol")
F32, BF16 = jnp.float32, jnp.bfloat16
MIB = 1 << 20
LIFTS = ((0, 4), (2, 6))
OWNER, GROUP = (0, 1, 1, 0), (0, 0, 1, 1)


def device(y, x, z, core):
    return ((y % 8) * NX + x % NX) * NZ * NC + z * NC + core


def every():
    for y in range(8):
        for x in range(NX):
            for z in range(NZ):
                for core in range(NC):
                    yield y, x, z, core


def moved(down_y=0, right_x=0, flip=0):
    return [(device(y, x, z, k), device(y - down_y, x + right_x, z, k ^ flip)) for y, x, z, k in every()]


def to_sibling():
    return moved(flip=1)


def to_previous_row(flip):
    rows, cols = 8 * NX, NZ * NC
    return [(r * cols + c, (r - 1) * cols + (c ^ flip)) for r in range(1, rows) for c in range(cols)]


def transposing(which):
    pairs = []
    for y, x, z, k in every():
        place = [i for i in range(4) if (OWNER[i], GROUP[i]) == (x % 2, k)][0]
        pairs.append((device(y, x, z, k), device(z - y + LIFTS[k][which], place - 2 * (x // 2), y, x // 2)))
    return pairs


def send(value, pairs):
    return lax.ppermute(value, AXES, pairs)


def split(value):
    high = value.astype(BF16)
    return high, (value - high.astype(F32)).astype(BF16)


def dot3(a, b, dims):
    (a_high, a_low), (b_high, b_low) = a, b
    mul = functools.partial(lax.dot_general, dimension_numbers=(dims, ((), ())), preferred_element_type=F32)
    return mul(a_high, b_high) + (mul(a_high, b_low) + mul(a_low, b_high))


def place_kernel(row_ref, targets_ref, own, following, sibling_own, sibling_following, inverse, pieces, both):
    row = row_ref[0]
    blocks = 3
    count = targets_ref.shape[1]
    for panel in range(2):
        for slot in range(4):
            into = slice(slot * BLOCK, (slot + 1) * BLOCK)
            hits = []
            for source in range(2 * blocks):
                index = row * blocks + source
                target = targets_ref[panel, jnp.minimum(index, count - 1)]
                hits.append(jnp.logical_and(index < count, target == row * 4 + slot))
            for core, refs in enumerate(((own, following), (sibling_own, sibling_following))):
                total = jnp.zeros((own.shape[1], BLOCK), F32)
                for source, hit in enumerate(hits):
                    at = (source % blocks) * BLOCK
                    total = jnp.where(hit, refs[source // blocks][panel, :, at : at + BLOCK], total)
                pieces[core, panel, :, into] = total
                if core == 0:
                    both[panel, :, into] = total
        both[2 + panel] = inverse[panel]


def rows_kernel(info, gathered_ref, high, low, scales, weight, scale):
    for panel in range(2):
        inverse = gathered_ref[:, 2 + panel].reshape(512, 512)
        rows = gathered_ref[:, panel].reshape(512, 512)
        factor = dot3(split(inverse), split(rows), ((0,), (0,)))
        largest = jnp.max(jnp.abs(inverse), axis=1, keepdims=True)
        weight[panel] = dot3(split(inverse / largest), split(factor), ((1,), (0,)))
        scale[panel] = jnp.broadcast_to(largest, (512, BLOCK))
    for chunk in range(2):
        for group in range(2):
            pieces = []
            for which in range(2):
                for core in (group, 1 - group):
                    start = pl.multiple_of(info[8 + chunk * 4 + group * 2 + which] * 64 + core * 32, 32)
                    for panel in range(2):
                        into = len(pieces) * 32
                        pieces.append(weight[panel, pl.ds(start, 32), :])
                        scales[chunk, group, into : into + 32, :] = scale[panel, pl.ds(start, 32), :]
            high[chunk, group], low[chunk, group] = split(jnp.concatenate(pieces).T)


def product(value, at, high, low, scale):
    scaled = value.reshape(256, 512) * jnp.concatenate([scale[at]] * 4, axis=1)
    return dot3((high[at], low[at]), split(scaled), ((1,), (0,)))


def part(info, chunk, at, value, weights):
    return product(value[...], (chunk, info[4 + at]), *weights)


def add_to(out, info, at, value):
    where = pl.multiple_of(info[at] * 512, 512)
    out[:, pl.ds(where, 512)] += value


def first_kernel(info, high, low, scale, mine, left, right, across, out):
    out[...] = jnp.zeros(out.shape, F32)
    for at, value in enumerate((mine, left, right, across)):
        add_to(out, info, at, part(info, 0, at, value, (high, low, scale)))


def near_kernel(info, high, low, scale, mine, left, right, begun, out):
    out[...] = begun[...]
    for at, value in enumerate((mine, left, right)):
        add_to(out, info, at, part(info, 1, at, value, (high, low, scale)))


def last_kernel(info, high, low, scale, across, near, out):
    out[...] = near[...]
    add_to(out, info, 3, part(info, 1, 3, across, (high, low, scale)))


def after_kernel(*refs):
    pass


def after(value, *others):
    anywhere = pl.BlockSpec(memory_space=pl.ANY)
    return pl.pallas_call(
        after_kernel,
        out_shape=jax.ShapeDtypeStruct(value.shape, value.dtype),
        in_specs=[anywhere] * (1 + len(others)),
        out_specs=anywhere,
        input_output_aliases={0: 0},
        name="after",
    )(value, *others)


VMEM = pl.BlockSpec(memory_space=pltpu.VMEM)
SMEM = pl.BlockSpec(memory_space=pltpu.SMEM)


def body(panel, inverse, targets):
    row, col = lax.axis_index("prow"), lax.axis_index("pcol")
    y, x, z, core = row // NX, row % NX, col // NC, col % NC

    pieces, both = pl.pallas_call(
        place_kernel,
        out_shape=(jax.ShapeDtypeStruct((2, 2, 32, 512), F32), jax.ShapeDtypeStruct((4, 32, 512), F32)),
        in_specs=[SMEM] * 2 + [VMEM] * 5,
        out_specs=(VMEM, VMEM),
        name="place",
    )(
        row.reshape(1),
        targets,
        panel,
        send(panel, to_previous_row(0)),
        send(panel, to_sibling()),
        send(panel, to_previous_row(1)),
        inverse,
    )

    gathered = lax.all_gather(both, "pcol")

    to_right, to_left = moved(right_x=1), moved(right_x=-1)
    mine = jnp.stack([send(pieces, transposing(0)), send(pieces, transposing(1))])
    late = send(mine, moved(down_y=1))
    left, right = send(mine, to_right), send(mine, to_left)
    across = send(left, to_right)
    late_left, late_right = send(late, to_right), send(late, to_left)
    late_across = send(late_right, to_left)

    holders = (x + 2 * core + jnp.array([0, -1, 1, 2], jnp.int32)) % 4
    sources = jnp.array([chunk - lift for chunk in range(2) for lift in LIFTS[0] + LIFTS[1]], jnp.int32)
    info = jnp.concatenate([(holders + 1) // 2 % 2, holders // 2, (y + z + sources) % 8])

    def kernel(run, out_shape, operands, gflop, name, scratch=()):
        return pl.pallas_call(
            run,
            out_shape=out_shape,
            in_specs=[SMEM] + [VMEM] * len(operands),
            out_specs=(VMEM,) * len(out_shape) if isinstance(out_shape, tuple) else VMEM,
            scratch_shapes=scratch,
            compiler_params=pltpu.CompilerParams(vmem_limit_bytes=28 * MIB),
            cost_estimate=pl.CostEstimate(flops=int(gflop * 1e9), bytes_accessed=4 * MIB, transcendentals=0),
            name=name,
        )(info, *operands)

    halves = jax.ShapeDtypeStruct((2, 2, 512, 256), BF16)
    scratch = [pltpu.VMEM((2, 512, 512), F32), pltpu.VMEM((2, 512, BLOCK), F32)]
    made = (halves, halves, jax.ShapeDtypeStruct((2, 2, 256, BLOCK), F32))
    weights = kernel(rows_kernel, made, (gathered,), 3.2, "rows", scratch)

    result = jax.ShapeDtypeStruct((512, 1024), F32)
    total = kernel(first_kernel, result, weights + (mine, left, right, across), 1.6, "first")
    total = kernel(near_kernel, result, weights + (late, late_left, late_right, total), 1.2, "near")
    return kernel(last_kernel, result, weights + (late_across, total), 0.4, "last")


def solution(mesh):
    specs = (P(None, "pcol", "prow"), P(None, "pcol", None), P())
    return jax.shard_map(body, mesh=mesh, in_specs=specs, out_specs=P("prow", "pcol"), check_vma=False)
```

time: 408 us -> 120 us (0.29)
  the two profiles are of different devices: /device:TPU:64 before, /device:TPU:89 now
where the time goes in v2:
time: 120 us
  waiting for transfers between devices  48 us (40%)
  starting transfers between devices  38.7 us (32%)
  Pallas kernels  15 us (12%)
  between operations  13.6 us (11%)
  local copies, waits for them, and re-layouts  2.82 us (2%)
  other arithmetic  1.48 us (1%)
    ppermute x12, waiting for transfers between devices, send(): return lax.ppermute(value, AXES, pairs)  48 us
    ppermute x12, starting transfers between devices, send(): return lax.ppermute(value, AXES, pairs)  38.7 us
    pallas_call x4, Pallas kernels, kernel(): pl.pallas_call(run, out_shape=out_shape, in_specs=[SMEM] + [VMEM] * len(o...  13 us
    unnamed x8, local copies, waits for them, and re-layouts  2.82 us
  transfers between devices with their start and end apart: 13, of which 8 were waited for; matrix products, arithmetic and copies ran while one was open for 1% of the time, Pallas kernels for 8%

profile of v2, /device:TPU:89, one launch (start us, length us, event | category | flops | bytes accessed | tf_op | source)
XLA Modules:
  0.0 119.7 jit_solution(1659595374691710472)
XLA Ops:
  6.5 2.6 %collective-permute-start.1 = (f32[2,32,384]{2,1,0:T(8,128)}, f32[2,32,384]{2,1,0:T(8,128)S(1)}, u32[]{:S(2)}, u32[]{:S(2)}) collective-permute-start(f32[2,32,384]{2,1,0:T(8,128)} %own.1), channel_id=1, source_target_pairs={{0,1},{1,0},{2,3},{3,2},{4,5},{5,4},{6,7},{7,6},{8,9},{9,8},{10,11... | collective-permute-start | bytes 294920 | tf_op jit(solution)/shard_map/ppermute | solution.py:52
  9.1 4.3 %collective-permute-start = (f32[2,32,384]{2,1,0:T(8,128)}, f32[2,32,384]{2,1,0:T(8,128)S(1)}, u32[]{:S(2)}, u32[]{:S(2)}) collective-permute-start(f32[2,32,384]{2,1,0:T(8,128)} %own.1), channel_id=1, source_target_pairs={{16,0},{17,1},{18,2},{19,3},{20,4},{21,5},{22,6},{23,7},{24,8},{25... | collective-permute-start | bytes 294920 | tf_op jit(solution)/shard_map/ppermute | solution.py:52
  13.4 2.6 %collective-permute-start.2 = (f32[2,32,384]{2,1,0:T(8,128)}, f32[2,32,384]{2,1,0:T(8,128)S(1)}, u32[]{:S(2)}, u32[]{:S(2)}) collective-permute-start(f32[2,32,384]{2,1,0:T(8,128)} %own.1), channel_id=1, source_target_pairs={{16,1},{17,0},{18,3},{19,2},{20,5},{21,4},{22,7},{23,6},{24,9},{25... | collective-permute-start | bytes 294920 | tf_op jit(solution)/shard_map/ppermute | solution.py:52
  16.1 4.1 %collective-permute-done.2.sibling_following = f32[2,32,384]{2,1,0:T(8,128)S(1)} collective-permute-done((f32[2,32,384]{2,1,0:T(8,128)}, f32[2,32,384]{2,1,0:T(8,128)S(1)}, u32[]{:S(2)}, u32[]{:S(2)}) %collective-permute-start.2) | collective-permute-done | bytes 98336 | tf_op jit(solution)/shard_map/ppermute | solution.py:52
  20.2 0.6 copy-done.3
  20.8 2.0 %place.1 = (f32[2,2,32,512]{3,2,1,0:T(8,128)}, f32[4,32,512]{2,1,0:T(8,128)}) custom-call(s32[1]{0:T(128)} %bitcast.row_ref, s32[2,96]{1,0:T(2,128)} %targets_ref.1, f32[2,32,384]{2,1,0:T(8,128)} %own.1, f32[2,32,384]{2,1,0:T(8,128)} %copy-done.2, f32[2,32,384]{2,1,0:T(8,128)} %copy-done.1, f32[2,32,384]{2,1,0:T(8,128)} %copy-done.3, f32[2,32,512]{2,1,0:T(8,128)} %inverse.1), custom_call_target="tpu_custom_call" | custom-call | tf_op jit(solution)/shard_map/place/pallas_call | solution.py:165
  22.8 0.0 all-gather.3.cloned.1.call-update
  22.8 10.8 %collective-permute-start.4 = (f32[2,2,32,512]{3,2,1,0:T(8,128)}, f32[2,2,32,512]{3,2,1,0:T(8,128)S(1)}, u32[]{:S(2)}, u32[]{:S(2)}) collective-permute-start(f32[2,2,32,512]{3,2,1,0:T(8,128)} %get-tuple-element.14), channel_id=1, source_target_pairs={{0,256},{1,432},{2,320},{3,496},{4,384},{5,48},{6,448},{7,112},{8,... | collective-permute-start | bytes 786440 | tf_op jit(solution)/shard_map/ppermute | solution.py:52
  33.6 1.9 %collective-permute-start.3 = (f32[2,2,32,512]{3,2,1,0:T(8,128)}, f32[2,2,32,512]{3,2,1,0:T(8,128)S(1)}, u32[]{:S(2)}, u32[]{:S(2)}) collective-permute-start(f32[2,2,32,512]{3,2,1,0:T(8,128)} %get-tuple-element.14), channel_id=1, source_target_pairs={{0,0},{1,176},{2,64},{3,240},{4,128},{5,304},{6,192},{7,368},{8,25... | collective-permute-start | bytes 786440 | tf_op jit(solution)/shard_map/ppermute | solution.py:52
  35.6 11.0 %collective-permute-done.4 = f32[2,2,32,512]{3,2,1,0:T(8,128)S(1)} collective-permute-done((f32[2,2,32,512]{3,2,1,0:T(8,128)}, f32[2,2,32,512]{3,2,1,0:T(8,128)S(1)}, u32[]{:S(2)}, u32[]{:S(2)}) %collective-permute-start.4) | collective-permute-done | bytes 262176 | tf_op jit(solution)/shard_map/ppermute | solution.py:52
  46.6 6.3 %collective-permute-done.3 = f32[2,2,32,512]{3,2,1,0:T(8,128)S(1)} collective-permute-done((f32[2,2,32,512]{3,2,1,0:T(8,128)}, f32[2,2,32,512]{3,2,1,0:T(8,128)S(1)}, u32[]{:S(2)}, u32[]{:S(2)}) %collective-permute-start.3) | collective-permute-done | bytes 262176 | tf_op jit(solution)/shard_map/ppermute | solution.py:52
  52.9 1.9 %collective-permute-start.5 = (f32[2,2,2,32,512]{4,3,2,1,0:T(8,128)S(1)}, f32[2,2,2,32,512]{4,3,2,1,0:T(8,128)S(1)}, u32[]{:S(2)}, u32[]{:S(2)}) collective-permute-start(f32[2,2,2,32,512]{4,3,2,1,0:T(8,128)S(1)} %pad_maximum_fusion.mine), channel_id=1, source_target_pairs={{0,448},{1,449},{2,450},{3,451},{4,452},{5,453},{6,454},{7,455},{8... | collective-permute-start | bytes 1572872 | tf_op jit(solution)/shard_map/ppermute | solution.py:52
  54.8 1.9 %collective-permute-start.9 = (f32[2,2,2,32,512]{4,3,2,1,0:T(8,128)S(1)}, f32[2,2,2,32,512]{4,3,2,1,0:T(8,128)S(1)}, u32[]{:S(2)}, u32[]{:S(2)}) collective-permute-start(f32[2,2,2,32,512]{4,3,2,1,0:T(8,128)S(1)} %pad_maximum_fusion.mine), channel_id=1, source_target_pairs={{0,16},{1,17},{2,18},{3,19},{4,20},{5,21},{6,22},{7,23},{8,24},{9,... | collective-permute-start | bytes 1572872 | tf_op jit(solution)/shard_map/ppermute | solution.py:52
  56.8 0.7 and_select_fusion.2
  57.5 14.9 %collective-permute-done.5.mine = f32[2,2,2,32,512]{4,3,2,1,0:T(8,128)S(1)} collective-permute-done((f32[2,2,2,32,512]{4,3,2,1,0:T(8,128)S(1)}, f32[2,2,2,32,512]{4,3,2,1,0:T(8,128)S(1)}, u32[]{:S(2)}, u32[]{:S(2)}) %collective-permute-start.5) | collective-permute-done | bytes 524320 | tf_op jit(solution)/shard_map/ppermute | solution.py:52
  72.4 1.9 %collective-permute-start.6 = (f32[2,2,2,32,512]{4,3,2,1,0:T(8,128)S(1)}, f32[2,2,2,32,512]{4,3,2,1,0:T(8,128)S(1)}, u32[]{:S(2)}, u32[]{:S(2)}) collective-permute-start(f32[2,2,2,32,512]{4,3,2,1,0:T(8,128)S(1)} %collective-permute-done.5.mine), channel_id=1, source_target_pairs={{0,48},{1,49},{2,50},{3,51},{4,52},{5,53},{6,54},{7,55},{8,56},{9,... | collective-permute-start | bytes 1572872 | tf_op jit(solution)/shard_map/ppermute | solution.py:52
  74.3 1.9 %collective-permute-start.10 = (f32[2,2,2,32,512]{4,3,2,1,0:T(8,128)S(1)}, f32[2,2,2,32,512]{4,3,2,1,0:T(8,128)S(1)}, u32[]{:S(2)}, u32[]{:S(2)}) collective-permute-start(f32[2,2,2,32,512]{4,3,2,1,0:T(8,128)S(1)} %pad_maximum_fusion.mine), channel_id=1, source_target_pairs={{0,48},{1,49},{2,50},{3,51},{4,52},{5,53},{6,54},{7,55},{8,56},{9,... | collective-permute-start | bytes 1572872 | tf_op jit(solution)/shard_map/ppermute | solution.py:52
  76.2 3.4 %collective-permute-start.11 = (f32[2,2,2,32,512]{4,3,2,1,0:T(8,128)S(1)}, f32[2,2,2,32,512]{4,3,2,1,0:T(8,128)}, u32[]{:S(2)}, u32[]{:S(2)}) collective-permute-start(f32[2,2,2,32,512]{4,3,2,1,0:T(8,128)S(1)} %collective-permute-done.9.left), channel_id=1, source_target_pairs={{0,16},{1,17},{2,18},{3,19},{4,20},{5,21},{6,22},{7,23},{8,24},{9,... | collective-permute-start | bytes 1572872 | tf_op jit(solution)/shard_map/ppermute | solution.py:52
  79.6 0.7 and_select_fusion
  80.3 3.4 %collective-permute-start.8 = (f32[2,2,2,32,512]{4,3,2,1,0:T(8,128)S(1)}, f32[2,2,2,32,512]{4,3,2,1,0:T(8,128)S(1)}, u32[]{:S(2)}, u32[]{:S(2)}) collective-permute-start(f32[2,2,2,32,512]{4,3,2,1,0:T(8,128)S(1)} %collective-permute-done.5.mine), channel_id=1, source_target_pairs={{0,16},{1,17},{2,18},{3,19},{4,20},{5,21},{6,22},{7,23},{8,24},{9,... | collective-permute-start | bytes 1572872 | tf_op jit(solution)/shard_map/ppermute | solution.py:52
  83.6 0.1 pad_add_fusion.info
  83.7 4.5 %collective-permute-done.6.right = f32[2,2,2,32,512]{4,3,2,1,0:T(8,128)S(1)} collective-permute-done((f32[2,2,2,32,512]{4,3,2,1,0:T(8,128)S(1)}, f32[2,2,2,32,512]{4,3,2,1,0:T(8,128)S(1)}, u32[]{:S(2)}, u32[]{:S(2)}) %collective-permute-start.6) | collective-permute-done | bytes 524320 | tf_op jit(solution)/shard_map/ppermute | solution.py:52
  88.2 2.2 %collective-permute-start.7 = (f32[2,2,2,32,512]{4,3,2,1,0:T(8,128)S(1)}, f32[2,2,2,32,512]{4,3,2,1,0:T(8,128)}, u32[]{:S(2)}, u32[]{:S(2)}) collective-permute-start(f32[2,2,2,32,512]{4,3,2,1,0:T(8,128)S(1)} %collective-permute-done.6.right), channel_id=1, source_target_pairs={{0,48},{1,49},{2,50},{3,51},{4,52},{5,53},{6,54},{7,55},{8,56},{9,... | collective-permute-start | bytes 1572872 | tf_op jit(solution)/shard_map/ppermute | solution.py:52
  90.4 0.0 all-gather.3.cloned.1.call-done
  90.5 2.2 %copy-done = f32[64,32,512]{2,1,0:T(8,128)S(1)} copy-done((f32[64,32,512]{2,1,0:T(8,128)S(1)}, f32[64,32,512]{2,1,0:T(8,128)}, u32[]{:S(2)}) %copy-start) | copy-done | bytes 4194328
  92.6 4.9 %rows.1 = (bf16[2,2,512,256]{3,2,1,0:T(8,128)(2,1)S(1)}, bf16[2,2,512,256]{3,2,1,0:T(8,128)(2,1)S(1)}, f32[2,2,256,128]{3,2,1,0:T(8,128)S(1)}) custom-call(s32[16]{0:T(128)S(1)} %pad_add_fusion.info, f32[16,4,32,512]{3,2,1,0:T(8,128)S(1)} %bitcast.4), custom_call_target="tpu_custom_call" | custom-call | flops 3200000000 | bytes 4194304 | tf_op jit(solution)/shard_map/rows/pallas_call | solution.py:196
  97.5 2.0 %collective-permute-done.10.right = f32[2,2,2,32,512]{4,3,2,1,0:T(8,128)S(1)} collective-permute-done((f32[2,2,2,32,512]{4,3,2,1,0:T(8,128)S(1)}, f32[2,2,2,32,512]{4,3,2,1,0:T(8,128)S(1)}, u32[]{:S(2)}, u32[]{:S(2)}) %collective-permute-start.10) | collective-permute-done | bytes 524320 | tf_op jit(solution)/shard_map/ppermute | solution.py:52
  99.5 3.1 %first.1.begun = f32[512,1024]{1,0:T(8,128)S(1)} custom-call(s32[16]{0:T(128)S(1)} %pad_add_fusion.info, bf16[2,2,512,256]{3,2,1,0:T(8,128)(2,1)S(1)} %get-tuple-element.11.high, bf16[2,2,512,256]{3,2,1,0:T(8,128)(2,1)S(1)} %get-tuple-element.12.low, f32[2,2,256,128]{3,2,1,0:T(8,128)S(1)} %get-tuple-element.13.scale, ...), custom_call_target="tpu_custom_call" | custom-call | flops 1600000000 | bytes 4194304 | tf_op jit(solution)/shard_map/first/pallas_call | solution.py:196
  102.6 0.7 collective-permute-done.8.left
  103.3 2.1 %near.1 = f32[512,1024]{1,0:T(8,128)S(1)} custom-call(s32[16]{0:T(128)S(1)} %pad_add_fusion.info, bf16[2,2,512,256]{3,2,1,0:T(8,128)(2,1)S(1)} %get-tuple-element.11.high, bf16[2,2,512,256]{3,2,1,0:T(8,128)(2,1)S(1)} %get-tuple-element.12.low, f32[2,2,256,128]{3,2,1,0:T(8,128)S(1)} %get-tuple-element.13.scale, ...), custom_call_target="tpu_custom_call" | custom-call | flops 1200000000 | bytes 4194304 | tf_op jit(solution)/shard_map/near/pallas_call | solution.py:196
  105.4 4.5 %collective-permute-done.7.across = f32[2,2,2,32,512]{4,3,2,1,0:T(8,128)} collective-permute-done((f32[2,2,2,32,512]{4,3,2,1,0:T(8,128)S(1)}, f32[2,2,2,32,512]{4,3,2,1,0:T(8,128)}, u32[]{:S(2)}, u32[]{:S(2)}) %collective-permute-start.7) | collective-permute-done | bytes 524320 | tf_op jit(solution)/shard_map/ppermute | solution.py:52
  109.9 3.0 %last.1 = f32[512,1024]{1,0:T(8,128)} custom-call(s32[16]{0:T(128)S(1)} %pad_add_fusion.info, bf16[2,2,512,256]{3,2,1,0:T(8,128)(2,1)S(1)} %get-tuple-element.11.high, bf16[2,2,512,256]{3,2,1,0:T(8,128)(2,1)S(1)} %get-tuple-element.12.low, f32[2,2,256,128]{3,2,1,0:T(8,128)S(1)} %get-tuple-element.13.scale, ...), custom_call_target="tpu_custom_call" | custom-call | flops 400000000 | bytes 4194304 | tf_op jit(solution)/shard_map/last/pallas_call | solution.py:196
  (13 shorter events, 0.1 us)
Async XLA Ops:
  6.5 83.9 %all-gather.3.cloned.1.call-start = ((), (), s32[]{:S(2)}) async-start(), calls=%async_computation | async-start | bytes 4456448 | tf_op jit(solution)/shard_map/all_gather | solution.py:181
  6.5 9.5 %collective-permute-start.1 = (f32[2,32,384]{2,1,0:T(8,128)}, f32[2,32,384]{2,1,0:T(8,128)S(1)}, u32[]{:S(2)}, u32[]{:S(2)}) collective-permute-start(f32[2,32,384]{2,1,0:T(8,128)} %own.1), channel_id=1, source_target_pairs={{0,1},{1,0},{2,3},{3,2},{4,5},{5,4},{6,7},{7,6},{8,9},{9,8},{10,11... | collective-permute-start | bytes 294920 | tf_op jit(solution)/shard_map/ppermute | solution.py:52
  9.1 7.0 %collective-permute-start = (f32[2,32,384]{2,1,0:T(8,128)}, f32[2,32,384]{2,1,0:T(8,128)S(1)}, u32[]{:S(2)}, u32[]{:S(2)}) collective-permute-start(f32[2,32,384]{2,1,0:T(8,128)} %own.1), channel_id=1, source_target_pairs={{16,0},{17,1},{18,2},{19,3},{20,4},{21,5},{22,6},{23,7},{24,8},{25... | collective-permute-start | bytes 294920 | tf_op jit(solution)/shard_map/ppermute | solution.py:52
  13.4 6.8 %collective-permute-start.2 = (f32[2,32,384]{2,1,0:T(8,128)}, f32[2,32,384]{2,1,0:T(8,128)S(1)}, u32[]{:S(2)}, u32[]{:S(2)}) collective-permute-start(f32[2,32,384]{2,1,0:T(8,128)} %own.1), channel_id=1, source_target_pairs={{16,1},{17,0},{18,3},{19,2},{20,5},{21,4},{22,7},{23,6},{24,9},{25... | collective-permute-start | bytes 294920 | tf_op jit(solution)/shard_map/ppermute | solution.py:52
  16.1 4.1 %copy-start.1 = (f32[2,32,384]{2,1,0:T(8,128)}, f32[2,32,384]{2,1,0:T(8,128)S(1)}, u32[]{:S(2)}) copy-start(f32[2,32,384]{2,1,0:T(8,128)S(1)} %collective-permute-done.1.sibling_own) | copy-start | bytes 294916
  16.1 4.1 %copy-start.2 = (f32[2,32,384]{2,1,0:T(8,128)}, f32[2,32,384]{2,1,0:T(8,128)S(1)}, u32[]{:S(2)}) copy-start(f32[2,32,384]{2,1,0:T(8,128)S(1)} %collective-permute-done.following) | copy-start | bytes 294916
  20.2 0.6 copy-start.3
  22.8 23.7 %collective-permute-start.4 = (f32[2,2,32,512]{3,2,1,0:T(8,128)}, f32[2,2,32,512]{3,2,1,0:T(8,128)S(1)}, u32[]{:S(2)}, u32[]{:S(2)}) collective-permute-start(f32[2,2,32,512]{3,2,1,0:T(8,128)} %get-tuple-element.14), channel_id=1, source_target_pairs={{0,256},{1,432},{2,320},{3,496},{4,384},{5,48},{6,448},{7,112},{8,... | collective-permute-start | bytes 786440 | tf_op jit(solution)/shard_map/ppermute | solution.py:52
  33.6 19.2 %collective-permute-start.3 = (f32[2,2,32,512]{3,2,1,0:T(8,128)}, f32[2,2,32,512]{3,2,1,0:T(8,128)S(1)}, u32[]{:S(2)}, u32[]{:S(2)}) collective-permute-start(f32[2,2,32,512]{3,2,1,0:T(8,128)} %get-tuple-element.14), channel_id=1, source_target_pairs={{0,0},{1,176},{2,64},{3,240},{4,128},{5,304},{6,192},{7,368},{8,25... | collective-permute-start | bytes 786440 | tf_op jit(solution)/shard_map/ppermute | solution.py:52
  52.9 19.5 %collective-permute-start.5 = (f32[2,2,2,32,512]{4,3,2,1,0:T(8,128)S(1)}, f32[2,2,2,32,512]{4,3,2,1,0:T(8,128)S(1)}, u32[]{:S(2)}, u32[]{:S(2)}) collective-permute-start(f32[2,2,2,32,512]{4,3,2,1,0:T(8,128)S(1)} %pad_maximum_fusion.mine), channel_id=1, source_target_pairs={{0,448},{1,449},{2,450},{3,451},{4,452},{5,453},{6,454},{7,455},{8... | collective-permute-start | bytes 1572872 | tf_op jit(solution)/shard_map/ppermute | solution.py:52
  54.8 21.4 %collective-permute-start.9 = (f32[2,2,2,32,512]{4,3,2,1,0:T(8,128)S(1)}, f32[2,2,2,32,512]{4,3,2,1,0:T(8,128)S(1)}, u32[]{:S(2)}, u32[]{:S(2)}) collective-permute-start(f32[2,2,2,32,512]{4,3,2,1,0:T(8,128)S(1)} %pad_maximum_fusion.mine), channel_id=1, source_target_pairs={{0,16},{1,17},{2,18},{3,19},{4,20},{5,21},{6,22},{7,23},{8,24},{9,... | collective-permute-start | bytes 1572872 | tf_op jit(solution)/shard_map/ppermute | solution.py:52
  72.4 15.9 %collective-permute-start.6 = (f32[2,2,2,32,512]{4,3,2,1,0:T(8,128)S(1)}, f32[2,2,2,32,512]{4,3,2,1,0:T(8,128)S(1)}, u32[]{:S(2)}, u32[]{:S(2)}) collective-permute-start(f32[2,2,2,32,512]{4,3,2,1,0:T(8,128)S(1)} %collective-permute-done.5.mine), channel_id=1, source_target_pairs={{0,48},{1,49},{2,50},{3,51},{4,52},{5,53},{6,54},{7,55},{8,56},{9,... | collective-permute-start | bytes 1572872 | tf_op jit(solution)/shard_map/ppermute | solution.py:52
  74.3 25.2 %collective-permute-start.10 = (f32[2,2,2,32,512]{4,3,2,1,0:T(8,128)S(1)}, f32[2,2,2,32,512]{4,3,2,1,0:T(8,128)S(1)}, u32[]{:S(2)}, u32[]{:S(2)}) collective-permute-start(f32[2,2,2,32,512]{4,3,2,1,0:T(8,128)S(1)} %pad_maximum_fusion.mine), channel_id=1, source_target_pairs={{0,48},{1,49},{2,50},{3,51},{4,52},{5,53},{6,54},{7,55},{8,56},{9,... | collective-permute-start | bytes 1572872 | tf_op jit(solution)/shard_map/ppermute | solution.py:52
  76.2 23.2 %collective-permute-start.11 = (f32[2,2,2,32,512]{4,3,2,1,0:T(8,128)S(1)}, f32[2,2,2,32,512]{4,3,2,1,0:T(8,128)}, u32[]{:S(2)}, u32[]{:S(2)}) collective-permute-start(f32[2,2,2,32,512]{4,3,2,1,0:T(8,128)S(1)} %collective-permute-done.9.left), channel_id=1, source_target_pairs={{0,16},{1,17},{2,18},{3,19},{4,20},{5,21},{6,22},{7,23},{8,24},{9,... | collective-permute-start | bytes 1572872 | tf_op jit(solution)/shard_map/ppermute | solution.py:52
  80.3 23.0 %collective-permute-start.8 = (f32[2,2,2,32,512]{4,3,2,1,0:T(8,128)S(1)}, f32[2,2,2,32,512]{4,3,2,1,0:T(8,128)S(1)}, u32[]{:S(2)}, u32[]{:S(2)}) collective-permute-start(f32[2,2,2,32,512]{4,3,2,1,0:T(8,128)S(1)} %collective-permute-done.5.mine), channel_id=1, source_target_pairs={{0,16},{1,17},{2,18},{3,19},{4,20},{5,21},{6,22},{7,23},{8,24},{9,... | collective-permute-start | bytes 1572872 | tf_op jit(solution)/shard_map/ppermute | solution.py:52
  88.2 21.7 %collective-permute-start.7 = (f32[2,2,2,32,512]{4,3,2,1,0:T(8,128)S(1)}, f32[2,2,2,32,512]{4,3,2,1,0:T(8,128)}, u32[]{:S(2)}, u32[]{:S(2)}) collective-permute-start(f32[2,2,2,32,512]{4,3,2,1,0:T(8,128)S(1)} %collective-permute-done.6.right), channel_id=1, source_target_pairs={{0,48},{1,49},{2,50},{3,51},{4,52},{5,53},{6,54},{7,55},{8,56},{9,... | collective-permute-start | bytes 1572872 | tf_op jit(solution)/shard_map/ppermute | solution.py:52
  90.4 2.2 %copy-start = (f32[64,32,512]{2,1,0:T(8,128)S(1)}, f32[64,32,512]{2,1,0:T(8,128)}, u32[]{:S(2)}) copy-start(f32[64,32,512]{2,1,0:T(8,128)} %all-gather.3.cloned.1.call-done) | copy-start | bytes 12582916
Sparse Core Ops, SparseCore 0:
  23.0 56.2 all-gather.2

commit v3 on v2

--- a/solution.py
+++ b/solution.py
@@ -27,12 +27,16 @@
                     yield y, x, z, core
 
 
-def moved(down_y=0, right_x=0, flip=0):
-    return [(device(y, x, z, k), device(y - down_y, x + right_x, z, k ^ flip)) for y, x, z, k in every()]
+def swapped(x_of):
+    return [(device(y, x, z, k), device(y, x_of(x), z, k)) for y, x, z, k in every()]
+
+
+def from_y(distance):
+    return [(device(y + distance, x, z, k), device(y, x, z, k)) for y, x, z, k in every()]
 
 
 def to_sibling():
-    return moved(flip=1)
+    return [(device(y, x, z, k), device(y, x, z, 1 - k)) for y, x, z, k in every()]
 
 
 def to_previous_row(flip):
@@ -94,7 +98,7 @@
         largest = jnp.max(jnp.abs(inverse), axis=1, keepdims=True)
         weight[panel] = dot3(split(inverse / largest), split(factor), ((1,), (0,)))
         scale[panel] = jnp.broadcast_to(largest, (512, BLOCK))
-    for chunk in range(2):
+    for chunk in range(3):
         for group in range(2):
             pieces = []
             for which in range(2):
@@ -121,37 +125,16 @@
     out[:, pl.ds(where, 512)] += value
 
 
-def first_kernel(info, high, low, scale, mine, left, right, across, out):
+def first_kernel(info, high, low, scale, mine, mate, next_one, above, below, out):
     out[...] = jnp.zeros(out.shape, F32)
-    for at, value in enumerate((mine, left, right, across)):
-        add_to(out, info, at, part(info, 0, at, value, (high, low, scale)))
-
-
-def near_kernel(info, high, low, scale, mine, left, right, begun, out):
+    for chunk, at, value in ((0, 0, mine), (0, 1, mate), (0, 2, next_one), (1, 0, above), (2, 0, below)):
+        add_to(out, info, at, part(info, chunk, at, value, (high, low, scale)))
+
+
+def last_kernel(info, high, low, scale, across, above_mate, below_mate, begun, out):
     out[...] = begun[...]
-    for at, value in enumerate((mine, left, right)):
-        add_to(out, info, at, part(info, 1, at, value, (high, low, scale)))
-
-
-def last_kernel(info, high, low, scale, across, near, out):
-    out[...] = near[...]
-    add_to(out, info, 3, part(info, 1, 3, across, (high, low, scale)))
-
-
-def after_kernel(*refs):
-    pass
-
-
-def after(value, *others):
-    anywhere = pl.BlockSpec(memory_space=pl.ANY)
-    return pl.pallas_call(
-        after_kernel,
-        out_shape=jax.ShapeDtypeStruct(value.shape, value.dtype),
-        in_specs=[anywhere] * (1 + len(others)),
-        out_specs=anywhere,
-        input_output_aliases={0: 0},
-        name="after",
-    )(value, *others)
+    for chunk, at, value in ((0, 3, across), (1, 1, above_mate), (2, 1, below_mate)):
+        add_to(out, info, at, part(info, chunk, at, value, (high, low, scale)))
 
 
 VMEM = pl.BlockSpec(memory_space=pltpu.VMEM)
@@ -180,17 +163,17 @@
 
     gathered = lax.all_gather(both, "pcol")
 
-    to_right, to_left = moved(right_x=1), moved(right_x=-1)
     mine = jnp.stack([send(pieces, transposing(0)), send(pieces, transposing(1))])
-    late = send(mine, moved(down_y=1))
-    left, right = send(mine, to_right), send(mine, to_left)
-    across = send(left, to_right)
-    late_left, late_right = send(late, to_right), send(late, to_left)
-    late_across = send(late_right, to_left)
-
-    holders = (x + 2 * core + jnp.array([0, -1, 1, 2], jnp.int32)) % 4
-    sources = jnp.array([chunk - lift for chunk in range(2) for lift in LIFTS[0] + LIFTS[1]], jnp.int32)
-    info = jnp.concatenate([(holders + 1) // 2 % 2, holders // 2, (y + z + sources) % 8])
+    to_mate, to_next = swapped(lambda x: x ^ 1), swapped(lambda x: 3 - x)
+    mate, next_one = send(mine, to_mate), send(mine, to_next)
+    above, below = send(mine, from_y(1)), send(mine, from_y(-1))
+    above_mate, below_mate = send(mate, from_y(1)), send(mate, from_y(-1))
+    across = send(next_one, to_mate)
+
+    w = (x + 2 * core) & 3
+    holders = jnp.stack([w, w ^ 1, 3 - w, w ^ 2])
+    sources = jnp.array([step - lift for step in (0, 1, -1) for lift in LIFTS[0] + LIFTS[1]], jnp.int32)
+    info = jnp.concatenate([((holders + 1) >> 1) & 1, holders >> 1, (y + z + sources) & 7])
 
     def kernel(run, out_shape, operands, gflop, name, scratch=()):
         return pl.pallas_call(
@@ -204,15 +187,13 @@
             name=name,
         )(info, *operands)
 
-    halves = jax.ShapeDtypeStruct((2, 2, 512, 256), BF16)
+    halves = jax.ShapeDtypeStruct((3, 2, 512, 256), BF16)
     scratch = [pltpu.VMEM((2, 512, 512), F32), pltpu.VMEM((2, 512, BLOCK), F32)]
-    made = (halves, halves, jax.ShapeDtypeStruct((2, 2, 256, BLOCK), F32))
+    made = (halves, halves, jax.ShapeDtypeStruct((3, 2, 256, BLOCK), F32))
     weights = kernel(rows_kernel, made, (gathered,), 3.2, "rows", scratch)
-
     result = jax.ShapeDtypeStruct((512, 1024), F32)
-    total = kernel(first_kernel, result, weights + (mine, left, right, across), 1.6, "first")
-    total = kernel(near_kernel, result, weights + (late, late_left, late_right, total), 1.2, "near")
-    return kernel(last_kernel, result, weights + (late_across, total), 0.4, "last")
+    total = kernel(first_kernel, result, weights + (mine, mate, next_one, above, below), 2.0, "first")
+    return kernel(last_kernel, result, weights + (across, above_mate, below_mate, total), 1.2, "last")
 
 
 def solution(mesh):

time: 120 us -> 107 us (0.89)
  the two profiles are of different devices: /device:TPU:89 before, /device:TPU:26 now
where the time goes in v3:
time: 107 us; the launch traced here: 106 us
  starting transfers between devices  55.1 us (51%)
  waiting for transfers between devices  19.6 us (18%)
  Pallas kernels  14.2 us (13%)
  between operations  13.6 us (13%)
  local copies, waits for them, and re-layouts  2.82 us (3%)
    ppermute x12, starting transfers between devices, send(): return lax.ppermute(value, AXES, pairs)  55.1 us
    ppermute x12, waiting for transfers between devices, send(): return lax.ppermute(value, AXES, pairs)  19.2 us
    pallas_call x3, Pallas kernels, kernel(): pl.pallas_call(run, out_shape=out_shape, in_specs=[SMEM] + [VMEM] * len(o...  12.3 us
    unnamed x8, local copies, waits for them, and re-layouts  2.82 us
  transfers between devices with their start and end apart: 13, of which 5 were waited for; matrix products, arithmetic and copies ran while one was open for 1% of the time, Pallas kernels for 8%

profile of v3, /device:TPU:26, one launch (start us, length us, event | category | flops | bytes accessed | tf_op | source)
XLA Modules:
  0.0 106.2 jit_solution(6975699330923438544)
XLA Ops:
  6.5 1.9 %collective-permute-start.1 = (f32[2,32,384]{2,1,0:T(8,128)}, f32[2,32,384]{2,1,0:T(8,128)S(1)}, u32[]{:S(2)}, u32[]{:S(2)}) collective-permute-start(f32[2,32,384]{2,1,0:T(8,128)} %own.1), channel_id=1, source_target_pairs={{0,1},{1,0},{2,3},{3,2},{4,5},{5,4},{6,7},{7,6},{8,9},{9,8},{10,11... | collective-permute-start | bytes 294920 | tf_op jit(solution)/shard_map/ppermute | solution.py:56
  8.5 2.4 %collective-permute-start = (f32[2,32,384]{2,1,0:T(8,128)}, f32[2,32,384]{2,1,0:T(8,128)S(1)}, u32[]{:S(2)}, u32[]{:S(2)}) collective-permute-start(f32[2,32,384]{2,1,0:T(8,128)} %own.1), channel_id=1, source_target_pairs={{16,0},{17,1},{18,2},{19,3},{20,4},{21,5},{22,6},{23,7},{24,8},{25... | collective-permute-start | bytes 294920 | tf_op jit(solution)/shard_map/ppermute | solution.py:56
  10.9 4.4 %collective-permute-start.2 = (f32[2,32,384]{2,1,0:T(8,128)}, f32[2,32,384]{2,1,0:T(8,128)S(1)}, u32[]{:S(2)}, u32[]{:S(2)}) collective-permute-start(f32[2,32,384]{2,1,0:T(8,128)} %own.1), channel_id=1, source_target_pairs={{16,1},{17,0},{18,3},{19,2},{20,5},{21,4},{22,7},{23,6},{24,9},{25... | collective-permute-start | bytes 294920 | tf_op jit(solution)/shard_map/ppermute | solution.py:56
  15.3 0.0 collective-permute-done.1.sibling_own
  15.3 0.4 collective-permute-done.following
  15.8 2.6 %collective-permute-done.2.sibling_following = f32[2,32,384]{2,1,0:T(8,128)S(1)} collective-permute-done((f32[2,32,384]{2,1,0:T(8,128)}, f32[2,32,384]{2,1,0:T(8,128)S(1)}, u32[]{:S(2)}, u32[]{:S(2)}) %collective-permute-start.2) | collective-permute-done | bytes 98336 | tf_op jit(solution)/shard_map/ppermute | solution.py:56
  18.4 0.6 copy-done.3
  19.0 2.0 %place.1 = (f32[2,2,32,512]{3,2,1,0:T(8,128)}, f32[4,32,512]{2,1,0:T(8,128)}) custom-call(s32[1]{0:T(128)} %bitcast.4.row_ref, s32[2,96]{1,0:T(2,128)} %targets_ref.1, f32[2,32,384]{2,1,0:T(8,128)} %own.1, f32[2,32,384]{2,1,0:T(8,128)} %copy-done.2, f32[2,32,384]{2,1,0:T(8,128)} %copy-done.1, f32[2,32,384]{2,1,0:T(8,128)} %copy-done.3, f32[2,32,512]{2,1,0:T(8,128)} %inverse.1), custom_call_target="tpu_custom_call" | custom-call | tf_op jit(solution)/shard_map/place/pallas_call | solution.py:148
  21.0 0.0 all-gather.3.cloned.1.call-update
  21.0 7.7 %collective-permute-start.4 = (f32[2,2,32,512]{3,2,1,0:T(8,128)}, f32[2,2,32,512]{3,2,1,0:T(8,128)S(1)}, u32[]{:S(2)}, u32[]{:S(2)}) collective-permute-start(f32[2,2,32,512]{3,2,1,0:T(8,128)} %get-tuple-element.14), channel_id=1, source_target_pairs={{0,256},{1,432},{2,320},{3,496},{4,384},{5,48},{6,448},{7,112},{8,... | collective-permute-start | bytes 786440 | tf_op jit(solution)/shard_map/ppermute | solution.py:56
  28.7 9.5 %collective-permute-start.3 = (f32[2,2,32,512]{3,2,1,0:T(8,128)}, f32[2,2,32,512]{3,2,1,0:T(8,128)S(1)}, u32[]{:S(2)}, u32[]{:S(2)}) collective-permute-start(f32[2,2,32,512]{3,2,1,0:T(8,128)} %get-tuple-element.14), channel_id=1, source_target_pairs={{0,0},{1,176},{2,64},{3,240},{4,128},{5,304},{6,192},{7,368},{8,25... | collective-permute-start | bytes 786440 | tf_op jit(solution)/shard_map/ppermute | solution.py:56
  38.3 10.9 %collective-permute-done.3 = f32[2,2,32,512]{3,2,1,0:T(8,128)S(1)} collective-permute-done((f32[2,2,32,512]{3,2,1,0:T(8,128)}, f32[2,2,32,512]{3,2,1,0:T(8,128)S(1)}, u32[]{:S(2)}, u32[]{:S(2)}) %collective-permute-start.3) | collective-permute-done | bytes 262176 | tf_op jit(solution)/shard_map/ppermute | solution.py:56
  49.2 4.6 %collective-permute-start.7 = (f32[2,2,2,32,512]{4,3,2,1,0:T(8,128)S(1)}, f32[2,2,2,32,512]{4,3,2,1,0:T(8,128)S(1)}, u32[]{:S(2)}, u32[]{:S(2)}) collective-permute-start(f32[2,2,2,32,512]{4,3,2,1,0:T(8,128)S(1)} %pad_maximum_fusion.mine), channel_id=1, source_target_pairs={{0,16},{1,17},{2,18},{3,19},{4,20},{5,21},{6,22},{7,23},{8,24},{9,... | collective-permute-start | bytes 1572872 | tf_op jit(solution)/shard_map/ppermute | solution.py:56
  53.8 1.9 %collective-permute-start.5 = (f32[2,2,2,32,512]{4,3,2,1,0:T(8,128)S(1)}, f32[2,2,2,32,512]{4,3,2,1,0:T(8,128)S(1)}, u32[]{:S(2)}, u32[]{:S(2)}) collective-permute-start(f32[2,2,2,32,512]{4,3,2,1,0:T(8,128)S(1)} %pad_maximum_fusion.mine), channel_id=1, source_target_pairs={{0,48},{1,49},{2,50},{3,51},{4,52},{5,53},{6,54},{7,55},{8,56},{9,... | collective-permute-start | bytes 1572872 | tf_op jit(solution)/shard_map/ppermute | solution.py:56
  55.8 0.1 shift-right-arithmetic_and_fusion
  55.9 11.2 %collective-permute-start.11 = (f32[2,2,2,32,512]{4,3,2,1,0:T(8,128)S(1)}, f32[2,2,2,32,512]{4,3,2,1,0:T(8,128)S(1)}, u32[]{:S(2)}, u32[]{:S(2)}) collective-permute-start(f32[2,2,2,32,512]{4,3,2,1,0:T(8,128)S(1)} %pad_maximum_fusion.mine), channel_id=1, source_target_pairs={{448,0},{449,1},{450,2},{451,3},{452,4},{453,5},{454,6},{455,7},{4... | collective-permute-start | bytes 1572872 | tf_op jit(solution)/shard_map/ppermute | solution.py:56
  67.1 1.9 %collective-permute-start.10 = (f32[2,2,2,32,512]{4,3,2,1,0:T(8,128)S(1)}, f32[2,2,2,32,512]{4,3,2,1,0:T(8,128)S(1)}, u32[]{:S(2)}, u32[]{:S(2)}) collective-permute-start(f32[2,2,2,32,512]{4,3,2,1,0:T(8,128)S(1)} %pad_maximum_fusion.mine), channel_id=1, source_target_pairs={{64,0},{65,1},{66,2},{67,3},{68,4},{69,5},{70,6},{71,7},{72,8},{73... | collective-permute-start | bytes 1572872 | tf_op jit(solution)/shard_map/ppermute | solution.py:56
  69.0 0.7 add_and_fusion
  69.6 0.0 collective-permute-done.7.mate
  69.6 5.1 %collective-permute-start.9 = (f32[2,2,2,32,512]{4,3,2,1,0:T(8,128)S(1)}, f32[2,2,2,32,512]{4,3,2,1,0:T(8,128)S(1)}, u32[]{:S(2)}, u32[]{:S(2)}) collective-permute-start(f32[2,2,2,32,512]{4,3,2,1,0:T(8,128)S(1)} %collective-permute-done.7.mate), channel_id=1, source_target_pairs={{448,0},{449,1},{450,2},{451,3},{452,4},{453,5},{454,6},{455,7},{4... | collective-permute-start | bytes 1572872 | tf_op jit(solution)/shard_map/ppermute | solution.py:56
  74.8 1.9 %collective-permute-start.8 = (f32[2,2,2,32,512]{4,3,2,1,0:T(8,128)S(1)}, f32[2,2,2,32,512]{4,3,2,1,0:T(8,128)}, u32[]{:S(2)}, u32[]{:S(2)}) collective-permute-start(f32[2,2,2,32,512]{4,3,2,1,0:T(8,128)S(1)} %collective-permute-done.7.mate), channel_id=1, source_target_pairs={{64,0},{65,1},{66,2},{67,3},{68,4},{69,5},{70,6},{71,7},{72,8},{73... | collective-permute-start | bytes 1572872 | tf_op jit(solution)/shard_map/ppermute | solution.py:56
  76.7 0.0 collective-permute-done.5.next_one
  76.7 2.5 %collective-permute-start.6 = (f32[2,2,2,32,512]{4,3,2,1,0:T(8,128)S(1)}, f32[2,2,2,32,512]{4,3,2,1,0:T(8,128)}, u32[]{:S(2)}, u32[]{:S(2)}) collective-permute-start(f32[2,2,2,32,512]{4,3,2,1,0:T(8,128)S(1)} %collective-permute-done.5.next_one), channel_id=1, source_target_pairs={{0,16},{1,17},{2,18},{3,19},{4,20},{5,21},{6,22},{7,23},{8,24},{9,... | collective-permute-start | bytes 1572872 | tf_op jit(solution)/shard_map/ppermute | solution.py:56
  79.3 0.1 pad_add_fusion.1.info
  79.3 0.4 all-gather.3.cloned.1.call-done
  79.8 2.2 %copy-done = f32[64,32,512]{2,1,0:T(8,128)S(1)} copy-done((f32[64,32,512]{2,1,0:T(8,128)S(1)}, f32[64,32,512]{2,1,0:T(8,128)}, u32[]{:S(2)}) %copy-start) | copy-done | bytes 4194328
  81.9 5.1 %rows.1 = (bf16[3,2,512,256]{3,2,1,0:T(8,128)(2,1)S(1)}, bf16[3,2,512,256]{3,2,1,0:T(8,128)(2,1)S(1)}, f32[3,2,256,128]{3,2,1,0:T(8,128)S(1)}) custom-call(s32[20]{0:T(128)S(1)} %pad_add_fusion.1.info, f32[16,4,32,512]{3,2,1,0:T(8,128)S(1)} %bitcast.8), custom_call_target="tpu_custom_call" | custom-call | flops 3200000000 | bytes 4194304 | tf_op jit(solution)/shard_map/rows/pallas_call | solution.py:179
  87.1 0.0 collective-permute-done.11.below
  87.1 0.0 collective-permute-done.10.above
  87.1 3.0 %first.1.begun = f32[512,1024]{1,0:T(8,128)S(1)} custom-call(s32[20]{0:T(128)S(1)} %pad_add_fusion.1.info, bf16[3,2,512,256]{3,2,1,0:T(8,128)(2,1)S(1)} %get-tuple-element.11.high, bf16[3,2,512,256]{3,2,1,0:T(8,128)(2,1)S(1)} %get-tuple-element.12.low, f32[3,2,256,128]{3,2,1,0:T(8,128)S(1)} %get-tuple-element.13.scale, ...), custom_call_target="tpu_custom_call" | custom-call | flops 2000000000 | bytes 4194304 | tf_op jit(solution)/shard_map/first/pallas_call | solution.py:179
  90.2 5.2 %collective-permute-done.8.above_mate = f32[2,2,2,32,512]{4,3,2,1,0:T(8,128)} collective-permute-done((f32[2,2,2,32,512]{4,3,2,1,0:T(8,128)S(1)}, f32[2,2,2,32,512]{4,3,2,1,0:T(8,128)}, u32[]{:S(2)}, u32[]{:S(2)}) %collective-permute-start.8) | collective-permute-done | bytes 524320 | tf_op jit(solution)/shard_map/ppermute | solution.py:56
  95.3 4.1 %last.1 = f32[512,1024]{1,0:T(8,128)} custom-call(s32[20]{0:T(128)S(1)} %pad_add_fusion.1.info, bf16[3,2,512,256]{3,2,1,0:T(8,128)(2,1)S(1)} %get-tuple-element.11.high, bf16[3,2,512,256]{3,2,1,0:T(8,128)(2,1)S(1)} %get-tuple-element.12.low, f32[3,2,256,128]{3,2,1,0:T(8,128)S(1)} %get-tuple-element.13.scale, ...), custom_call_target="tpu_custom_call" | custom-call | flops 1200000000 | bytes 4194304 | tf_op jit(solution)/shard_map/last/pallas_call | solution.py:179
  (12 shorter events, 0.1 us)
Async XLA Ops:
  6.5 73.2 %all-gather.3.cloned.1.call-start = ((), (), s32[]{:S(2)}) async-start(), calls=%async_computation | async-start | bytes 4456448 | tf_op jit(solution)/shard_map/all_gather | solution.py:164
  6.5 8.8 %collective-permute-start.1 = (f32[2,32,384]{2,1,0:T(8,128)}, f32[2,32,384]{2,1,0:T(8,128)S(1)}, u32[]{:S(2)}, u32[]{:S(2)}) collective-permute-start(f32[2,32,384]{2,1,0:T(8,128)} %own.1), channel_id=1, source_target_pairs={{0,1},{1,0},{2,3},{3,2},{4,5},{5,4},{6,7},{7,6},{8,9},{9,8},{10,11... | collective-permute-start | bytes 294920 | tf_op jit(solution)/shard_map/ppermute | solution.py:56
  8.5 7.3 %collective-permute-start = (f32[2,32,384]{2,1,0:T(8,128)}, f32[2,32,384]{2,1,0:T(8,128)S(1)}, u32[]{:S(2)}, u32[]{:S(2)}) collective-permute-start(f32[2,32,384]{2,1,0:T(8,128)} %own.1), channel_id=1, source_target_pairs={{16,0},{17,1},{18,2},{19,3},{20,4},{21,5},{22,6},{23,7},{24,8},{25... | collective-permute-start | bytes 294920 | tf_op jit(solution)/shard_map/ppermute | solution.py:56
  10.9 7.5 %collective-permute-start.2 = (f32[2,32,384]{2,1,0:T(8,128)}, f32[2,32,384]{2,1,0:T(8,128)S(1)}, u32[]{:S(2)}, u32[]{:S(2)}) collective-permute-start(f32[2,32,384]{2,1,0:T(8,128)} %own.1), channel_id=1, source_target_pairs={{16,1},{17,0},{18,3},{19,2},{20,5},{21,4},{22,7},{23,6},{24,9},{25... | collective-permute-start | bytes 294920 | tf_op jit(solution)/shard_map/ppermute | solution.py:56
  15.3 3.1 %copy-start.1 = (f32[2,32,384]{2,1,0:T(8,128)}, f32[2,32,384]{2,1,0:T(8,128)S(1)}, u32[]{:S(2)}) copy-start(f32[2,32,384]{2,1,0:T(8,128)S(1)} %collective-permute-done.1.sibling_own) | copy-start | bytes 294916
  15.8 2.6 %copy-start.2 = (f32[2,32,384]{2,1,0:T(8,128)}, f32[2,32,384]{2,1,0:T(8,128)S(1)}, u32[]{:S(2)}) copy-start(f32[2,32,384]{2,1,0:T(8,128)S(1)} %collective-permute-done.following) | copy-start | bytes 294916
  18.4 0.6 copy-start.3
  21.0 17.3 %collective-permute-start.4 = (f32[2,2,32,512]{3,2,1,0:T(8,128)}, f32[2,2,32,512]{3,2,1,0:T(8,128)S(1)}, u32[]{:S(2)}, u32[]{:S(2)}) collective-permute-start(f32[2,2,32,512]{3,2,1,0:T(8,128)} %get-tuple-element.14), channel_id=1, source_target_pairs={{0,256},{1,432},{2,320},{3,496},{4,384},{5,48},{6,448},{7,112},{8,... | collective-permute-start | bytes 786440 | tf_op jit(solution)/shard_map/ppermute | solution.py:56
  28.7 20.5 %collective-permute-start.3 = (f32[2,2,32,512]{3,2,1,0:T(8,128)}, f32[2,2,32,512]{3,2,1,0:T(8,128)S(1)}, u32[]{:S(2)}, u32[]{:S(2)}) collective-permute-start(f32[2,2,32,512]{3,2,1,0:T(8,128)} %get-tuple-element.14), channel_id=1, source_target_pairs={{0,0},{1,176},{2,64},{3,240},{4,128},{5,304},{6,192},{7,368},{8,25... | collective-permute-start | bytes 786440 | tf_op jit(solution)/shard_map/ppermute | solution.py:56
  49.2 20.4 %collective-permute-start.7 = (f32[2,2,2,32,512]{4,3,2,1,0:T(8,128)S(1)}, f32[2,2,2,32,512]{4,3,2,1,0:T(8,128)S(1)}, u32[]{:S(2)}, u32[]{:S(2)}) collective-permute-start(f32[2,2,2,32,512]{4,3,2,1,0:T(8,128)S(1)} %pad_maximum_fusion.mine), channel_id=1, source_target_pairs={{0,16},{1,17},{2,18},{3,19},{4,20},{5,21},{6,22},{7,23},{8,24},{9,... | collective-permute-start | bytes 1572872 | tf_op jit(solution)/shard_map/ppermute | solution.py:56
  53.8 22.9 %collective-permute-start.5 = (f32[2,2,2,32,512]{4,3,2,1,0:T(8,128)S(1)}, f32[2,2,2,32,512]{4,3,2,1,0:T(8,128)S(1)}, u32[]{:S(2)}, u32[]{:S(2)}) collective-permute-start(f32[2,2,2,32,512]{4,3,2,1,0:T(8,128)S(1)} %pad_maximum_fusion.mine), channel_id=1, source_target_pairs={{0,48},{1,49},{2,50},{3,51},{4,52},{5,53},{6,54},{7,55},{8,56},{9,... | collective-permute-start | bytes 1572872 | tf_op jit(solution)/shard_map/ppermute | solution.py:56
  55.9 31.2 %collective-permute-start.11 = (f32[2,2,2,32,512]{4,3,2,1,0:T(8,128)S(1)}, f32[2,2,2,32,512]{4,3,2,1,0:T(8,128)S(1)}, u32[]{:S(2)}, u32[]{:S(2)}) collective-permute-start(f32[2,2,2,32,512]{4,3,2,1,0:T(8,128)S(1)} %pad_maximum_fusion.mine), channel_id=1, source_target_pairs={{448,0},{449,1},{450,2},{451,3},{452,4},{453,5},{454,6},{455,7},{4... | collective-permute-start | bytes 1572872 | tf_op jit(solution)/shard_map/ppermute | solution.py:56
  67.1 20.0 %collective-permute-start.10 = (f32[2,2,2,32,512]{4,3,2,1,0:T(8,128)S(1)}, f32[2,2,2,32,512]{4,3,2,1,0:T(8,128)S(1)}, u32[]{:S(2)}, u32[]{:S(2)}) collective-permute-start(f32[2,2,2,32,512]{4,3,2,1,0:T(8,128)S(1)} %pad_maximum_fusion.mine), channel_id=1, source_target_pairs={{64,0},{65,1},{66,2},{67,3},{68,4},{69,5},{70,6},{71,7},{72,8},{73... | collective-permute-start | bytes 1572872 | tf_op jit(solution)/shard_map/ppermute | solution.py:56
  69.6 20.5 %collective-permute-start.9 = (f32[2,2,2,32,512]{4,3,2,1,0:T(8,128)S(1)}, f32[2,2,2,32,512]{4,3,2,1,0:T(8,128)S(1)}, u32[]{:S(2)}, u32[]{:S(2)}) collective-permute-start(f32[2,2,2,32,512]{4,3,2,1,0:T(8,128)S(1)} %collective-permute-done.7.mate), channel_id=1, source_target_pairs={{448,0},{449,1},{450,2},{451,3},{452,4},{453,5},{454,6},{455,7},{4... | collective-permute-start | bytes 1572872 | tf_op jit(solution)/shard_map/ppermute | solution.py:56
  74.8 20.5 %collective-permute-start.8 = (f32[2,2,2,32,512]{4,3,2,1,0:T(8,128)S(1)}, f32[2,2,2,32,512]{4,3,2,1,0:T(8,128)}, u32[]{:S(2)}, u32[]{:S(2)}) collective-permute-start(f32[2,2,2,32,512]{4,3,2,1,0:T(8,128)S(1)} %collective-permute-done.7.mate), channel_id=1, source_target_pairs={{64,0},{65,1},{66,2},{67,3},{68,4},{69,5},{70,6},{71,7},{72,8},{73... | collective-permute-start | bytes 1572872 | tf_op jit(solution)/shard_map/ppermute | solution.py:56
  76.7 18.6 %collective-permute-start.6 = (f32[2,2,2,32,512]{4,3,2,1,0:T(8,128)S(1)}, f32[2,2,2,32,512]{4,3,2,1,0:T(8,128)}, u32[]{:S(2)}, u32[]{:S(2)}) collective-permute-start(f32[2,2,2,32,512]{4,3,2,1,0:T(8,128)S(1)} %collective-permute-done.5.next_one), channel_id=1, source_target_pairs={{0,16},{1,17},{2,18},{3,19},{4,20},{5,21},{6,22},{7,23},{8,24},{9,... | collective-permute-start | bytes 1572872 | tf_op jit(solution)/shard_map/ppermute | solution.py:56
  79.8 2.2 %copy-start = (f32[64,32,512]{2,1,0:T(8,128)S(1)}, f32[64,32,512]{2,1,0:T(8,128)}, u32[]{:S(2)}) copy-start(f32[64,32,512]{2,1,0:T(8,128)} %all-gather.3.cloned.1.call-done) | copy-start | bytes 12582916
Sparse Core Ops, SparseCore 0:
  21.1 58.5 all-gather.2

commit v4 on v3

v4 whole, which is shorter than its diff:
```python
import functools
import jax
import jax.numpy as jnp
from jax import lax
from jax.experimental import pallas as pl
from jax.experimental.pallas import tpu as pltpu
from jax.sharding import PartitionSpec as P

BLOCK = 128
NX, NZ, NC = 4, 8, 2
AXES = ("prow", "pcol")
F32, BF16 = jnp.float32, jnp.bfloat16
MIB = 1 << 20
LIFTS = ((0, 4), (2, 6))
OWNER, GROUP = (0, 1, 1, 0), (0, 0, 1, 1)


def device(y, x, z, core):
    return ((y % 8) * NX + x % NX) * NZ * NC + z * NC + core


def every():
    for y in range(8):
        for x in range(NX):
            for z in range(NZ):
                for core in range(NC):
                    yield y, x, z, core


def swapped(x_of):
    return [(device(y, x, z, k), device(y, x_of(x), z, k)) for y, x, z, k in every()]


def from_y(distance):
    return [(device(y + distance, x, z, k), device(y, x, z, k)) for y, x, z, k in every()]


def to_sibling():
    return [(device(y, x, z, k), device(y, x, z, 1 - k)) for y, x, z, k in every()]


def to_previous_row():
    rows, cols = 8 * NX, NZ * NC
    return [(r * cols + c, (r - 1) * cols + c) for r in range(1, rows) for c in range(cols)]


def transposing(which):
    pairs = []
    for y, x, z, k in every():
        place = [i for i in range(4) if (OWNER[i], GROUP[i]) == (x % 2, k)][0]
        pairs.append((device(y, x, z, k), device(z - y + LIFTS[k][which], place - 2 * (x // 2), y, x // 2)))
    return pairs


def send(value, pairs):
    return lax.ppermute(value, AXES, pairs)


def split(value):
    high = value.astype(BF16)
    return high, (value - high.astype(F32)).astype(BF16)


def dot3(a, b, dims):
    (a_high, a_low), (b_high, b_low) = a, b
    mul = functools.partial(lax.dot_general, dimension_numbers=(dims, ((), ())), preferred_element_type=F32)
    return mul(a_high, b_high) + (mul(a_high, b_low) + mul(a_low, b_high))


def place_kernel(row_ref, targets_ref, own_ref, next_ref, inverse_ref, placed_ref, both_ref):
    row = row_ref[0]
    blocks = 3
    count = targets_ref.shape[1]
    for panel in range(2):
        for slot in range(4):
            total = jnp.zeros((own_ref.shape[1], BLOCK), F32)
            for source in range(2 * blocks):
                index = row * blocks + source
                target = targets_ref[panel, jnp.minimum(index, count - 1)]
                hit = jnp.logical_and(index < count, target == row * 4 + slot)
                ref = own_ref if source < blocks else next_ref
                at = (source % blocks) * BLOCK
                total = jnp.where(hit, ref[panel, :, at : at + BLOCK], total)
            placed_ref[panel, :, slot * BLOCK : (slot + 1) * BLOCK] = total
            both_ref[panel, :, slot * BLOCK : (slot + 1) * BLOCK] = total
        both_ref[2 + panel] = inverse_ref[panel]


def rows_kernel(info, rows_ref, inverse_ref, high, low, scales, weight, scale):
    panel = pl.program_id(0)
    inverse = inverse_ref[:, 0].reshape(512, 512)
    factor = dot3(split(inverse), split(rows_ref[:, 0].reshape(512, 512)), ((0,), (0,)))
    largest = jnp.max(jnp.abs(inverse), axis=1, keepdims=True)
    weight[panel] = dot3(split(inverse / largest), split(factor), ((1,), (0,)))
    scale[panel] = jnp.broadcast_to(largest, (512, BLOCK))

    @pl.when(panel == 1)
    def _():
        for chunk in range(3):
            for group in range(2):
                pieces = []
                for which in range(2):
                    for core in (group, 1 - group):
                        start = pl.multiple_of(info[8 + chunk * 4 + group * 2 + which] * 64 + core * 32, 32)
                        for panel in range(2):
                            into = len(pieces) * 32
                            pieces.append(weight[panel, pl.ds(start, 32), :])
                            scales[chunk, group, into : into + 32, :] = scale[panel, pl.ds(start, 32), :]
                high[chunk, group], low[chunk, group] = split(jnp.concatenate(pieces).T)


def product(info, weights, parts):
    high, low, scale = weights
    total = None
    for chunk, at, ref in parts:
        group = info[4 + at]
        value = ref[...].reshape(256, 512) * jnp.concatenate([scale[chunk, group]] * 4, axis=1)
        one = dot3((high[chunk, group], low[chunk, group]), split(value), ((1,), (0,)))
        total = one if total is None else total + one
    return total


def first_kernel(info, high, low, scale, mine, mate, next_one, above, below, out):
    weights = high, low, scale
    at, other = pl.multiple_of(info[0] * 512, 512), pl.multiple_of(info[1] * 512, 512)
    out[:, pl.ds(at, 512)] = product(info, weights, ((0, 0, mine), (0, 2, next_one), (1, 0, above), (2, 0, below)))
    out[:, pl.ds(other, 512)] = product(info, weights, ((0, 1, mate),))


def last_kernel(info, high, low, scale, across, above_mate, below_mate, begun, out):
    parts = (0, 3, across), (1, 1, above_mate), (2, 1, below_mate)
    out[...] = begun[...]
    out[:, pl.ds(pl.multiple_of(info[1] * 512, 512), 512)] += product(info, (high, low, scale), parts)


VMEM = pl.BlockSpec(memory_space=pltpu.VMEM)
SMEM = pl.BlockSpec(memory_space=pltpu.SMEM)


def body(panel, inverse, targets):
    row, col = lax.axis_index("prow"), lax.axis_index("pcol")
    y, x, z, core = row // NX, row % NX, col // NC, col % NC

    following = send(panel, to_previous_row())
    placed, both = pl.pallas_call(
        place_kernel,
        out_shape=(jax.ShapeDtypeStruct((2, 32, 512), F32), jax.ShapeDtypeStruct((4, 32, 512), F32)),
        in_specs=[SMEM, SMEM, VMEM, VMEM, VMEM],
        out_specs=(VMEM, VMEM),
        name="place",
    )(row.reshape(1), targets, panel, following, inverse)

    gathered = lax.all_gather(both, "pcol")

    pieces = jnp.stack([placed, send(placed, to_sibling())])
    mine = jnp.stack([send(pieces, transposing(0)), send(pieces, transposing(1))])
    to_mate, to_next = swapped(lambda x: x ^ 1), swapped(lambda x: 3 - x)
    mate, next_one = send(mine, to_mate), send(mine, to_next)
    above, below = send(mine, from_y(1)), send(mine, from_y(-1))
    above_mate, below_mate = send(mate, from_y(1)), send(mate, from_y(-1))
    across = send(next_one, to_mate)

    w = (x + 2 * core) & 3
    holders = jnp.stack([w, w ^ 1, 3 - w, w ^ 2])
    sources = jnp.array([step - lift for step in (0, 1, -1) for lift in LIFTS[0] + LIFTS[1]], jnp.int32)
    info = jnp.concatenate([((holders + 1) >> 1) & 1, holders >> 1, (y + z + sources) & 7])

    def kernel(run, out_shape, operands, gflop, name, **more):
        return pl.pallas_call(
            run,
            out_shape=out_shape,
            compiler_params=pltpu.CompilerParams(vmem_limit_bytes=28 * MIB),
            cost_estimate=pl.CostEstimate(flops=int(gflop * 1e9), bytes_accessed=4 * MIB, transcendentals=0),
            name=name,
            **more,
        )(info, *operands)

    halves = jax.ShapeDtypeStruct((3, 2, 512, 256), BF16)
    made = (halves, halves, jax.ShapeDtypeStruct((3, 2, 256, BLOCK), F32))
    weights = kernel(
        rows_kernel,
        made,
        (gathered, gathered),
        3.2,
        "rows",
        grid=(2,),
        in_specs=[
            SMEM,
            pl.BlockSpec((16, 1, 32, 512), lambda panel: (0, panel, 0, 0)),
            pl.BlockSpec((16, 1, 32, 512), lambda panel: (0, panel + 2, 0, 0)),
        ],
        out_specs=[pl.BlockSpec(one.shape, lambda panel, rank=len(one.shape): (0,) * rank) for one in made],
        scratch_shapes=[pltpu.VMEM((2, 512, 512), F32), pltpu.VMEM((2, 512, BLOCK), F32)],
    )
    result = jax.ShapeDtypeStruct((512, 1024), F32)
    total = kernel(
        first_kernel,
        result,
        (*weights, mine, mate, next_one, above, below),
        2.0,
        "first",
        in_specs=[SMEM] + [VMEM] * 8,
        out_specs=VMEM,
    )
    return kernel(
        last_kernel,
        result,
        (*weights, across, above_mate, below_mate, total),
        1.2,
        "last",
        in_specs=[SMEM] + [VMEM] * 7,
        out_specs=VMEM,
    )


def solution(mesh):
    specs = (P(None, "pcol", "prow"), P(None, "pcol", None), P())
    return jax.shard_map(body, mesh=mesh, in_specs=specs, out_specs=P("prow", "pcol"), check_vma=False)
```

time: 107 us -> 104 us (0.972)
  the two profiles are of different devices: /device:TPU:26 before, /device:TPU:29 now
where the time goes in v4:
time: 104 us; the launch traced here: 103 us
  starting transfers between devices  55 us (53%)
  waiting for transfers between devices  16.6 us (16%)
  Pallas kernels  14 us (13%)
  between operations  13.6 us (13%)
  local copies, waits for them, and re-layouts  2.83 us (3%)
  other arithmetic  1.13 us (1%)
    ppermute x11, starting transfers between devices, send(): return lax.ppermute(value, AXES, pairs)  55 us
    ppermute x11, waiting for transfers between devices, send(): return lax.ppermute(value, AXES, pairs)  16 us
    pallas_call x3, Pallas kernels, kernel(): pl.pallas_call(run, out_shape=out_shape, compiler_params=pltpu.CompilerPa...  12.2 us
    unnamed x6, local copies, waits for them, and re-layouts  2.83 us
  transfers between devices with their start and end apart: 12, of which 6 were waited for; matrix products, arithmetic and copies ran while one was open for 1% of the time, Pallas kernels for 8%

profile of v4, /device:TPU:29, one launch (start us, length us, event | category | flops | bytes accessed | tf_op | source)
XLA Modules:
  0.0 103.3 jit_solution(14633283964678928136)
XLA Ops:
  6.5 2.3 %collective-permute-start = (f32[2,32,384]{2,1,0:T(8,128)}, f32[2,32,384]{2,1,0:T(8,128)S(1)}, u32[]{:S(2)}, u32[]{:S(2)}) collective-permute-start(f32[2,32,384]{2,1,0:T(8,128)} %own_ref.1), channel_id=1, source_target_pairs={{16,0},{17,1},{18,2},{19,3},{20,4},{21,5},{22,6},{23,7},{24,8},{25... | collective-permute-start | bytes 294920 | tf_op jit(solution)/shard_map/ppermute | solution.py:56
  8.8 3.4 %collective-permute-done.next_ref = f32[2,32,384]{2,1,0:T(8,128)S(1)} collective-permute-done((f32[2,32,384]{2,1,0:T(8,128)}, f32[2,32,384]{2,1,0:T(8,128)S(1)}, u32[]{:S(2)}, u32[]{:S(2)}) %collective-permute-start) | collective-permute-done | bytes 98336 | tf_op jit(solution)/shard_map/ppermute | solution.py:56
  12.2 0.6 copy-done.1
  12.9 1.8 %place.1 = (f32[2,32,512]{2,1,0:T(8,128)}, f32[4,32,512]{2,1,0:T(8,128)}) custom-call(s32[1]{0:T(128)} %bitcast.4.row_ref, s32[2,96]{1,0:T(2,128)} %targets_ref.1, f32[2,32,384]{2,1,0:T(8,128)} %own_ref.1, f32[2,32,384]{2,1,0:T(8,128)} %copy-done.1, f32[2,32,512]{2,1,0:T(8,128)} %inverse_ref.1), custom_call_target="tpu_custom_call" | custom-call | tf_op jit(solution)/shard_map/place/pallas_call | solution.py:145
  14.7 0.0 all-gather.3.cloned.1.call-update
  14.7 3.7 %collective-permute-start.1 = (f32[2,32,512]{2,1,0:T(8,128)}, f32[2,32,512]{2,1,0:T(8,128)S(1)}, u32[]{:S(2)}, u32[]{:S(2)}) collective-permute-start(f32[2,32,512]{2,1,0:T(8,128)} %get-tuple-element.14), channel_id=1, source_target_pairs={{0,1},{1,0},{2,3},{3,2},{4,5},{5,4},{6,7},{7,6},{8,9},{9,8},{10,11... | collective-permute-start | bytes 393224 | tf_op jit(solution)/shard_map/ppermute | solution.py:56
  18.5 1.2 %collective-permute-done.1 = f32[2,32,512]{2,1,0:T(8,128)S(1)} collective-permute-done((f32[2,32,512]{2,1,0:T(8,128)}, f32[2,32,512]{2,1,0:T(8,128)S(1)}, u32[]{:S(2)}, u32[]{:S(2)}) %collective-permute-start.1) | collective-permute-done | bytes 131104 | tf_op jit(solution)/shard_map/ppermute | solution.py:56
  19.6 0.9 pad_maximum_fusion.1
  20.6 7.6 %collective-permute-start.3 = (f32[2,2,32,512]{3,2,1,0:T(8,128)S(1)}, f32[2,2,32,512]{3,2,1,0:T(8,128)S(1)}, u32[]{:S(2)}, u32[]{:S(2)}) collective-permute-start(f32[2,2,32,512]{3,2,1,0:T(8,128)S(1)} %pad_maximum_fusion.1), channel_id=1, source_target_pairs={{0,256},{1,432},{2,320},{3,496},{4,384},{5,48},{6,448},{7,112},{8,... | collective-permute-start | bytes 786440 | tf_op jit(solution)/shard_map/ppermute | solution.py:56
  28.2 12.9 %collective-permute-start.2 = (f32[2,2,32,512]{3,2,1,0:T(8,128)S(1)}, f32[2,2,32,512]{3,2,1,0:T(8,128)S(1)}, u32[]{:S(2)}, u32[]{:S(2)}) collective-permute-start(f32[2,2,32,512]{3,2,1,0:T(8,128)S(1)} %pad_maximum_fusion.1), channel_id=1, source_target_pairs={{0,0},{1,176},{2,64},{3,240},{4,128},{5,304},{6,192},{7,368},{8,25... | collective-permute-start | bytes 786440 | tf_op jit(solution)/shard_map/ppermute | solution.py:56
  41.1 0.0 collective-permute-done.3
  41.1 5.4 %collective-permute-done.2 = f32[2,2,32,512]{3,2,1,0:T(8,128)S(1)} collective-permute-done((f32[2,2,32,512]{3,2,1,0:T(8,128)S(1)}, f32[2,2,32,512]{3,2,1,0:T(8,128)S(1)}, u32[]{:S(2)}, u32[]{:S(2)}) %collective-permute-start.2) | collective-permute-done | bytes 262176 | tf_op jit(solution)/shard_map/ppermute | solution.py:56
  46.6 4.1 %collective-permute-start.6 = (f32[2,2,2,32,512]{4,3,2,1,0:T(8,128)S(1)}, f32[2,2,2,32,512]{4,3,2,1,0:T(8,128)S(1)}, u32[]{:S(2)}, u32[]{:S(2)}) collective-permute-start(f32[2,2,2,32,512]{4,3,2,1,0:T(8,128)S(1)} %pad_maximum_fusion.mine), channel_id=1, source_target_pairs={{0,16},{1,17},{2,18},{3,19},{4,20},{5,21},{6,22},{7,23},{8,24},{9,... | collective-permute-start | bytes 1572872 | tf_op jit(solution)/shard_map/ppermute | solution.py:56
  50.7 8.2 %collective-permute-start.4 = (f32[2,2,2,32,512]{4,3,2,1,0:T(8,128)S(1)}, f32[2,2,2,32,512]{4,3,2,1,0:T(8,128)S(1)}, u32[]{:S(2)}, u32[]{:S(2)}) collective-permute-start(f32[2,2,2,32,512]{4,3,2,1,0:T(8,128)S(1)} %pad_maximum_fusion.mine), channel_id=1, source_target_pairs={{0,48},{1,49},{2,50},{3,51},{4,52},{5,53},{6,54},{7,55},{8,56},{9,... | collective-permute-start | bytes 1572872 | tf_op jit(solution)/shard_map/ppermute | solution.py:56
  59.0 0.1 shift-right-arithmetic_and_fusion
  59.1 5.2 %collective-permute-start.10 = (f32[2,2,2,32,512]{4,3,2,1,0:T(8,128)S(1)}, f32[2,2,2,32,512]{4,3,2,1,0:T(8,128)S(1)}, u32[]{:S(2)}, u32[]{:S(2)}) collective-permute-start(f32[2,2,2,32,512]{4,3,2,1,0:T(8,128)S(1)} %pad_maximum_fusion.mine), channel_id=1, source_target_pairs={{448,0},{449,1},{450,2},{451,3},{452,4},{453,5},{454,6},{455,7},{4... | collective-permute-start | bytes 1572872 | tf_op jit(solution)/shard_map/ppermute | solution.py:56
  64.2 1.9 %collective-permute-start.9 = (f32[2,2,2,32,512]{4,3,2,1,0:T(8,128)S(1)}, f32[2,2,2,32,512]{4,3,2,1,0:T(8,128)S(1)}, u32[]{:S(2)}, u32[]{:S(2)}) collective-permute-start(f32[2,2,2,32,512]{4,3,2,1,0:T(8,128)S(1)} %pad_maximum_fusion.mine), channel_id=1, source_target_pairs={{64,0},{65,1},{66,2},{67,3},{68,4},{69,5},{70,6},{71,7},{72,8},{73... | collective-permute-start | bytes 1572872 | tf_op jit(solution)/shard_map/ppermute | solution.py:56
  66.2 0.0 collective-permute-done.6.mate
  66.2 4.6 %collective-permute-start.8 = (f32[2,2,2,32,512]{4,3,2,1,0:T(8,128)S(1)}, f32[2,2,2,32,512]{4,3,2,1,0:T(8,128)S(1)}, u32[]{:S(2)}, u32[]{:S(2)}) collective-permute-start(f32[2,2,2,32,512]{4,3,2,1,0:T(8,128)S(1)} %collective-permute-done.6.mate), channel_id=1, source_target_pairs={{448,0},{449,1},{450,2},{451,3},{452,4},{453,5},{454,6},{455,7},{4... | collective-permute-start | bytes 1572872 | tf_op jit(solution)/shard_map/ppermute | solution.py:56
  70.8 1.9 %collective-permute-start.7 = (f32[2,2,2,32,512]{4,3,2,1,0:T(8,128)S(1)}, f32[2,2,2,32,512]{4,3,2,1,0:T(8,128)}, u32[]{:S(2)}, u32[]{:S(2)}) collective-permute-start(f32[2,2,2,32,512]{4,3,2,1,0:T(8,128)S(1)} %collective-permute-done.6.mate), channel_id=1, source_target_pairs={{64,0},{65,1},{66,2},{67,3},{68,4},{69,5},{70,6},{71,7},{72,8},{73... | collective-permute-start | bytes 1572872 | tf_op jit(solution)/shard_map/ppermute | solution.py:56
  72.7 0.0 collective-permute-done.4.next_one
  72.7 2.6 %collective-permute-start.5 = (f32[2,2,2,32,512]{4,3,2,1,0:T(8,128)S(1)}, f32[2,2,2,32,512]{4,3,2,1,0:T(8,128)}, u32[]{:S(2)}, u32[]{:S(2)}) collective-permute-start(f32[2,2,2,32,512]{4,3,2,1,0:T(8,128)S(1)} %collective-permute-done.4.next_one), channel_id=1, source_target_pairs={{0,16},{1,17},{2,18},{3,19},{4,20},{5,21},{6,22},{7,23},{8,24},{9,... | collective-permute-start | bytes 1572872 | tf_op jit(solution)/shard_map/ppermute | solution.py:56
  75.3 0.1 pad_add_fusion.1.info
  75.4 0.6 all-gather.3.cloned.1.call-done
  76.0 2.2 %copy-done = f32[64,32,512]{2,1,0:T(8,128)S(1)} copy-done((f32[64,32,512]{2,1,0:T(8,128)S(1)}, f32[64,32,512]{2,1,0:T(8,128)}, u32[]{:S(2)}) %copy-start) | copy-done | bytes 4194328
  78.2 5.4 %rows.1 = (bf16[3,2,512,256]{3,2,1,0:T(8,128)(2,1)S(1)}, bf16[3,2,512,256]{3,2,1,0:T(8,128)(2,1)S(1)}, f32[3,2,256,128]{3,2,1,0:T(8,128)S(1)}) custom-call(s32[20]{0:T(128)S(1)} %pad_add_fusion.1.info, f32[16,4,32,512]{3,2,1,0:T(8,128)S(1)} %bitcast.10, f32[16,4,32,512]{3,2,1,0:T(8,128)S(1)} %bitcast.11), custom_call_target="tpu_custom_call" | custom-call | flops 3200000000 | bytes 4194304 | tf_op jit(solution)/shard_map/rows/pallas_call | solution.py:169
  83.7 0.0 collective-permute-done.10.below
  83.7 0.0 collective-permute-done.9.above
  83.7 2.8 %first.1.begun = f32[512,1024]{1,0:T(8,128)S(1)} custom-call(s32[20]{0:T(128)S(1)} %pad_add_fusion.1.info, bf16[3,2,512,256]{3,2,1,0:T(8,128)(2,1)S(1)} %get-tuple-element.11.high, bf16[3,2,512,256]{3,2,1,0:T(8,128)(2,1)S(1)} %get-tuple-element.12.low, f32[3,2,256,128]{3,2,1,0:T(8,128)S(1)} %get-tuple-element.13.scale, ...), custom_call_target="tpu_custom_call" | custom-call | flops 2000000000 | bytes 4194304 | tf_op jit(solution)/shard_map/first/pallas_call | solution.py:169
  86.5 0.7 collective-permute-done.8.below_mate
  87.2 5.3 %collective-permute-done.7.above_mate = f32[2,2,2,32,512]{4,3,2,1,0:T(8,128)} collective-permute-done((f32[2,2,2,32,512]{4,3,2,1,0:T(8,128)S(1)}, f32[2,2,2,32,512]{4,3,2,1,0:T(8,128)}, u32[]{:S(2)}, u32[]{:S(2)}) %collective-permute-start.7) | collective-permute-done | bytes 524320 | tf_op jit(solution)/shard_map/ppermute | solution.py:56
  92.5 4.0 %last.1 = f32[512,1024]{1,0:T(8,128)} custom-call(s32[20]{0:T(128)S(1)} %pad_add_fusion.1.info, bf16[3,2,512,256]{3,2,1,0:T(8,128)(2,1)S(1)} %get-tuple-element.11.high, bf16[3,2,512,256]{3,2,1,0:T(8,128)(2,1)S(1)} %get-tuple-element.12.low, f32[3,2,256,128]{3,2,1,0:T(8,128)S(1)} %get-tuple-element.13.scale, ...), custom_call_target="tpu_custom_call" | custom-call | flops 1200000000 | bytes 4194304 | tf_op jit(solution)/shard_map/last/pallas_call | solution.py:169
  (9 shorter events, 0.1 us)
Async XLA Ops:
  6.5 59.6 %copy-start.2 = (s32[12]{0:T(128)S(1)}, s32[12]{0:T(128)}, u32[]{:S(2)}) copy-start(s32[12]{0:T(128)} %constant.58.clone) | copy-start | bytes 148
  6.5 69.5 %all-gather.3.cloned.1.call-start = ((), (), s32[]{:S(2)}) async-start(), calls=%async_computation | async-start | bytes 4456448 | tf_op jit(solution)/shard_map/all_gather | solution.py:153
  6.5 5.7 %collective-permute-start = (f32[2,32,384]{2,1,0:T(8,128)}, f32[2,32,384]{2,1,0:T(8,128)S(1)}, u32[]{:S(2)}, u32[]{:S(2)}) collective-permute-start(f32[2,32,384]{2,1,0:T(8,128)} %own_ref.1), channel_id=1, source_target_pairs={{16,0},{17,1},{18,2},{19,3},{20,4},{21,5},{22,6},{23,7},{24,8},{25... | collective-permute-start | bytes 294920 | tf_op jit(solution)/shard_map/ppermute | solution.py:56
  12.2 0.6 copy-start.1
  14.7 4.9 %collective-permute-start.1 = (f32[2,32,512]{2,1,0:T(8,128)}, f32[2,32,512]{2,1,0:T(8,128)S(1)}, u32[]{:S(2)}, u32[]{:S(2)}) collective-permute-start(f32[2,32,512]{2,1,0:T(8,128)} %get-tuple-element.14), channel_id=1, source_target_pairs={{0,1},{1,0},{2,3},{3,2},{4,5},{5,4},{6,7},{7,6},{8,9},{9,8},{10,11... | collective-permute-start | bytes 393224 | tf_op jit(solution)/shard_map/ppermute | solution.py:56
  20.6 20.6 %collective-permute-start.3 = (f32[2,2,32,512]{3,2,1,0:T(8,128)S(1)}, f32[2,2,32,512]{3,2,1,0:T(8,128)S(1)}, u32[]{:S(2)}, u32[]{:S(2)}) collective-permute-start(f32[2,2,32,512]{3,2,1,0:T(8,128)S(1)} %pad_maximum_fusion.1), channel_id=1, source_target_pairs={{0,256},{1,432},{2,320},{3,496},{4,384},{5,48},{6,448},{7,112},{8,... | collective-permute-start | bytes 786440 | tf_op jit(solution)/shard_map/ppermute | solution.py:56
  28.2 18.4 %collective-permute-start.2 = (f32[2,2,32,512]{3,2,1,0:T(8,128)S(1)}, f32[2,2,32,512]{3,2,1,0:T(8,128)S(1)}, u32[]{:S(2)}, u32[]{:S(2)}) collective-permute-start(f32[2,2,32,512]{3,2,1,0:T(8,128)S(1)} %pad_maximum_fusion.1), channel_id=1, source_target_pairs={{0,0},{1,176},{2,64},{3,240},{4,128},{5,304},{6,192},{7,368},{8,25... | collective-permute-start | bytes 786440 | tf_op jit(solution)/shard_map/ppermute | solution.py:56
  46.6 19.6 %collective-permute-start.6 = (f32[2,2,2,32,512]{4,3,2,1,0:T(8,128)S(1)}, f32[2,2,2,32,512]{4,3,2,1,0:T(8,128)S(1)}, u32[]{:S(2)}, u32[]{:S(2)}) collective-permute-start(f32[2,2,2,32,512]{4,3,2,1,0:T(8,128)S(1)} %pad_maximum_fusion.mine), channel_id=1, source_target_pairs={{0,16},{1,17},{2,18},{3,19},{4,20},{5,21},{6,22},{7,23},{8,24},{9,... | collective-permute-start | bytes 1572872 | tf_op jit(solution)/shard_map/ppermute | solution.py:56
  50.7 22.0 %collective-permute-start.4 = (f32[2,2,2,32,512]{4,3,2,1,0:T(8,128)S(1)}, f32[2,2,2,32,512]{4,3,2,1,0:T(8,128)S(1)}, u32[]{:S(2)}, u32[]{:S(2)}) collective-permute-start(f32[2,2,2,32,512]{4,3,2,1,0:T(8,128)S(1)} %pad_maximum_fusion.mine), channel_id=1, source_target_pairs={{0,48},{1,49},{2,50},{3,51},{4,52},{5,53},{6,54},{7,55},{8,56},{9,... | collective-permute-start | bytes 1572872 | tf_op jit(solution)/shard_map/ppermute | solution.py:56
  59.1 24.6 %collective-permute-start.10 = (f32[2,2,2,32,512]{4,3,2,1,0:T(8,128)S(1)}, f32[2,2,2,32,512]{4,3,2,1,0:T(8,128)S(1)}, u32[]{:S(2)}, u32[]{:S(2)}) collective-permute-start(f32[2,2,2,32,512]{4,3,2,1,0:T(8,128)S(1)} %pad_maximum_fusion.mine), channel_id=1, source_target_pairs={{448,0},{449,1},{450,2},{451,3},{452,4},{453,5},{454,6},{455,7},{4... | collective-permute-start | bytes 1572872 | tf_op jit(solution)/shard_map/ppermute | solution.py:56
  64.2 19.4 %collective-permute-start.9 = (f32[2,2,2,32,512]{4,3,2,1,0:T(8,128)S(1)}, f32[2,2,2,32,512]{4,3,2,1,0:T(8,128)S(1)}, u32[]{:S(2)}, u32[]{:S(2)}) collective-permute-start(f32[2,2,2,32,512]{4,3,2,1,0:T(8,128)S(1)} %pad_maximum_fusion.mine), channel_id=1, source_target_pairs={{64,0},{65,1},{66,2},{67,3},{68,4},{69,5},{70,6},{71,7},{72,8},{73... | collective-permute-start | bytes 1572872 | tf_op jit(solution)/shard_map/ppermute | solution.py:56
  66.2 21.0 %collective-permute-start.8 = (f32[2,2,2,32,512]{4,3,2,1,0:T(8,128)S(1)}, f32[2,2,2,32,512]{4,3,2,1,0:T(8,128)S(1)}, u32[]{:S(2)}, u32[]{:S(2)}) collective-permute-start(f32[2,2,2,32,512]{4,3,2,1,0:T(8,128)S(1)} %collective-permute-done.6.mate), channel_id=1, source_target_pairs={{448,0},{449,1},{450,2},{451,3},{452,4},{453,5},{454,6},{455,7},{4... | collective-permute-start | bytes 1572872 | tf_op jit(solution)/shard_map/ppermute | solution.py:56
  70.8 21.7 %collective-permute-start.7 = (f32[2,2,2,32,512]{4,3,2,1,0:T(8,128)S(1)}, f32[2,2,2,32,512]{4,3,2,1,0:T(8,128)}, u32[]{:S(2)}, u32[]{:S(2)}) collective-permute-start(f32[2,2,2,32,512]{4,3,2,1,0:T(8,128)S(1)} %collective-permute-done.6.mate), channel_id=1, source_target_pairs={{64,0},{65,1},{66,2},{67,3},{68,4},{69,5},{70,6},{71,7},{72,8},{73... | collective-permute-start | bytes 1572872 | tf_op jit(solution)/shard_map/ppermute | solution.py:56
  72.7 19.7 %collective-permute-start.5 = (f32[2,2,2,32,512]{4,3,2,1,0:T(8,128)S(1)}, f32[2,2,2,32,512]{4,3,2,1,0:T(8,128)}, u32[]{:S(2)}, u32[]{:S(2)}) collective-permute-start(f32[2,2,2,32,512]{4,3,2,1,0:T(8,128)S(1)} %collective-permute-done.4.next_one), channel_id=1, source_target_pairs={{0,16},{1,17},{2,18},{3,19},{4,20},{5,21},{6,22},{7,23},{8,24},{9,... | collective-permute-start | bytes 1572872 | tf_op jit(solution)/shard_map/ppermute | solution.py:56
  76.0 2.2 %copy-start = (f32[64,32,512]{2,1,0:T(8,128)S(1)}, f32[64,32,512]{2,1,0:T(8,128)}, u32[]{:S(2)}) copy-start(f32[64,32,512]{2,1,0:T(8,128)} %all-gather.3.cloned.1.call-done) | copy-start | bytes 12582916
Sparse Core Ops, SparseCore 0:
  14.9 61.1 all-gather.2

commit v5 on v4

--- a/solution.py
+++ b/solution.py
@@ -67,7 +67,7 @@
     return mul(a_high, b_high) + (mul(a_high, b_low) + mul(a_low, b_high))
 
 
-def place_kernel(row_ref, targets_ref, own_ref, next_ref, inverse_ref, placed_ref, both_ref):
+def place_kernel(row_ref, targets_ref, own_ref, next_ref, inverse_ref, placed_ref, pair_ref, both_ref):
     row = row_ref[0]
     blocks = 3
     count = targets_ref.shape[1]
@@ -83,6 +83,7 @@
                 total = jnp.where(hit, ref[panel, :, at : at + BLOCK], total)
             placed_ref[panel, :, slot * BLOCK : (slot + 1) * BLOCK] = total
             both_ref[panel, :, slot * BLOCK : (slot + 1) * BLOCK] = total
+            pair_ref[0, panel, :, slot * BLOCK : (slot + 1) * BLOCK] = total
         both_ref[2 + panel] = inverse_ref[panel]
 
 
@@ -129,8 +130,9 @@
 
 def last_kernel(info, high, low, scale, across, above_mate, below_mate, begun, out):
     parts = (0, 3, across), (1, 1, above_mate), (2, 1, below_mate)
-    out[...] = begun[...]
-    out[:, pl.ds(pl.multiple_of(info[1] * 512, 512), 512)] += product(info, (high, low, scale), parts)
+    at, other = pl.multiple_of(info[0] * 512, 512), pl.multiple_of(info[1] * 512, 512)
+    out[:, pl.ds(at, 512)] = begun[:, pl.ds(at, 512)]
+    out[:, pl.ds(other, 512)] = begun[:, pl.ds(other, 512)] + product(info, (high, low, scale), parts)
 
 
 VMEM = pl.BlockSpec(memory_space=pltpu.VMEM)
@@ -142,17 +144,17 @@
     y, x, z, core = row // NX, row % NX, col // NC, col % NC
 
     following = send(panel, to_previous_row())
-    placed, both = pl.pallas_call(
+    placed, pieces, both = pl.pallas_call(
         place_kernel,
-        out_shape=(jax.ShapeDtypeStruct((2, 32, 512), F32), jax.ShapeDtypeStruct((4, 32, 512), F32)),
+        out_shape=tuple(jax.ShapeDtypeStruct(shape, F32) for shape in ((2, 32, 512), (2, 2, 32, 512), (4, 32, 512))),
         in_specs=[SMEM, SMEM, VMEM, VMEM, VMEM],
-        out_specs=(VMEM, VMEM),
+        out_specs=(VMEM, VMEM, VMEM),
         name="place",
     )(row.reshape(1), targets, panel, following, inverse)
 
     gathered = lax.all_gather(both, "pcol")
 
-    pieces = jnp.stack([placed, send(placed, to_sibling())])
+    pieces = lax.dynamic_update_slice(pieces, send(placed, to_sibling())[None], (1, 0, 0, 0))
     mine = jnp.stack([send(pieces, transposing(0)), send(pieces, transposing(1))])
     to_mate, to_next = swapped(lambda x: x ^ 1), swapped(lambda x: 3 - x)
     mate, next_one = send(mine, to_mate), send(mine, to_next)

time: 104 us -> 104 us (level)
    unnamed x6 -> x4, local copies, waits for them, and re-layouts: 2.83 us -> 2.83 us
  transfers between devices with their start and end apart: 12 -> 12, of which waited for: 6 -> 5; matrix products, arithmetic and copies ran while one was open for 1% -> 1% of each run, Pallas kernels for 8% -> 8%
where the time goes in v5:
time: 104 us; the launch traced here: 103 us
  starting transfers between devices  54.9 us (53%)
  waiting for transfers between devices  16.3 us (16%)
  Pallas kernels  14.1 us (14%)
  between operations  13.6 us (13%)
  local copies, waits for them, and re-layouts  3.49 us (3%)
    ppermute x11, starting transfers between devices, send(): return lax.ppermute(value, AXES, pairs)  54.9 us
    ppermute x11, waiting for transfers between devices, send(): return lax.ppermute(value, AXES, pairs)  16.3 us
    pallas_call x3, Pallas kernels, kernel(): pl.pallas_call(run, out_shape=out_shape, compiler_params=pltpu.CompilerPa...  12.1 us
    unnamed x4, local copies, waits for them, and re-layouts  2.83 us
  transfers between devices with their start and end apart: 12, of which 5 were waited for; matrix products, arithmetic and copies ran while one was open for 1% of the time, Pallas kernels for 8%

profile of v5, /device:TPU:29, one launch (start us, length us, event | category | flops | bytes accessed | tf_op | source)
XLA Modules:
  0.0 103.2 jit_solution(4187688115099868641)
XLA Ops:
  6.5 2.2 %collective-permute-start = (f32[2,32,384]{2,1,0:T(8,128)}, f32[2,32,384]{2,1,0:T(8,128)S(1)}, u32[]{:S(2)}, u32[]{:S(2)}) collective-permute-start(f32[2,32,384]{2,1,0:T(8,128)} %own_ref.1), channel_id=1, source_target_pairs={{16,0},{17,1},{18,2},{19,3},{20,4},{21,5},{22,6},{23,7},{24,8},{25... | collective-permute-start | bytes 294920 | tf_op jit(solution)/shard_map/ppermute | solution.py:56
  8.7 3.4 %collective-permute-done.next_ref = f32[2,32,384]{2,1,0:T(8,128)S(1)} collective-permute-done((f32[2,32,384]{2,1,0:T(8,128)}, f32[2,32,384]{2,1,0:T(8,128)S(1)}, u32[]{:S(2)}, u32[]{:S(2)}) %collective-permute-start) | collective-permute-done | bytes 98336 | tf_op jit(solution)/shard_map/ppermute | solution.py:56
  12.1 0.6 copy-done.1
  12.7 2.0 %place.1 = (f32[2,32,512]{2,1,0:T(8,128)}, f32[2,2,32,512]{3,2,1,0:T(8,128)}, f32[4,32,512]{2,1,0:T(8,128)}) custom-call(s32[1]{0:T(128)} %bitcast.4.row_ref, s32[2,96]{1,0:T(2,128)} %targets_ref.1, f32[2,32,384]{2,1,0:T(8,128)} %own_ref.1, f32[2,32,384]{2,1,0:T(8,128)} %copy-done.1, f32[2,32,512]{2,1,0:T(8,128)} %inverse_ref.1), custom_call_target="tpu_custom_call" | custom-call | tf_op jit(solution)/shard_map/place/pallas_call | solution.py:147
  14.7 0.0 all-gather.3.cloned.1.call-update
  14.7 3.7 %collective-permute-start.1 = (f32[2,32,512]{2,1,0:T(8,128)}, f32[2,32,512]{2,1,0:T(8,128)S(1)}, u32[]{:S(2)}, u32[]{:S(2)}) collective-permute-start(f32[2,32,512]{2,1,0:T(8,128)} %get-tuple-element.16), channel_id=1, source_target_pairs={{0,1},{1,0},{2,3},{3,2},{4,5},{5,4},{6,7},{7,6},{8,9},{9,8},{10,11... | collective-permute-start | bytes 393224 | tf_op jit(solution)/shard_map/ppermute | solution.py:56
  18.5 1.2 %collective-permute-done.1 = f32[2,32,512]{2,1,0:T(8,128)S(1)} collective-permute-done((f32[2,32,512]{2,1,0:T(8,128)}, f32[2,32,512]{2,1,0:T(8,128)S(1)}, u32[]{:S(2)}, u32[]{:S(2)}) %collective-permute-start.1) | collective-permute-done | bytes 131104 | tf_op jit(solution)/shard_map/ppermute | solution.py:56
  19.6 0.7 bitcast_dynamic-update-slice_fusion
  20.3 7.6 %collective-permute-start.3 = (f32[2,2,32,512]{3,2,1,0:T(8,128)}, f32[2,2,32,512]{3,2,1,0:T(8,128)S(1)}, u32[]{:S(2)}, u32[]{:S(2)}) collective-permute-start(f32[2,2,32,512]{3,2,1,0:T(8,128)} %bitcast_dynamic-update-slice_fusion), channel_id=1, source_target_pairs={{0,256},{1,432},{2,320},{3,496},{4,384},{5,48},{6,448},{7,112},{8,... | collective-permute-start | bytes 786440 | tf_op jit(solution)/shard_map/ppermute | solution.py:56
  27.9 12.9 %collective-permute-start.2 = (f32[2,2,32,512]{3,2,1,0:T(8,128)}, f32[2,2,32,512]{3,2,1,0:T(8,128)S(1)}, u32[]{:S(2)}, u32[]{:S(2)}) collective-permute-start(f32[2,2,32,512]{3,2,1,0:T(8,128)} %bitcast_dynamic-update-slice_fusion), channel_id=1, source_target_pairs={{0,0},{1,176},{2,64},{3,240},{4,128},{5,304},{6,192},{7,368},{8,25... | collective-permute-start | bytes 786440 | tf_op jit(solution)/shard_map/ppermute | solution.py:56
  40.8 0.0 collective-permute-done.3
  40.9 5.6 %collective-permute-done.2 = f32[2,2,32,512]{3,2,1,0:T(8,128)S(1)} collective-permute-done((f32[2,2,32,512]{3,2,1,0:T(8,128)}, f32[2,2,32,512]{3,2,1,0:T(8,128)S(1)}, u32[]{:S(2)}, u32[]{:S(2)}) %collective-permute-start.2) | collective-permute-done | bytes 262176 | tf_op jit(solution)/shard_map/ppermute | solution.py:56
  46.5 4.1 %collective-permute-start.6 = (f32[2,2,2,32,512]{4,3,2,1,0:T(8,128)S(1)}, f32[2,2,2,32,512]{4,3,2,1,0:T(8,128)S(1)}, u32[]{:S(2)}, u32[]{:S(2)}) collective-permute-start(f32[2,2,2,32,512]{4,3,2,1,0:T(8,128)S(1)} %pad_maximum_fusion.mine), channel_id=1, source_target_pairs={{0,16},{1,17},{2,18},{3,19},{4,20},{5,21},{6,22},{7,23},{8,24},{9,... | collective-permute-start | bytes 1572872 | tf_op jit(solution)/shard_map/ppermute | solution.py:56
  50.7 7.3 %collective-permute-start.4 = (f32[2,2,2,32,512]{4,3,2,1,0:T(8,128)S(1)}, f32[2,2,2,32,512]{4,3,2,1,0:T(8,128)S(1)}, u32[]{:S(2)}, u32[]{:S(2)}) collective-permute-start(f32[2,2,2,32,512]{4,3,2,1,0:T(8,128)S(1)} %pad_maximum_fusion.mine), channel_id=1, source_target_pairs={{0,48},{1,49},{2,50},{3,51},{4,52},{5,53},{6,54},{7,55},{8,56},{9,... | collective-permute-start | bytes 1572872 | tf_op jit(solution)/shard_map/ppermute | solution.py:56
  57.9 0.1 shift-right-arithmetic_and_fusion
  58.0 6.2 %collective-permute-start.10 = (f32[2,2,2,32,512]{4,3,2,1,0:T(8,128)S(1)}, f32[2,2,2,32,512]{4,3,2,1,0:T(8,128)S(1)}, u32[]{:S(2)}, u32[]{:S(2)}) collective-permute-start(f32[2,2,2,32,512]{4,3,2,1,0:T(8,128)S(1)} %pad_maximum_fusion.mine), channel_id=1, source_target_pairs={{448,0},{449,1},{450,2},{451,3},{452,4},{453,5},{454,6},{455,7},{4... | collective-permute-start | bytes 1572872 | tf_op jit(solution)/shard_map/ppermute | solution.py:56
  64.2 1.9 %collective-permute-start.9 = (f32[2,2,2,32,512]{4,3,2,1,0:T(8,128)S(1)}, f32[2,2,2,32,512]{4,3,2,1,0:T(8,128)S(1)}, u32[]{:S(2)}, u32[]{:S(2)}) collective-permute-start(f32[2,2,2,32,512]{4,3,2,1,0:T(8,128)S(1)} %pad_maximum_fusion.mine), channel_id=1, source_target_pairs={{64,0},{65,1},{66,2},{67,3},{68,4},{69,5},{70,6},{71,7},{72,8},{73... | collective-permute-start | bytes 1572872 | tf_op jit(solution)/shard_map/ppermute | solution.py:56
  66.1 0.7 add_and_fusion
  66.8 0.0 collective-permute-done.6.mate
  66.8 4.6 %collective-permute-start.8 = (f32[2,2,2,32,512]{4,3,2,1,0:T(8,128)S(1)}, f32[2,2,2,32,512]{4,3,2,1,0:T(8,128)S(1)}, u32[]{:S(2)}, u32[]{:S(2)}) collective-permute-start(f32[2,2,2,32,512]{4,3,2,1,0:T(8,128)S(1)} %collective-permute-done.6.mate), channel_id=1, source_target_pairs={{448,0},{449,1},{450,2},{451,3},{452,4},{453,5},{454,6},{455,7},{4... | collective-permute-start | bytes 1572872 | tf_op jit(solution)/shard_map/ppermute | solution.py:56
  71.4 1.9 %collective-permute-start.7 = (f32[2,2,2,32,512]{4,3,2,1,0:T(8,128)S(1)}, f32[2,2,2,32,512]{4,3,2,1,0:T(8,128)}, u32[]{:S(2)}, u32[]{:S(2)}) collective-permute-start(f32[2,2,2,32,512]{4,3,2,1,0:T(8,128)S(1)} %collective-permute-done.6.mate), channel_id=1, source_target_pairs={{64,0},{65,1},{66,2},{67,3},{68,4},{69,5},{70,6},{71,7},{72,8},{73... | collective-permute-start | bytes 1572872 | tf_op jit(solution)/shard_map/ppermute | solution.py:56
  73.3 0.0 collective-permute-done.4.next_one
  73.3 2.6 %collective-permute-start.5 = (f32[2,2,2,32,512]{4,3,2,1,0:T(8,128)S(1)}, f32[2,2,2,32,512]{4,3,2,1,0:T(8,128)}, u32[]{:S(2)}, u32[]{:S(2)}) collective-permute-start(f32[2,2,2,32,512]{4,3,2,1,0:T(8,128)S(1)} %collective-permute-done.4.next_one), channel_id=1, source_target_pairs={{0,16},{1,17},{2,18},{3,19},{4,20},{5,21},{6,22},{7,23},{8,24},{9,... | collective-permute-start | bytes 1572872 | tf_op jit(solution)/shard_map/ppermute | solution.py:56
  75.9 0.1 pad_add_fusion.1.info
  76.0 2.2 %copy-done = f32[64,32,512]{2,1,0:T(8,128)S(1)} copy-done((f32[64,32,512]{2,1,0:T(8,128)S(1)}, f32[64,32,512]{2,1,0:T(8,128)}, u32[]{:S(2)}) %copy-start) | copy-done | bytes 4194328
  78.2 5.4 %rows.1 = (bf16[3,2,512,256]{3,2,1,0:T(8,128)(2,1)S(1)}, bf16[3,2,512,256]{3,2,1,0:T(8,128)(2,1)S(1)}, f32[3,2,256,128]{3,2,1,0:T(8,128)S(1)}) custom-call(s32[20]{0:T(128)S(1)} %pad_add_fusion.1.info, f32[16,4,32,512]{3,2,1,0:T(8,128)S(1)} %bitcast.10, f32[16,4,32,512]{3,2,1,0:T(8,128)S(1)} %bitcast.11), custom_call_target="tpu_custom_call" | custom-call | flops 3200000000 | bytes 4194304 | tf_op jit(solution)/shard_map/rows/pallas_call | solution.py:171
  83.6 0.0 collective-permute-done.10.below
  83.6 2.8 %first.1.begun = f32[512,1024]{1,0:T(8,128)S(1)} custom-call(s32[20]{0:T(128)S(1)} %pad_add_fusion.1.info, bf16[3,2,512,256]{3,2,1,0:T(8,128)(2,1)S(1)} %get-tuple-element.12.high, bf16[3,2,512,256]{3,2,1,0:T(8,128)(2,1)S(1)} %get-tuple-element.13.low, f32[3,2,256,128]{3,2,1,0:T(8,128)S(1)} %get-tuple-element.14.scale, ...), custom_call_target="tpu_custom_call" | custom-call | flops 2000000000 | bytes 4194304 | tf_op jit(solution)/shard_map/first/pallas_call | solution.py:171
  86.4 0.7 collective-permute-done.8.below_mate
  87.1 5.4 %collective-permute-done.7.above_mate = f32[2,2,2,32,512]{4,3,2,1,0:T(8,128)} collective-permute-done((f32[2,2,2,32,512]{4,3,2,1,0:T(8,128)S(1)}, f32[2,2,2,32,512]{4,3,2,1,0:T(8,128)}, u32[]{:S(2)}, u32[]{:S(2)}) %collective-permute-start.7) | collective-permute-done | bytes 524320 | tf_op jit(solution)/shard_map/ppermute | solution.py:56
  92.5 0.0 collective-permute-done.5.across
  92.5 3.9 %last.1 = f32[512,1024]{1,0:T(8,128)} custom-call(s32[20]{0:T(128)S(1)} %pad_add_fusion.1.info, bf16[3,2,512,256]{3,2,1,0:T(8,128)(2,1)S(1)} %get-tuple-element.12.high, bf16[3,2,512,256]{3,2,1,0:T(8,128)(2,1)S(1)} %get-tuple-element.13.low, f32[3,2,256,128]{3,2,1,0:T(8,128)S(1)} %get-tuple-element.14.scale, ...), custom_call_target="tpu_custom_call" | custom-call | flops 1200000000 | bytes 4194304 | tf_op jit(solution)/shard_map/last/pallas_call | solution.py:171
  (7 shorter events, 0.0 us)
Async XLA Ops:
  6.5 69.4 %all-gather.3.cloned.1.call-start = ((), (), s32[]{:S(2)}) async-start(), calls=%async_computation | async-start | bytes 4456448 | tf_op jit(solution)/shard_map/all_gather | solution.py:155
  6.5 5.6 %collective-permute-start = (f32[2,32,384]{2,1,0:T(8,128)}, f32[2,32,384]{2,1,0:T(8,128)S(1)}, u32[]{:S(2)}, u32[]{:S(2)}) collective-permute-start(f32[2,32,384]{2,1,0:T(8,128)} %own_ref.1), channel_id=1, source_target_pairs={{16,0},{17,1},{18,2},{19,3},{20,4},{21,5},{22,6},{23,7},{24,8},{25... | collective-permute-start | bytes 294920 | tf_op jit(solution)/shard_map/ppermute | solution.py:56
  12.1 0.6 copy-start.1
  14.7 4.9 %collective-permute-start.1 = (f32[2,32,512]{2,1,0:T(8,128)}, f32[2,32,512]{2,1,0:T(8,128)S(1)}, u32[]{:S(2)}, u32[]{:S(2)}) collective-permute-start(f32[2,32,512]{2,1,0:T(8,128)} %get-tuple-element.16), channel_id=1, source_target_pairs={{0,1},{1,0},{2,3},{3,2},{4,5},{5,4},{6,7},{7,6},{8,9},{9,8},{10,11... | collective-permute-start | bytes 393224 | tf_op jit(solution)/shard_map/ppermute | solution.py:56
  20.3 20.5 %collective-permute-start.3 = (f32[2,2,32,512]{3,2,1,0:T(8,128)}, f32[2,2,32,512]{3,2,1,0:T(8,128)S(1)}, u32[]{:S(2)}, u32[]{:S(2)}) collective-permute-start(f32[2,2,32,512]{3,2,1,0:T(8,128)} %bitcast_dynamic-update-slice_fusion), channel_id=1, source_target_pairs={{0,256},{1,432},{2,320},{3,496},{4,384},{5,48},{6,448},{7,112},{8,... | collective-permute-start | bytes 786440 | tf_op jit(solution)/shard_map/ppermute | solution.py:56
  27.9 18.6 %collective-permute-start.2 = (f32[2,2,32,512]{3,2,1,0:T(8,128)}, f32[2,2,32,512]{3,2,1,0:T(8,128)S(1)}, u32[]{:S(2)}, u32[]{:S(2)}) collective-permute-start(f32[2,2,32,512]{3,2,1,0:T(8,128)} %bitcast_dynamic-update-slice_fusion), channel_id=1, source_target_pairs={{0,0},{1,176},{2,64},{3,240},{4,128},{5,304},{6,192},{7,368},{8,25... | collective-permute-start | bytes 786440 | tf_op jit(solution)/shard_map/ppermute | solution.py:56
  46.5 20.2 %collective-permute-start.6 = (f32[2,2,2,32,512]{4,3,2,1,0:T(8,128)S(1)}, f32[2,2,2,32,512]{4,3,2,1,0:T(8,128)S(1)}, u32[]{:S(2)}, u32[]{:S(2)}) collective-permute-start(f32[2,2,2,32,512]{4,3,2,1,0:T(8,128)S(1)} %pad_maximum_fusion.mine), channel_id=1, source_target_pairs={{0,16},{1,17},{2,18},{3,19},{4,20},{5,21},{6,22},{7,23},{8,24},{9,... | collective-permute-start | bytes 1572872 | tf_op jit(solution)/shard_map/ppermute | solution.py:56
  50.7 22.6 %collective-permute-start.4 = (f32[2,2,2,32,512]{4,3,2,1,0:T(8,128)S(1)}, f32[2,2,2,32,512]{4,3,2,1,0:T(8,128)S(1)}, u32[]{:S(2)}, u32[]{:S(2)}) collective-permute-start(f32[2,2,2,32,512]{4,3,2,1,0:T(8,128)S(1)} %pad_maximum_fusion.mine), channel_id=1, source_target_pairs={{0,48},{1,49},{2,50},{3,51},{4,52},{5,53},{6,54},{7,55},{8,56},{9,... | collective-permute-start | bytes 1572872 | tf_op jit(solution)/shard_map/ppermute | solution.py:56
  58.0 25.6 %collective-permute-start.10 = (f32[2,2,2,32,512]{4,3,2,1,0:T(8,128)S(1)}, f32[2,2,2,32,512]{4,3,2,1,0:T(8,128)S(1)}, u32[]{:S(2)}, u32[]{:S(2)}) collective-permute-start(f32[2,2,2,32,512]{4,3,2,1,0:T(8,128)S(1)} %pad_maximum_fusion.mine), channel_id=1, source_target_pairs={{448,0},{449,1},{450,2},{451,3},{452,4},{453,5},{454,6},{455,7},{4... | collective-permute-start | bytes 1572872 | tf_op jit(solution)/shard_map/ppermute | solution.py:56
  64.2 19.4 %collective-permute-start.9 = (f32[2,2,2,32,512]{4,3,2,1,0:T(8,128)S(1)}, f32[2,2,2,32,512]{4,3,2,1,0:T(8,128)S(1)}, u32[]{:S(2)}, u32[]{:S(2)}) collective-permute-start(f32[2,2,2,32,512]{4,3,2,1,0:T(8,128)S(1)} %pad_maximum_fusion.mine), channel_id=1, source_target_pairs={{64,0},{65,1},{66,2},{67,3},{68,4},{69,5},{70,6},{71,7},{72,8},{73... | collective-permute-start | bytes 1572872 | tf_op jit(solution)/shard_map/ppermute | solution.py:56
  66.8 20.3 %collective-permute-start.8 = (f32[2,2,2,32,512]{4,3,2,1,0:T(8,128)S(1)}, f32[2,2,2,32,512]{4,3,2,1,0:T(8,128)S(1)}, u32[]{:S(2)}, u32[]{:S(2)}) collective-permute-start(f32[2,2,2,32,512]{4,3,2,1,0:T(8,128)S(1)} %collective-permute-done.6.mate), channel_id=1, source_target_pairs={{448,0},{449,1},{450,2},{451,3},{452,4},{453,5},{454,6},{455,7},{4... | collective-permute-start | bytes 1572872 | tf_op jit(solution)/shard_map/ppermute | solution.py:56
  71.4 21.1 %collective-permute-start.7 = (f32[2,2,2,32,512]{4,3,2,1,0:T(8,128)S(1)}, f32[2,2,2,32,512]{4,3,2,1,0:T(8,128)}, u32[]{:S(2)}, u32[]{:S(2)}) collective-permute-start(f32[2,2,2,32,512]{4,3,2,1,0:T(8,128)S(1)} %collective-permute-done.6.mate), channel_id=1, source_target_pairs={{64,0},{65,1},{66,2},{67,3},{68,4},{69,5},{70,6},{71,7},{72,8},{73... | collective-permute-start | bytes 1572872 | tf_op jit(solution)/shard_map/ppermute | solution.py:56
  73.3 19.2 %collective-permute-start.5 = (f32[2,2,2,32,512]{4,3,2,1,0:T(8,128)S(1)}, f32[2,2,2,32,512]{4,3,2,1,0:T(8,128)}, u32[]{:S(2)}, u32[]{:S(2)}) collective-permute-start(f32[2,2,2,32,512]{4,3,2,1,0:T(8,128)S(1)} %collective-permute-done.4.next_one), channel_id=1, source_target_pairs={{0,16},{1,17},{2,18},{3,19},{4,20},{5,21},{6,22},{7,23},{8,24},{9,... | collective-permute-start | bytes 1572872 | tf_op jit(solution)/shard_map/ppermute | solution.py:56
  76.0 2.2 %copy-start = (f32[64,32,512]{2,1,0:T(8,128)S(1)}, f32[64,32,512]{2,1,0:T(8,128)}, u32[]{:S(2)}) copy-start(f32[64,32,512]{2,1,0:T(8,128)} %all-gather.3.cloned.1.call-done) | copy-start | bytes 12582916
Sparse Core Ops, SparseCore 0:
  14.8 61.0 all-gather.2

commit v6 on v5

--- a/solution.py
+++ b/solution.py
@@ -110,12 +110,13 @@
                 high[chunk, group], low[chunk, group] = split(jnp.concatenate(pieces).T)
 
 
-def product(info, weights, parts):
+def product(info, weights, parts, columns=slice(0, 512)):
     high, low, scale = weights
     total = None
     for chunk, at, ref in parts:
         group = info[4 + at]
-        value = ref[...].reshape(256, 512) * jnp.concatenate([scale[chunk, group]] * 4, axis=1)
+        wide = columns.stop - columns.start
+        value = ref[..., columns].reshape(256, wide) * jnp.concatenate([scale[chunk, group]] * (wide // BLOCK), axis=1)
         one = dot3((high[chunk, group], low[chunk, group]), split(value), ((1,), (0,)))
         total = one if total is None else total + one
     return total
@@ -128,11 +129,19 @@
     out[:, pl.ds(other, 512)] = product(info, weights, ((0, 1, mate),))
 
 
-def last_kernel(info, high, low, scale, across, above_mate, below_mate, begun, out):
+def last_kernel(info, high, low, scale, across, above_mate, below_mate, begun, out, held, sems):
     parts = (0, 3, across), (1, 1, above_mate), (2, 1, below_mate)
     at, other = pl.multiple_of(info[0] * 512, 512), pl.multiple_of(info[1] * 512, 512)
-    out[:, pl.ds(at, 512)] = begun[:, pl.ds(at, 512)]
-    out[:, pl.ds(other, 512)] = begun[:, pl.ds(other, 512)] + product(info, (high, low, scale), parts)
+    finished = pl.ds(at, 512)
+    copies = [pltpu.make_async_copy(begun.at[:, finished], out.at[:, finished], sems.at[2])]
+    copies[0].start()
+    for piece in range(2):
+        columns, into = slice(piece * 256, piece * 256 + 256), pl.ds(other + piece * 256, 256)
+        held[piece] = begun[:, into] + product(info, (high, low, scale), parts, columns)
+        copies.append(pltpu.make_async_copy(held.at[piece], out.at[:, into], sems.at[piece]))
+        copies[-1].start()
+    for copy in copies:
+        copy.wait()
 
 
 VMEM = pl.BlockSpec(memory_space=pltpu.VMEM)
@@ -211,7 +220,8 @@
         1.2,
         "last",
         in_specs=[SMEM] + [VMEM] * 7,
-        out_specs=VMEM,
+        out_specs=pl.BlockSpec(memory_space=pl.ANY),
+        scratch_shapes=[pltpu.VMEM((2, 512, 256), F32), pltpu.SemaphoreType.DMA((3,))],
     )
 
 

time: 104 us -> 103 us (level)
  no operation moved by 1% of the time
where the time goes in v6:
time: 103 us
  starting transfers between devices  54.9 us (53%)
  waiting for transfers between devices  16.3 us (16%)
  Pallas kernels  13.8 us (13%)
  between operations  13.6 us (13%)
  local copies, waits for them, and re-layouts  3.49 us (3%)
    ppermute x11, starting transfers between devices, send(): return lax.ppermute(value, AXES, pairs)  54.9 us
    ppermute x11, waiting for transfers between devices, send(): return lax.ppermute(value, AXES, pairs)  16.3 us
    pallas_call x3, Pallas kernels, kernel(): pl.pallas_call(run, out_shape=out_shape, compiler_params=pltpu.CompilerPa...  11.9 us
    unnamed x4, local copies, waits for them, and re-layouts  2.83 us
  transfers between devices with their start and end apart: 12, of which 5 were waited for; matrix products, arithmetic and copies ran while one was open for 1% of the time, Pallas kernels for 8%

profile of v6, /device:TPU:29, one launch (start us, length us, event | category | flops | bytes accessed | tf_op | source)
XLA Modules:
  0.0 103.0 jit_solution(278322072825680661)
XLA Ops:
  6.5 2.2 %collective-permute-start = (f32[2,32,384]{2,1,0:T(8,128)}, f32[2,32,384]{2,1,0:T(8,128)S(1)}, u32[]{:S(2)}, u32[]{:S(2)}) collective-permute-start(f32[2,32,384]{2,1,0:T(8,128)} %own_ref.1), channel_id=1, source_target_pairs={{16,0},{17,1},{18,2},{19,3},{20,4},{21,5},{22,6},{23,7},{24,8},{25... | collective-permute-start | bytes 294920 | tf_op jit(solution)/shard_map/ppermute | solution.py:56
  8.7 3.4 %collective-permute-done.next_ref = f32[2,32,384]{2,1,0:T(8,128)S(1)} collective-permute-done((f32[2,32,384]{2,1,0:T(8,128)}, f32[2,32,384]{2,1,0:T(8,128)S(1)}, u32[]{:S(2)}, u32[]{:S(2)}) %collective-permute-start) | collective-permute-done | bytes 98336 | tf_op jit(solution)/shard_map/ppermute | solution.py:56
  12.1 0.6 copy-done.1
  12.7 2.0 %place.1 = (f32[2,32,512]{2,1,0:T(8,128)}, f32[2,2,32,512]{3,2,1,0:T(8,128)}, f32[4,32,512]{2,1,0:T(8,128)}) custom-call(s32[1]{0:T(128)} %bitcast.4.row_ref, s32[2,96]{1,0:T(2,128)} %targets_ref.1, f32[2,32,384]{2,1,0:T(8,128)} %own_ref.1, f32[2,32,384]{2,1,0:T(8,128)} %copy-done.1, f32[2,32,512]{2,1,0:T(8,128)} %inverse_ref.1), custom_call_target="tpu_custom_call" | custom-call | tf_op jit(solution)/shard_map/place/pallas_call | solution.py:156
  14.7 0.0 all-gather.3.cloned.1.call-update
  14.7 3.7 %collective-permute-start.1 = (f32[2,32,512]{2,1,0:T(8,128)}, f32[2,32,512]{2,1,0:T(8,128)S(1)}, u32[]{:S(2)}, u32[]{:S(2)}) collective-permute-start(f32[2,32,512]{2,1,0:T(8,128)} %get-tuple-element.16), channel_id=1, source_target_pairs={{0,1},{1,0},{2,3},{3,2},{4,5},{5,4},{6,7},{7,6},{8,9},{9,8},{10,11... | collective-permute-start | bytes 393224 | tf_op jit(solution)/shard_map/ppermute | solution.py:56
  18.5 1.2 %collective-permute-done.1 = f32[2,32,512]{2,1,0:T(8,128)S(1)} collective-permute-done((f32[2,32,512]{2,1,0:T(8,128)}, f32[2,32,512]{2,1,0:T(8,128)S(1)}, u32[]{:S(2)}, u32[]{:S(2)}) %collective-permute-start.1) | collective-permute-done | bytes 131104 | tf_op jit(solution)/shard_map/ppermute | solution.py:56
  19.6 0.7 bitcast_dynamic-update-slice_fusion
  20.3 7.6 %collective-permute-start.3 = (f32[2,2,32,512]{3,2,1,0:T(8,128)}, f32[2,2,32,512]{3,2,1,0:T(8,128)S(1)}, u32[]{:S(2)}, u32[]{:S(2)}) collective-permute-start(f32[2,2,32,512]{3,2,1,0:T(8,128)} %bitcast_dynamic-update-slice_fusion), channel_id=1, source_target_pairs={{0,256},{1,432},{2,320},{3,496},{4,384},{5,48},{6,448},{7,112},{8,... | collective-permute-start | bytes 786440 | tf_op jit(solution)/shard_map/ppermute | solution.py:56
  27.9 12.9 %collective-permute-start.2 = (f32[2,2,32,512]{3,2,1,0:T(8,128)}, f32[2,2,32,512]{3,2,1,0:T(8,128)S(1)}, u32[]{:S(2)}, u32[]{:S(2)}) collective-permute-start(f32[2,2,32,512]{3,2,1,0:T(8,128)} %bitcast_dynamic-update-slice_fusion), channel_id=1, source_target_pairs={{0,0},{1,176},{2,64},{3,240},{4,128},{5,304},{6,192},{7,368},{8,25... | collective-permute-start | bytes 786440 | tf_op jit(solution)/shard_map/ppermute | solution.py:56
  40.8 0.0 collective-permute-done.3
  40.9 5.6 %collective-permute-done.2 = f32[2,2,32,512]{3,2,1,0:T(8,128)S(1)} collective-permute-done((f32[2,2,32,512]{3,2,1,0:T(8,128)}, f32[2,2,32,512]{3,2,1,0:T(8,128)S(1)}, u32[]{:S(2)}, u32[]{:S(2)}) %collective-permute-start.2) | collective-permute-done | bytes 262176 | tf_op jit(solution)/shard_map/ppermute | solution.py:56
  46.5 4.1 %collective-permute-start.6 = (f32[2,2,2,32,512]{4,3,2,1,0:T(8,128)S(1)}, f32[2,2,2,32,512]{4,3,2,1,0:T(8,128)S(1)}, u32[]{:S(2)}, u32[]{:S(2)}) collective-permute-start(f32[2,2,2,32,512]{4,3,2,1,0:T(8,128)S(1)} %pad_maximum_fusion.mine), channel_id=1, source_target_pairs={{0,16},{1,17},{2,18},{3,19},{4,20},{5,21},{6,22},{7,23},{8,24},{9,... | collective-permute-start | bytes 1572872 | tf_op jit(solution)/shard_map/ppermute | solution.py:56
  50.7 7.3 %collective-permute-start.4 = (f32[2,2,2,32,512]{4,3,2,1,0:T(8,128)S(1)}, f32[2,2,2,32,512]{4,3,2,1,0:T(8,128)S(1)}, u32[]{:S(2)}, u32[]{:S(2)}) collective-permute-start(f32[2,2,2,32,512]{4,3,2,1,0:T(8,128)S(1)} %pad_maximum_fusion.mine), channel_id=1, source_target_pairs={{0,48},{1,49},{2,50},{3,51},{4,52},{5,53},{6,54},{7,55},{8,56},{9,... | collective-permute-start | bytes 1572872 | tf_op jit(solution)/shard_map/ppermute | solution.py:56
  57.9 0.1 shift-right-arithmetic_and_fusion
  58.0 6.2 %collective-permute-start.10 = (f32[2,2,2,32,512]{4,3,2,1,0:T(8,128)S(1)}, f32[2,2,2,32,512]{4,3,2,1,0:T(8,128)S(1)}, u32[]{:S(2)}, u32[]{:S(2)}) collective-permute-start(f32[2,2,2,32,512]{4,3,2,1,0:T(8,128)S(1)} %pad_maximum_fusion.mine), channel_id=1, source_target_pairs={{448,0},{449,1},{450,2},{451,3},{452,4},{453,5},{454,6},{455,7},{4... | collective-permute-start | bytes 1572872 | tf_op jit(solution)/shard_map/ppermute | solution.py:56
  64.2 1.9 %collective-permute-start.9 = (f32[2,2,2,32,512]{4,3,2,1,0:T(8,128)S(1)}, f32[2,2,2,32,512]{4,3,2,1,0:T(8,128)S(1)}, u32[]{:S(2)}, u32[]{:S(2)}) collective-permute-start(f32[2,2,2,32,512]{4,3,2,1,0:T(8,128)S(1)} %pad_maximum_fusion.mine), channel_id=1, source_target_pairs={{64,0},{65,1},{66,2},{67,3},{68,4},{69,5},{70,6},{71,7},{72,8},{73... | collective-permute-start | bytes 1572872 | tf_op jit(solution)/shard_map/ppermute | solution.py:56
  66.1 0.7 add_and_fusion
  66.8 0.0 collective-permute-done.6.mate
  66.8 4.6 %collective-permute-start.8 = (f32[2,2,2,32,512]{4,3,2,1,0:T(8,128)S(1)}, f32[2,2,2,32,512]{4,3,2,1,0:T(8,128)S(1)}, u32[]{:S(2)}, u32[]{:S(2)}) collective-permute-start(f32[2,2,2,32,512]{4,3,2,1,0:T(8,128)S(1)} %collective-permute-done.6.mate), channel_id=1, source_target_pairs={{448,0},{449,1},{450,2},{451,3},{452,4},{453,5},{454,6},{455,7},{4... | collective-permute-start | bytes 1572872 | tf_op jit(solution)/shard_map/ppermute | solution.py:56
  71.4 1.9 %collective-permute-start.7 = (f32[2,2,2,32,512]{4,3,2,1,0:T(8,128)S(1)}, f32[2,2,2,32,512]{4,3,2,1,0:T(8,128)}, u32[]{:S(2)}, u32[]{:S(2)}) collective-permute-start(f32[2,2,2,32,512]{4,3,2,1,0:T(8,128)S(1)} %collective-permute-done.6.mate), channel_id=1, source_target_pairs={{64,0},{65,1},{66,2},{67,3},{68,4},{69,5},{70,6},{71,7},{72,8},{73... | collective-permute-start | bytes 1572872 | tf_op jit(solution)/shard_map/ppermute | solution.py:56
  73.3 0.0 collective-permute-done.4.next_one
  73.3 2.6 %collective-permute-start.5 = (f32[2,2,2,32,512]{4,3,2,1,0:T(8,128)S(1)}, f32[2,2,2,32,512]{4,3,2,1,0:T(8,128)}, u32[]{:S(2)}, u32[]{:S(2)}) collective-permute-start(f32[2,2,2,32,512]{4,3,2,1,0:T(8,128)S(1)} %collective-permute-done.4.next_one), channel_id=1, source_target_pairs={{0,16},{1,17},{2,18},{3,19},{4,20},{5,21},{6,22},{7,23},{8,24},{9,... | collective-permute-start | bytes 1572872 | tf_op jit(solution)/shard_map/ppermute | solution.py:56
  75.9 0.1 pad_add_fusion.1.info
  76.0 2.2 %copy-done = f32[64,32,512]{2,1,0:T(8,128)S(1)} copy-done((f32[64,32,512]{2,1,0:T(8,128)S(1)}, f32[64,32,512]{2,1,0:T(8,128)}, u32[]{:S(2)}) %copy-start) | copy-done | bytes 4194328
  78.2 5.4 %rows.1 = (bf16[3,2,512,256]{3,2,1,0:T(8,128)(2,1)S(1)}, bf16[3,2,512,256]{3,2,1,0:T(8,128)(2,1)S(1)}, f32[3,2,256,128]{3,2,1,0:T(8,128)S(1)}) custom-call(s32[20]{0:T(128)S(1)} %pad_add_fusion.1.info, f32[16,4,32,512]{3,2,1,0:T(8,128)S(1)} %bitcast.10, f32[16,4,32,512]{3,2,1,0:T(8,128)S(1)} %bitcast.11), custom_call_target="tpu_custom_call" | custom-call | flops 3200000000 | bytes 4194304 | tf_op jit(solution)/shard_map/rows/pallas_call | solution.py:180
  83.6 0.0 collective-permute-done.10.below
  83.6 2.8 %first.1.begun = f32[512,1024]{1,0:T(8,128)S(1)} custom-call(s32[20]{0:T(128)S(1)} %pad_add_fusion.1.info, bf16[3,2,512,256]{3,2,1,0:T(8,128)(2,1)S(1)} %get-tuple-element.12.high, bf16[3,2,512,256]{3,2,1,0:T(8,128)(2,1)S(1)} %get-tuple-element.13.low, f32[3,2,256,128]{3,2,1,0:T(8,128)S(1)} %get-tuple-element.14.scale, ...), custom_call_target="tpu_custom_call" | custom-call | flops 2000000000 | bytes 4194304 | tf_op jit(solution)/shard_map/first/pallas_call | solution.py:180
  86.4 0.7 collective-permute-done.8.below_mate
  87.1 5.4 %collective-permute-done.7.above_mate = f32[2,2,2,32,512]{4,3,2,1,0:T(8,128)} collective-permute-done((f32[2,2,2,32,512]{4,3,2,1,0:T(8,128)S(1)}, f32[2,2,2,32,512]{4,3,2,1,0:T(8,128)}, u32[]{:S(2)}, u32[]{:S(2)}) %collective-permute-start.7) | collective-permute-done | bytes 524320 | tf_op jit(solution)/shard_map/ppermute | solution.py:56
  92.5 0.0 collective-permute-done.5.across
  92.5 3.7 %last.1 = f32[512,1024]{1,0:T(8,128)} custom-call(s32[20]{0:T(128)S(1)} %pad_add_fusion.1.info, bf16[3,2,512,256]{3,2,1,0:T(8,128)(2,1)S(1)} %get-tuple-element.12.high, bf16[3,2,512,256]{3,2,1,0:T(8,128)(2,1)S(1)} %get-tuple-element.13.low, f32[3,2,256,128]{3,2,1,0:T(8,128)S(1)} %get-tuple-element.14.scale, ...), custom_call_target="tpu_custom_call" | custom-call | flops 1200000000 | bytes 4194304 | tf_op jit(solution)/shard_map/last/pallas_call | solution.py:180
  (7 shorter events, 0.0 us)
Async XLA Ops:
  6.5 69.4 %all-gather.3.cloned.1.call-start = ((), (), s32[]{:S(2)}) async-start(), calls=%async_computation | async-start | bytes 4456448 | tf_op jit(solution)/shard_map/all_gather | solution.py:164
  6.5 5.6 %collective-permute-start = (f32[2,32,384]{2,1,0:T(8,128)}, f32[2,32,384]{2,1,0:T(8,128)S(1)}, u32[]{:S(2)}, u32[]{:S(2)}) collective-permute-start(f32[2,32,384]{2,1,0:T(8,128)} %own_ref.1), channel_id=1, source_target_pairs={{16,0},{17,1},{18,2},{19,3},{20,4},{21,5},{22,6},{23,7},{24,8},{25... | collective-permute-start | bytes 294920 | tf_op jit(solution)/shard_map/ppermute | solution.py:56
  12.1 0.6 copy-start.1
  14.7 4.9 %collective-permute-start.1 = (f32[2,32,512]{2,1,0:T(8,128)}, f32[2,32,512]{2,1,0:T(8,128)S(1)}, u32[]{:S(2)}, u32[]{:S(2)}) collective-permute-start(f32[2,32,512]{2,1,0:T(8,128)} %get-tuple-element.16), channel_id=1, source_target_pairs={{0,1},{1,0},{2,3},{3,2},{4,5},{5,4},{6,7},{7,6},{8,9},{9,8},{10,11... | collective-permute-start | bytes 393224 | tf_op jit(solution)/shard_map/ppermute | solution.py:56
  20.3 20.5 %collective-permute-start.3 = (f32[2,2,32,512]{3,2,1,0:T(8,128)}, f32[2,2,32,512]{3,2,1,0:T(8,128)S(1)}, u32[]{:S(2)}, u32[]{:S(2)}) collective-permute-start(f32[2,2,32,512]{3,2,1,0:T(8,128)} %bitcast_dynamic-update-slice_fusion), channel_id=1, source_target_pairs={{0,256},{1,432},{2,320},{3,496},{4,384},{5,48},{6,448},{7,112},{8,... | collective-permute-start | bytes 786440 | tf_op jit(solution)/shard_map/ppermute | solution.py:56
  27.9 18.6 %collective-permute-start.2 = (f32[2,2,32,512]{3,2,1,0:T(8,128)}, f32[2,2,32,512]{3,2,1,0:T(8,128)S(1)}, u32[]{:S(2)}, u32[]{:S(2)}) collective-permute-start(f32[2,2,32,512]{3,2,1,0:T(8,128)} %bitcast_dynamic-update-slice_fusion), channel_id=1, source_target_pairs={{0,0},{1,176},{2,64},{3,240},{4,128},{5,304},{6,192},{7,368},{8,25... | collective-permute-start | bytes 786440 | tf_op jit(solution)/shard_map/ppermute | solution.py:56
  46.5 20.2 %collective-permute-start.6 = (f32[2,2,2,32,512]{4,3,2,1,0:T(8,128)S(1)}, f32[2,2,2,32,512]{4,3,2,1,0:T(8,128)S(1)}, u32[]{:S(2)}, u32[]{:S(2)}) collective-permute-start(f32[2,2,2,32,512]{4,3,2,1,0:T(8,128)S(1)} %pad_maximum_fusion.mine), channel_id=1, source_target_pairs={{0,16},{1,17},{2,18},{3,19},{4,20},{5,21},{6,22},{7,23},{8,24},{9,... | collective-permute-start | bytes 1572872 | tf_op jit(solution)/shard_map/ppermute | solution.py:56
  50.7 22.6 %collective-permute-start.4 = (f32[2,2,2,32,512]{4,3,2,1,0:T(8,128)S(1)}, f32[2,2,2,32,512]{4,3,2,1,0:T(8,128)S(1)}, u32[]{:S(2)}, u32[]{:S(2)}) collective-permute-start(f32[2,2,2,32,512]{4,3,2,1,0:T(8,128)S(1)} %pad_maximum_fusion.mine), channel_id=1, source_target_pairs={{0,48},{1,49},{2,50},{3,51},{4,52},{5,53},{6,54},{7,55},{8,56},{9,... | collective-permute-start | bytes 1572872 | tf_op jit(solution)/shard_map/ppermute | solution.py:56
  58.0 25.6 %collective-permute-start.10 = (f32[2,2,2,32,512]{4,3,2,1,0:T(8,128)S(1)}, f32[2,2,2,32,512]{4,3,2,1,0:T(8,128)S(1)}, u32[]{:S(2)}, u32[]{:S(2)}) collective-permute-start(f32[2,2,2,32,512]{4,3,2,1,0:T(8,128)S(1)} %pad_maximum_fusion.mine), channel_id=1, source_target_pairs={{448,0},{449,1},{450,2},{451,3},{452,4},{453,5},{454,6},{455,7},{4... | collective-permute-start | bytes 1572872 | tf_op jit(solution)/shard_map/ppermute | solution.py:56
  64.2 19.4 %collective-permute-start.9 = (f32[2,2,2,32,512]{4,3,2,1,0:T(8,128)S(1)}, f32[2,2,2,32,512]{4,3,2,1,0:T(8,128)S(1)}, u32[]{:S(2)}, u32[]{:S(2)}) collective-permute-start(f32[2,2,2,32,512]{4,3,2,1,0:T(8,128)S(1)} %pad_maximum_fusion.mine), channel_id=1, source_target_pairs={{64,0},{65,1},{66,2},{67,3},{68,4},{69,5},{70,6},{71,7},{72,8},{73... | collective-permute-start | bytes 1572872 | tf_op jit(solution)/shard_map/ppermute | solution.py:56
  66.8 20.3 %collective-permute-start.8 = (f32[2,2,2,32,512]{4,3,2,1,0:T(8,128)S(1)}, f32[2,2,2,32,512]{4,3,2,1,0:T(8,128)S(1)}, u32[]{:S(2)}, u32[]{:S(2)}) collective-permute-start(f32[2,2,2,32,512]{4,3,2,1,0:T(8,128)S(1)} %collective-permute-done.6.mate), channel_id=1, source_target_pairs={{448,0},{449,1},{450,2},{451,3},{452,4},{453,5},{454,6},{455,7},{4... | collective-permute-start | bytes 1572872 | tf_op jit(solution)/shard_map/ppermute | solution.py:56
  71.4 21.1 %collective-permute-start.7 = (f32[2,2,2,32,512]{4,3,2,1,0:T(8,128)S(1)}, f32[2,2,2,32,512]{4,3,2,1,0:T(8,128)}, u32[]{:S(2)}, u32[]{:S(2)}) collective-permute-start(f32[2,2,2,32,512]{4,3,2,1,0:T(8,128)S(1)} %collective-permute-done.6.mate), channel_id=1, source_target_pairs={{64,0},{65,1},{66,2},{67,3},{68,4},{69,5},{70,6},{71,7},{72,8},{73... | collective-permute-start | bytes 1572872 | tf_op jit(solution)/shard_map/ppermute | solution.py:56
  73.3 19.2 %collective-permute-start.5 = (f32[2,2,2,32,512]{4,3,2,1,0:T(8,128)S(1)}, f32[2,2,2,32,512]{4,3,2,1,0:T(8,128)}, u32[]{:S(2)}, u32[]{:S(2)}) collective-permute-start(f32[2,2,2,32,512]{4,3,2,1,0:T(8,128)S(1)} %collective-permute-done.4.next_one), channel_id=1, source_target_pairs={{0,16},{1,17},{2,18},{3,19},{4,20},{5,21},{6,22},{7,23},{8,24},{9,... | collective-permute-start | bytes 1572872 | tf_op jit(solution)/shard_map/ppermute | solution.py:56
  76.0 2.2 %copy-start = (f32[64,32,512]{2,1,0:T(8,128)S(1)}, f32[64,32,512]{2,1,0:T(8,128)}, u32[]{:S(2)}) copy-start(f32[64,32,512]{2,1,0:T(8,128)} %all-gather.3.cloned.1.call-done) | copy-start | bytes 12582916
Sparse Core Ops, SparseCore 0:
  14.8 61.0 all-gather.2

commit v7 on v4

--- a/solution.py
+++ b/solution.py
@@ -11,7 +11,7 @@
 AXES = ("prow", "pcol")
 F32, BF16 = jnp.float32, jnp.bfloat16
 MIB = 1 << 20
-LIFTS = ((0, 4), (2, 6))
+LIFTS = ((0, 4), (6, 2))
 OWNER, GROUP = (0, 1, 1, 0), (0, 0, 1, 1)
 
 

time: 104 us -> 108 us (1.038)
  the two profiles are of different devices: /device:TPU:29 before, /device:TPU:25 now
where the time goes in v7:
time: 108 us; the launch traced here: 107 us
  starting transfers between devices  51.4 us (48%)
  waiting for transfers between devices  24.2 us (22%)
  Pallas kernels  14 us (13%)
  between operations  13.6 us (13%)
  local copies, waits for them, and re-layouts  2.83 us (3%)
  other arithmetic  1.13 us (1%)
    ppermute x11, starting transfers between devices, send(): return lax.ppermute(value, AXES, pairs)  51.4 us
    ppermute x11, waiting for transfers between devices, send(): return lax.ppermute(value, AXES, pairs)  24.2 us
    pallas_call x3, Pallas kernels, kernel(): pl.pallas_call(run, out_shape=out_shape, compiler_params=pltpu.CompilerPa...  12.2 us
    unnamed x6, local copies, waits for them, and re-layouts  2.83 us
  transfers between devices with their start and end apart: 12, of which 5 were waited for; matrix products, arithmetic and copies ran while one was open for 1% of the time, Pallas kernels for 8%

profile of v7, /device:TPU:25, one launch (start us, length us, event | category | flops | bytes accessed | tf_op | source)
XLA Modules:
  0.0 107.2 jit_solution(17950596625470059335)
XLA Ops:
  6.5 4.4 %collective-permute-start = (f32[2,32,384]{2,1,0:T(8,128)}, f32[2,32,384]{2,1,0:T(8,128)S(1)}, u32[]{:S(2)}, u32[]{:S(2)}) collective-permute-start(f32[2,32,384]{2,1,0:T(8,128)} %own_ref.1), channel_id=1, source_target_pairs={{16,0},{17,1},{18,2},{19,3},{20,4},{21,5},{22,6},{23,7},{24,8},{25... | collective-permute-start | bytes 294920 | tf_op jit(solution)/shard_map/ppermute | solution.py:56
  10.9 1.9 %collective-permute-done.next_ref = f32[2,32,384]{2,1,0:T(8,128)S(1)} collective-permute-done((f32[2,32,384]{2,1,0:T(8,128)}, f32[2,32,384]{2,1,0:T(8,128)S(1)}, u32[]{:S(2)}, u32[]{:S(2)}) %collective-permute-start) | collective-permute-done | bytes 98336 | tf_op jit(solution)/shard_map/ppermute | solution.py:56
  12.9 0.6 copy-done.1
  13.5 1.8 %place.1 = (f32[2,32,512]{2,1,0:T(8,128)}, f32[4,32,512]{2,1,0:T(8,128)}) custom-call(s32[1]{0:T(128)} %bitcast.4.row_ref, s32[2,96]{1,0:T(2,128)} %targets_ref.1, f32[2,32,384]{2,1,0:T(8,128)} %own_ref.1, f32[2,32,384]{2,1,0:T(8,128)} %copy-done.1, f32[2,32,512]{2,1,0:T(8,128)} %inverse_ref.1), custom_call_target="tpu_custom_call" | custom-call | tf_op jit(solution)/shard_map/place/pallas_call | solution.py:145
  15.4 0.0 all-gather.3.cloned.1.call-update
  15.4 3.4 %collective-permute-start.1 = (f32[2,32,512]{2,1,0:T(8,128)}, f32[2,32,512]{2,1,0:T(8,128)S(1)}, u32[]{:S(2)}, u32[]{:S(2)}) collective-permute-start(f32[2,32,512]{2,1,0:T(8,128)} %get-tuple-element.14), channel_id=1, source_target_pairs={{0,1},{1,0},{2,3},{3,2},{4,5},{5,4},{6,7},{7,6},{8,9},{9,8},{10,11... | collective-permute-start | bytes 393224 | tf_op jit(solution)/shard_map/ppermute | solution.py:56
  18.8 1.2 %collective-permute-done.1 = f32[2,32,512]{2,1,0:T(8,128)S(1)} collective-permute-done((f32[2,32,512]{2,1,0:T(8,128)}, f32[2,32,512]{2,1,0:T(8,128)S(1)}, u32[]{:S(2)}, u32[]{:S(2)}) %collective-permute-start.1) | collective-permute-done | bytes 131104 | tf_op jit(solution)/shard_map/ppermute | solution.py:56
  20.0 0.9 pad_maximum_fusion.1
  20.9 10.8 %collective-permute-start.3 = (f32[2,2,32,512]{3,2,1,0:T(8,128)S(1)}, f32[2,2,32,512]{3,2,1,0:T(8,128)S(1)}, u32[]{:S(2)}, u32[]{:S(2)}) collective-permute-start(f32[2,2,32,512]{3,2,1,0:T(8,128)S(1)} %pad_maximum_fusion.1), channel_id=1, source_target_pairs={{0,256},{1,176},{2,320},{3,240},{4,384},{5,304},{6,448},{7,368},{8... | collective-permute-start | bytes 786440 | tf_op jit(solution)/shard_map/ppermute | solution.py:56
  31.7 5.5 %collective-permute-start.2 = (f32[2,2,32,512]{3,2,1,0:T(8,128)S(1)}, f32[2,2,32,512]{3,2,1,0:T(8,128)S(1)}, u32[]{:S(2)}, u32[]{:S(2)}) collective-permute-start(f32[2,2,32,512]{3,2,1,0:T(8,128)S(1)} %pad_maximum_fusion.1), channel_id=1, source_target_pairs={{0,0},{1,432},{2,64},{3,496},{4,128},{5,48},{6,192},{7,112},{8,256... | collective-permute-start | bytes 786440 | tf_op jit(solution)/shard_map/ppermute | solution.py:56
  37.2 0.0 collective-permute-done.3
  37.3 14.7 %collective-permute-done.2 = f32[2,2,32,512]{3,2,1,0:T(8,128)S(1)} collective-permute-done((f32[2,2,32,512]{3,2,1,0:T(8,128)S(1)}, f32[2,2,32,512]{3,2,1,0:T(8,128)S(1)}, u32[]{:S(2)}, u32[]{:S(2)}) %collective-permute-start.2) | collective-permute-done | bytes 262176 | tf_op jit(solution)/shard_map/ppermute | solution.py:56
  52.0 1.9 %collective-permute-start.6 = (f32[2,2,2,32,512]{4,3,2,1,0:T(8,128)S(1)}, f32[2,2,2,32,512]{4,3,2,1,0:T(8,128)S(1)}, u32[]{:S(2)}, u32[]{:S(2)}) collective-permute-start(f32[2,2,2,32,512]{4,3,2,1,0:T(8,128)S(1)} %pad_maximum_fusion.mine), channel_id=1, source_target_pairs={{0,16},{1,17},{2,18},{3,19},{4,20},{5,21},{6,22},{7,23},{8,24},{9,... | collective-permute-start | bytes 1572872 | tf_op jit(solution)/shard_map/ppermute | solution.py:56
  53.9 4.0 %collective-permute-start.4 = (f32[2,2,2,32,512]{4,3,2,1,0:T(8,128)S(1)}, f32[2,2,2,32,512]{4,3,2,1,0:T(8,128)S(1)}, u32[]{:S(2)}, u32[]{:S(2)}) collective-permute-start(f32[2,2,2,32,512]{4,3,2,1,0:T(8,128)S(1)} %pad_maximum_fusion.mine), channel_id=1, source_target_pairs={{0,48},{1,49},{2,50},{3,51},{4,52},{5,53},{6,54},{7,55},{8,56},{9,... | collective-permute-start | bytes 1572872 | tf_op jit(solution)/shard_map/ppermute | solution.py:56
  57.9 0.1 shift-right-arithmetic_and_fusion
  58.0 11.0 %collective-permute-start.10 = (f32[2,2,2,32,512]{4,3,2,1,0:T(8,128)S(1)}, f32[2,2,2,32,512]{4,3,2,1,0:T(8,128)S(1)}, u32[]{:S(2)}, u32[]{:S(2)}) collective-permute-start(f32[2,2,2,32,512]{4,3,2,1,0:T(8,128)S(1)} %pad_maximum_fusion.mine), channel_id=1, source_target_pairs={{448,0},{449,1},{450,2},{451,3},{452,4},{453,5},{454,6},{455,7},{4... | collective-permute-start | bytes 1572872 | tf_op jit(solution)/shard_map/ppermute | solution.py:56
  69.1 1.9 %collective-permute-start.9 = (f32[2,2,2,32,512]{4,3,2,1,0:T(8,128)S(1)}, f32[2,2,2,32,512]{4,3,2,1,0:T(8,128)S(1)}, u32[]{:S(2)}, u32[]{:S(2)}) collective-permute-start(f32[2,2,2,32,512]{4,3,2,1,0:T(8,128)S(1)} %pad_maximum_fusion.mine), channel_id=1, source_target_pairs={{64,0},{65,1},{66,2},{67,3},{68,4},{69,5},{70,6},{71,7},{72,8},{73... | collective-permute-start | bytes 1572872 | tf_op jit(solution)/shard_map/ppermute | solution.py:56
  71.0 0.0 collective-permute-done.6.mate
  71.0 4.6 %collective-permute-start.8 = (f32[2,2,2,32,512]{4,3,2,1,0:T(8,128)S(1)}, f32[2,2,2,32,512]{4,3,2,1,0:T(8,128)S(1)}, u32[]{:S(2)}, u32[]{:S(2)}) collective-permute-start(f32[2,2,2,32,512]{4,3,2,1,0:T(8,128)S(1)} %collective-permute-done.6.mate), channel_id=1, source_target_pairs={{448,0},{449,1},{450,2},{451,3},{452,4},{453,5},{454,6},{455,7},{4... | collective-permute-start | bytes 1572872 | tf_op jit(solution)/shard_map/ppermute | solution.py:56
  75.6 1.9 %collective-permute-start.7 = (f32[2,2,2,32,512]{4,3,2,1,0:T(8,128)S(1)}, f32[2,2,2,32,512]{4,3,2,1,0:T(8,128)}, u32[]{:S(2)}, u32[]{:S(2)}) collective-permute-start(f32[2,2,2,32,512]{4,3,2,1,0:T(8,128)S(1)} %collective-permute-done.6.mate), channel_id=1, source_target_pairs={{64,0},{65,1},{66,2},{67,3},{68,4},{69,5},{70,6},{71,7},{72,8},{73... | collective-permute-start | bytes 1572872 | tf_op jit(solution)/shard_map/ppermute | solution.py:56
  77.5 0.0 collective-permute-done.4.next_one
  77.5 1.9 %collective-permute-start.5 = (f32[2,2,2,32,512]{4,3,2,1,0:T(8,128)S(1)}, f32[2,2,2,32,512]{4,3,2,1,0:T(8,128)}, u32[]{:S(2)}, u32[]{:S(2)}) collective-permute-start(f32[2,2,2,32,512]{4,3,2,1,0:T(8,128)S(1)} %collective-permute-done.4.next_one), channel_id=1, source_target_pairs={{0,16},{1,17},{2,18},{3,19},{4,20},{5,21},{6,22},{7,23},{8,24},{9,... | collective-permute-start | bytes 1572872 | tf_op jit(solution)/shard_map/ppermute | solution.py:56
  79.5 0.1 pad_add_fusion.1.info
  79.6 2.2 %copy-done = f32[64,32,512]{2,1,0:T(8,128)S(1)} copy-done((f32[64,32,512]{2,1,0:T(8,128)S(1)}, f32[64,32,512]{2,1,0:T(8,128)}, u32[]{:S(2)}) %copy-start) | copy-done | bytes 4194328
  81.7 5.4 %rows.1 = (bf16[3,2,512,256]{3,2,1,0:T(8,128)(2,1)S(1)}, bf16[3,2,512,256]{3,2,1,0:T(8,128)(2,1)S(1)}, f32[3,2,256,128]{3,2,1,0:T(8,128)S(1)}) custom-call(s32[20]{0:T(128)S(1)} %pad_add_fusion.1.info, f32[16,4,32,512]{3,2,1,0:T(8,128)S(1)} %bitcast.10, f32[16,4,32,512]{3,2,1,0:T(8,128)S(1)} %bitcast.11), custom_call_target="tpu_custom_call" | custom-call | flops 3200000000 | bytes 4194304 | tf_op jit(solution)/shard_map/rows/pallas_call | solution.py:169
  87.2 0.0 collective-permute-done.10.below
  87.2 0.0 collective-permute-done.9.above
  87.2 2.8 %first.1.begun = f32[512,1024]{1,0:T(8,128)S(1)} custom-call(s32[20]{0:T(128)S(1)} %pad_add_fusion.1.info, bf16[3,2,512,256]{3,2,1,0:T(8,128)(2,1)S(1)} %get-tuple-element.11.high, bf16[3,2,512,256]{3,2,1,0:T(8,128)(2,1)S(1)} %get-tuple-element.12.low, f32[3,2,256,128]{3,2,1,0:T(8,128)S(1)} %get-tuple-element.13.scale, ...), custom_call_target="tpu_custom_call" | custom-call | flops 2000000000 | bytes 4194304 | tf_op jit(solution)/shard_map/first/pallas_call | solution.py:169
  90.0 1.0 collective-permute-done.8.below_mate
  91.0 5.4 %collective-permute-done.7.above_mate = f32[2,2,2,32,512]{4,3,2,1,0:T(8,128)} collective-permute-done((f32[2,2,2,32,512]{4,3,2,1,0:T(8,128)S(1)}, f32[2,2,2,32,512]{4,3,2,1,0:T(8,128)}, u32[]{:S(2)}, u32[]{:S(2)}) %collective-permute-start.7) | collective-permute-done | bytes 524320 | tf_op jit(solution)/shard_map/ppermute | solution.py:56
  96.4 0.0 collective-permute-done.5.across
  96.4 4.0 %last.1 = f32[512,1024]{1,0:T(8,128)} custom-call(s32[20]{0:T(128)S(1)} %pad_add_fusion.1.info, bf16[3,2,512,256]{3,2,1,0:T(8,128)(2,1)S(1)} %get-tuple-element.11.high, bf16[3,2,512,256]{3,2,1,0:T(8,128)(2,1)S(1)} %get-tuple-element.12.low, f32[3,2,256,128]{3,2,1,0:T(8,128)S(1)} %get-tuple-element.13.scale, ...), custom_call_target="tpu_custom_call" | custom-call | flops 1200000000 | bytes 4194304 | tf_op jit(solution)/shard_map/last/pallas_call | solution.py:169
  (9 shorter events, 0.1 us)
Async XLA Ops:
  6.5 64.5 %copy-start.2 = (s32[12]{0:T(128)S(1)}, s32[12]{0:T(128)}, u32[]{:S(2)}) copy-start(s32[12]{0:T(128)} %constant.58.clone) | copy-start | bytes 148
  6.5 73.0 %all-gather.3.cloned.1.call-start = ((), (), s32[]{:S(2)}) async-start(), calls=%async_computation | async-start | bytes 4456448 | tf_op jit(solution)/shard_map/all_gather | solution.py:153
  6.5 6.3 %collective-permute-start = (f32[2,32,384]{2,1,0:T(8,128)}, f32[2,32,384]{2,1,0:T(8,128)S(1)}, u32[]{:S(2)}, u32[]{:S(2)}) collective-permute-start(f32[2,32,384]{2,1,0:T(8,128)} %own_ref.1), channel_id=1, source_target_pairs={{16,0},{17,1},{18,2},{19,3},{20,4},{21,5},{22,6},{23,7},{24,8},{25... | collective-permute-start | bytes 294920 | tf_op jit(solution)/shard_map/ppermute | solution.py:56
  12.9 0.6 copy-start.1
  15.4 4.6 %collective-permute-start.1 = (f32[2,32,512]{2,1,0:T(8,128)}, f32[2,32,512]{2,1,0:T(8,128)S(1)}, u32[]{:S(2)}, u32[]{:S(2)}) collective-permute-start(f32[2,32,512]{2,1,0:T(8,128)} %get-tuple-element.14), channel_id=1, source_target_pairs={{0,1},{1,0},{2,3},{3,2},{4,5},{5,4},{6,7},{7,6},{8,9},{9,8},{10,11... | collective-permute-start | bytes 393224 | tf_op jit(solution)/shard_map/ppermute | solution.py:56
  20.9 16.3 %collective-permute-start.3 = (f32[2,2,32,512]{3,2,1,0:T(8,128)S(1)}, f32[2,2,32,512]{3,2,1,0:T(8,128)S(1)}, u32[]{:S(2)}, u32[]{:S(2)}) collective-permute-start(f32[2,2,32,512]{3,2,1,0:T(8,128)S(1)} %pad_maximum_fusion.1), channel_id=1, source_target_pairs={{0,256},{1,176},{2,320},{3,240},{4,384},{5,304},{6,448},{7,368},{8... | collective-permute-start | bytes 786440 | tf_op jit(solution)/shard_map/ppermute | solution.py:56
  31.7 20.2 %collective-permute-start.2 = (f32[2,2,32,512]{3,2,1,0:T(8,128)S(1)}, f32[2,2,32,512]{3,2,1,0:T(8,128)S(1)}, u32[]{:S(2)}, u32[]{:S(2)}) collective-permute-start(f32[2,2,32,512]{3,2,1,0:T(8,128)S(1)} %pad_maximum_fusion.1), channel_id=1, source_target_pairs={{0,0},{1,432},{2,64},{3,496},{4,128},{5,48},{6,192},{7,112},{8,256... | collective-permute-start | bytes 786440 | tf_op jit(solution)/shard_map/ppermute | solution.py:56
  52.0 19.0 %collective-permute-start.6 = (f32[2,2,2,32,512]{4,3,2,1,0:T(8,128)S(1)}, f32[2,2,2,32,512]{4,3,2,1,0:T(8,128)S(1)}, u32[]{:S(2)}, u32[]{:S(2)}) collective-permute-start(f32[2,2,2,32,512]{4,3,2,1,0:T(8,128)S(1)} %pad_maximum_fusion.mine), channel_id=1, source_target_pairs={{0,16},{1,17},{2,18},{3,19},{4,20},{5,21},{6,22},{7,23},{8,24},{9,... | collective-permute-start | bytes 1572872 | tf_op jit(solution)/shard_map/ppermute | solution.py:56
  53.9 23.6 %collective-permute-start.4 = (f32[2,2,2,32,512]{4,3,2,1,0:T(8,128)S(1)}, f32[2,2,2,32,512]{4,3,2,1,0:T(8,128)S(1)}, u32[]{:S(2)}, u32[]{:S(2)}) collective-permute-start(f32[2,2,2,32,512]{4,3,2,1,0:T(8,128)S(1)} %pad_maximum_fusion.mine), channel_id=1, source_target_pairs={{0,48},{1,49},{2,50},{3,51},{4,52},{5,53},{6,54},{7,55},{8,56},{9,... | collective-permute-start | bytes 1572872 | tf_op jit(solution)/shard_map/ppermute | solution.py:56
  58.0 29.2 %collective-permute-start.10 = (f32[2,2,2,32,512]{4,3,2,1,0:T(8,128)S(1)}, f32[2,2,2,32,512]{4,3,2,1,0:T(8,128)S(1)}, u32[]{:S(2)}, u32[]{:S(2)}) collective-permute-start(f32[2,2,2,32,512]{4,3,2,1,0:T(8,128)S(1)} %pad_maximum_fusion.mine), channel_id=1, source_target_pairs={{448,0},{449,1},{450,2},{451,3},{452,4},{453,5},{454,6},{455,7},{4... | collective-permute-start | bytes 1572872 | tf_op jit(solution)/shard_map/ppermute | solution.py:56
  69.1 18.1 %collective-permute-start.9 = (f32[2,2,2,32,512]{4,3,2,1,0:T(8,128)S(1)}, f32[2,2,2,32,512]{4,3,2,1,0:T(8,128)S(1)}, u32[]{:S(2)}, u32[]{:S(2)}) collective-permute-start(f32[2,2,2,32,512]{4,3,2,1,0:T(8,128)S(1)} %pad_maximum_fusion.mine), channel_id=1, source_target_pairs={{64,0},{65,1},{66,2},{67,3},{68,4},{69,5},{70,6},{71,7},{72,8},{73... | collective-permute-start | bytes 1572872 | tf_op jit(solution)/shard_map/ppermute | solution.py:56
  71.0 20.0 %collective-permute-start.8 = (f32[2,2,2,32,512]{4,3,2,1,0:T(8,128)S(1)}, f32[2,2,2,32,512]{4,3,2,1,0:T(8,128)S(1)}, u32[]{:S(2)}, u32[]{:S(2)}) collective-permute-start(f32[2,2,2,32,512]{4,3,2,1,0:T(8,128)S(1)} %collective-permute-done.6.mate), channel_id=1, source_target_pairs={{448,0},{449,1},{450,2},{451,3},{452,4},{453,5},{454,6},{455,7},{4... | collective-permute-start | bytes 1572872 | tf_op jit(solution)/shard_map/ppermute | solution.py:56
  75.6 20.8 %collective-permute-start.7 = (f32[2,2,2,32,512]{4,3,2,1,0:T(8,128)S(1)}, f32[2,2,2,32,512]{4,3,2,1,0:T(8,128)}, u32[]{:S(2)}, u32[]{:S(2)}) collective-permute-start(f32[2,2,2,32,512]{4,3,2,1,0:T(8,128)S(1)} %collective-permute-done.6.mate), channel_id=1, source_target_pairs={{64,0},{65,1},{66,2},{67,3},{68,4},{69,5},{70,6},{71,7},{72,8},{73... | collective-permute-start | bytes 1572872 | tf_op jit(solution)/shard_map/ppermute | solution.py:56
  77.5 18.9 %collective-permute-start.5 = (f32[2,2,2,32,512]{4,3,2,1,0:T(8,128)S(1)}, f32[2,2,2,32,512]{4,3,2,1,0:T(8,128)}, u32[]{:S(2)}, u32[]{:S(2)}) collective-permute-start(f32[2,2,2,32,512]{4,3,2,1,0:T(8,128)S(1)} %collective-permute-done.4.next_one), channel_id=1, source_target_pairs={{0,16},{1,17},{2,18},{3,19},{4,20},{5,21},{6,22},{7,23},{8,24},{9,... | collective-permute-start | bytes 1572872 | tf_op jit(solution)/shard_map/ppermute | solution.py:56
  79.6 2.2 %copy-start = (f32[64,32,512]{2,1,0:T(8,128)S(1)}, f32[64,32,512]{2,1,0:T(8,128)}, u32[]{:S(2)}) copy-start(f32[64,32,512]{2,1,0:T(8,128)} %all-gather.3.cloned.1.call-done) | copy-start | bytes 12582916
Sparse Core Ops, SparseCore 0:
  15.5 63.6 all-gather.2
